TPU v7x, 32 devices: a whole 2x2x4 slice. The times are simulated.
32 devices in a mesh: dp: 4 (over z), expert: 8 (over y, x, core).
Axes of the slice: x: 2, y: 2, z: 4, core: 2. Of those that a mesh axis runs over, the one named last changes fastest.
Arguments:
- block_input: bfloat16 [2, 4096, 1536], P(None, ('dp', 'expert')), may hold values from -6 to 6
- out_grad: bfloat16 [2, 4096, 1536], P(None, ('dp', 'expert')), may hold values from -6 to 6
- routes: int32 [2, 4096, 6], P(None, ('dp', 'expert')), may hold values from 0 to 31, all different within a row; in each aligned block of 128 rows (0 to 127, 128 to 255, ..., all dimensions but the last counted through in order) at most 36 rows name the same one
- norm_in: bfloat16 [1536], P(('dp', 'expert')), may hold values from 0.5 to 1.5
- in_proj: bfloat16 [1536, 6448], P(('dp', 'expert')), may hold values from -0.15625 to 0.15625
- conv_weight: bfloat16 [4, 3328], replicated, may hold values from -3 to 3
- conv_bias: bfloat16 [3328], replicated, may hold values from -3 to 3
- step_bias: bfloat16 [48], replicated, may hold values from -4 to -1
- log_rate: bfloat16 [48], replicated, may hold values from -3 to 1.5
- skip_gain: bfloat16 [48], replicated, may hold values from 0.5 to 2
- mixer_gain: bfloat16 [3072], P(('dp', 'expert')), may hold values from 0.5 to 1.5
- out_proj: bfloat16 [3072, 1536], P(('dp', 'expert')), may hold values from -0.109375 to 0.109375
- norm_mid: bfloat16 [1536], P(('dp', 'expert')), may hold values from 0.5 to 1.5
- router: bfloat16 [1536, 32], P(('dp', 'expert')), may hold values from -0.078125 to 0.078125
- shared_gate: bfloat16 [1536, 1024], P(('dp', 'expert')), may hold values from -0.15625 to 0.15625
- shared_up: bfloat16 [1536, 1024], P(('dp', 'expert')), may hold values from -0.15625 to 0.15625
- shared_down: bfloat16 [1024, 1536], P(('dp', 'expert')), may hold values from -0.1875 to 0.1875
- expert_gate: bfloat16 [32, 1536, 512], P('expert', 'dp'), may hold values from -0.15625 to 0.15625
- expert_up: bfloat16 [32, 1536, 512], P('expert', 'dp'), may hold values from -0.15625 to 0.15625
- expert_down: bfloat16 [32, 512, 1536], P('expert', 'dp'), may hold values from -0.25 to 0.25
Outputs:
- block_output: bfloat16 [2, 4096, 1536], P(None, ('dp', 'expert'))
- input_grad: float32 [2, 4096, 1536], P(None, ('dp', 'expert'))
- grad_norm_in: float32 [1536], P(('dp', 'expert'))
- grad_in_proj: float32 [1536, 6448], P(('dp', 'expert'))
- grad_conv_weight: float32 [4, 3328], replicated
- grad_conv_bias: float32 [3328], replicated
- grad_step_bias: float32 [48], replicated
- grad_log_rate: float32 [48], replicated
- grad_skip_gain: float32 [48], replicated
- grad_mixer_gain: float32 [3072], P(('dp', 'expert'))
- grad_out_proj: float32 [3072, 1536], P(('dp', 'expert'))
- grad_norm_mid: float32 [1536], P(('dp', 'expert'))
- grad_router: float32 [1536, 32], P(('dp', 'expert'))
- grad_shared_gate: float32 [1536, 1024], P(('dp', 'expert'))
- grad_shared_up: float32 [1536, 1024], P(('dp', 'expert'))
- grad_shared_down: float32 [1024, 1536], P(('dp', 'expert'))
- grad_expert_gate: float32 [32, 1536, 512], P('expert', 'dp')
- grad_expert_up: float32 [32, 1536, 512], P('expert', 'dp')
- grad_expert_down: float32 [32, 512, 1536], P('expert', 'dp')
Inputs may be any that keep to these rules, and one draw needn't show every extreme that they name: `routes`: each row names 6 different experts; within the rows of one device in one micro-batch (aligned blocks of 128 rows) no expert is named more than 36 times, a bound that some block reaches.
All inputs are finite; a program needn't handle non-finite values.
Results may differ from a plain program's by a relative error of at most 0.013.
Values may be sent and summed in bfloat16 or wider, within the bound.
A program may use at most 512 MiB of HBM per device.

v0:
```python
from functools import partial

import jax
import jax.numpy as jnp
from jax import lax
from jax.sharding import PartitionSpec as P

H = 48
SPAN = 64


epsilon = 1e-05
highest = lax.Precision.HIGHEST


def rms_scale(value, gain):
    return value * lax.rsqrt(jnp.mean(value * value, axis=-1, keepdims=True) + epsilon) * gain


def silu_slope(value):
    sigma = jax.nn.sigmoid(value)
    return sigma * (1.0 + value * (1.0 - sigma))


def scan_blocks(inputs, input_map, output_map, decay, block):
    length, heads, width = inputs.shape
    number = length // block
    states = input_map.shape[-1]
    inputs = inputs.reshape(number, block, heads, width)
    input_map = input_map.reshape(number, block, states)
    output_map = output_map.reshape(number, block, states)
    cumul = jnp.cumsum(decay.reshape(number, block, heads), axis=1)
    rowidx = lax.broadcasted_iota(jnp.int32, (block, block), 0)
    colidx = lax.broadcasted_iota(jnp.int32, (block, block), 1)
    lower = (rowidx >= colidx)[None, :, :, None]
    spread = cumul[:, :, None, :] - cumul[:, None, :, :]
    weights = jnp.exp(jnp.where(lower, spread, 0.0)) * lower.astype(jnp.float32)
    inner = jnp.einsum("cin,cjn->cij", output_map, input_map, precision=highest)
    local_out = jnp.einsum("cij,cijh,cjhp->cihp", inner, weights, inputs, precision=highest)
    to_end = jnp.exp(cumul[:, -1:, :] - cumul)
    block_state = jnp.einsum("cjn,cjh,cjhp->chnp", input_map, to_end, inputs, precision=highest)
    block_decay = jnp.exp(cumul[:, -1, :])

    def advance(carry, item):
        state_now, decay_now = item
        return (carry * decay_now[:, None, None] + state_now, carry)

    anchor = jnp.zeros((heads, states, width), jnp.float32)
    unused, entering = lax.scan(advance, anchor, (block_state, block_decay))
    carried = jnp.einsum(
        "cin,chnp,cih->cihp", output_map, entering, jnp.exp(cumul), precision=highest
    )
    return (local_out + carried).reshape(length, heads, width)


def mixer(
    merged, conv_kernel, conv_shift, step_shift, rate_log, skip_scale, mix_gain, heads, block
):
    length = merged.shape[0]
    inner_width = mix_gain.shape[0]
    width = inner_width // heads
    conv_width = conv_shift.shape[0]
    states = (conv_width - inner_width) // 2
    kernel = conv_kernel.shape[0]
    gate_part = merged[:, :inner_width]
    signal = merged[:, inner_width : inner_width + conv_width]
    step_raw = merged[:, inner_width + conv_width :]
    padded = jnp.pad(signal, ((kernel - 1, 0), (0, 0)))
    summed = jnp.zeros_like(signal) + conv_shift
    for shift_at in range(kernel):
        summed = summed + conv_kernel[shift_at] * padded[shift_at : shift_at + length]
    activated = jax.nn.silu(summed)
    values = activated[:, :inner_width].reshape(length, heads, width)
    input_map = activated[:, inner_width : inner_width + states]
    output_map = activated[:, inner_width + states :]
    step = jax.nn.softplus(step_raw + step_shift)
    decay = -jnp.exp(rate_log) * step
    scanned = scan_blocks(values * step[:, :, None], input_map, output_map, decay, block)
    joined = (scanned + skip_scale[None, :, None] * values).reshape(length, inner_width)
    return rms_scale(joined * jax.nn.silu(gate_part), mix_gain)


def body(
    block_input,
    out_grad,
    routes,
    norm_in,
    in_proj,
    conv_weight,
    conv_bias,
    step_bias,
    log_rate,
    skip_gain,
    mixer_gain,
    out_proj,
    norm_mid,
    router,
    shared_gate,
    shared_up,
    shared_down,
    expert_gate,
    expert_up,
    expert_down,
):
    f32 = jnp.float32
    b16 = jnp.bfloat16
    micro, length, width = block_input.shape
    picks = routes.shape[-1]
    local_experts = expert_gate.shape[0]
    experts = local_experts * lax.axis_size("expert")
    capacity = 3 * length * picks // (2 * experts)
    conv_kernel = conv_weight.astype(f32)
    conv_shift = conv_bias.astype(f32)
    step_shift = step_bias.astype(f32)
    rate_log = log_rate.astype(f32)
    skip_scale = skip_gain.astype(f32)
    gain_in_sum = jnp.zeros((norm_in.shape[0] * lax.axis_size(("dp", "expert")),), f32)
    gain_mix_sum = jnp.zeros((mixer_gain.shape[0] * lax.axis_size(("dp", "expert")),), f32)
    gain_mid_sum = jnp.zeros((norm_mid.shape[0] * lax.axis_size(("dp", "expert")),), f32)
    small_sums = [
        jnp.zeros_like(conv_kernel),
        jnp.zeros_like(conv_shift),
        jnp.zeros_like(step_shift),
        jnp.zeros_like(rate_log),
        jnp.zeros_like(skip_scale),
    ]
    kept_normed, kept_merged, kept_mixed, kept_middle = ([], [], [], [])
    kept_routed, kept_logit, kept_spre, kept_slin, kept_shid, kept_dout = ([], [], [], [], [], [])
    kept_arrived, kept_gpre, kept_upre, kept_ehid, kept_agrad = ([], [], [], [], [])
    mix_fn = partial(mixer, heads=H, block=SPAN)
    expert_ids = jnp.arange(experts, dtype=jnp.int32)
    owners = jnp.arange(length * picks, dtype=jnp.int32) // picks
    outputs = []
    input_grads = []
    for turn in range(micro):
        dense = (
            lax.all_gather(norm_in, ("dp", "expert"), axis=0, tiled=True),
            lax.all_gather(in_proj, ("dp", "expert"), axis=0, tiled=True),
            lax.all_gather(mixer_gain, ("dp", "expert"), axis=0, tiled=True),
            lax.all_gather(out_proj, ("dp", "expert"), axis=0, tiled=True),
            lax.all_gather(norm_mid, ("dp", "expert"), axis=0, tiled=True),
            lax.all_gather(router, ("dp", "expert"), axis=0, tiled=True),
            lax.all_gather(shared_gate, ("dp", "expert"), axis=0, tiled=True),
            lax.all_gather(shared_up, ("dp", "expert"), axis=0, tiled=True),
            lax.all_gather(shared_down, ("dp", "expert"), axis=0, tiled=True),
        )
        banks = (
            lax.all_gather(expert_gate, "dp", axis=1, tiled=True),
            lax.all_gather(expert_up, "dp", axis=1, tiled=True),
            lax.all_gather(expert_down, "dp", axis=1, tiled=True),
        )
        (
            gain_in,
            proj_in,
            gain_mix,
            proj_out,
            gain_mid,
            route_proj,
            gate_proj,
            up_proj,
            down_proj,
        ) = dense
        gate_bank, up_bank, down_bank = banks
        start_in = block_input[turn].astype(f32)
        normed, norm_in_back = jax.vjp(rms_scale, start_in, gain_in.astype(f32))
        normed_low = normed.astype(b16)
        merged = jnp.dot(normed_low, proj_in, preferred_element_type=f32)
        mixed, mixer_back = jax.vjp(
            mix_fn,
            merged,
            conv_kernel,
            conv_shift,
            step_shift,
            rate_log,
            skip_scale,
            gain_mix.astype(f32),
        )
        mixed_low = mixed.astype(b16)
        middle = start_in + jnp.dot(mixed_low, proj_out, preferred_element_type=f32)
        normed_mid, norm_mid_back = jax.vjp(rms_scale, middle, gain_mid.astype(f32))
        routed = normed_mid.astype(b16)
        logits = jnp.dot(routed, route_proj, preferred_element_type=f32)
        route_ids = routes[turn]
        chosen = (route_ids[..., None] == expert_ids).astype(f32)
        picked = jnp.sum(chosen * logits[:, None, :], axis=-1)
        gates = jax.nn.softmax(picked, axis=-1)
        shared_pre = jnp.dot(routed, gate_proj, preferred_element_type=f32)
        shared_lin = jnp.dot(routed, up_proj, preferred_element_type=f32)
        shared_hidden = (jax.nn.silu(shared_pre) * shared_lin).astype(b16)
        shared_out = jnp.dot(shared_hidden, down_proj, preferred_element_type=f32)
        flat_ids = route_ids.reshape(length * picks)
        marks = (flat_ids[:, None] == expert_ids).astype(jnp.int32)
        before = jnp.cumsum(marks, axis=0) - marks
        places = flat_ids * capacity + jnp.sum(before * marks, axis=1)
        outgoing = jnp.zeros((experts * capacity, width), b16).at[places].set(routed[owners])
        arrived = lax.all_to_all(
            outgoing.reshape(experts, capacity, width),
            "expert",
            split_axis=0,
            concat_axis=0,
            tiled=True,
        )
        arrived = arrived.reshape(-1, local_experts, capacity, width)
        pre_gate = jnp.einsum("secd,edf->secf", arrived, gate_bank, preferred_element_type=f32)
        pre_up = jnp.einsum("secd,edf->secf", arrived, up_bank, preferred_element_type=f32)
        expert_hidden = (jax.nn.silu(pre_gate) * pre_up).astype(b16)
        produced = jnp.einsum(
            "secf,efd->secd", expert_hidden, down_bank, preferred_element_type=f32
        ).astype(b16)
        returned = lax.all_to_all(
            produced.reshape(experts, capacity, width),
            "expert",
            split_axis=0,
            concat_axis=0,
            tiled=True,
        )
        taken = (
            returned.reshape(experts * capacity, width)[places]
            .reshape(length, picks, width)
            .astype(f32)
        )
        expert_sum = jnp.sum(gates[..., None] * taken, axis=1)
        outputs.append((middle + expert_sum + shared_out).astype(b16))
        dense = (
            lax.all_gather(norm_in, ("dp", "expert"), axis=0, tiled=True),
            lax.all_gather(in_proj, ("dp", "expert"), axis=0, tiled=True),
            lax.all_gather(mixer_gain, ("dp", "expert"), axis=0, tiled=True),
            lax.all_gather(out_proj, ("dp", "expert"), axis=0, tiled=True),
            lax.all_gather(norm_mid, ("dp", "expert"), axis=0, tiled=True),
            lax.all_gather(router, ("dp", "expert"), axis=0, tiled=True),
            lax.all_gather(shared_gate, ("dp", "expert"), axis=0, tiled=True),
            lax.all_gather(shared_up, ("dp", "expert"), axis=0, tiled=True),
            lax.all_gather(shared_down, ("dp", "expert"), axis=0, tiled=True),
        )
        banks = (
            lax.all_gather(expert_gate, "dp", axis=1, tiled=True),
            lax.all_gather(expert_up, "dp", axis=1, tiled=True),
            lax.all_gather(expert_down, "dp", axis=1, tiled=True),
        )
        (
            gain_in,
            proj_in,
            gain_mix,
            proj_out,
            gain_mid,
            route_proj,
            gate_proj,
            up_proj,
            down_proj,
        ) = dense
        gate_bank, up_bank, down_bank = banks
        grad_out = out_grad[turn].astype(f32)
        grad_low = grad_out.astype(b16)
        shared_hidden_grad = jnp.einsum(
            "ld,fd->lf", grad_low, down_proj, preferred_element_type=f32
        )
        shared_pre_grad = (shared_hidden_grad * shared_lin * silu_slope(shared_pre)).astype(b16)
        shared_lin_grad = (shared_hidden_grad * jax.nn.silu(shared_pre)).astype(b16)
        routed_grad = jnp.einsum(
            "lf,df->ld", shared_pre_grad, gate_proj, preferred_element_type=f32
        )
        routed_grad = routed_grad + jnp.einsum(
            "lf,df->ld", shared_lin_grad, up_proj, preferred_element_type=f32
        )
        gate_grad = jnp.einsum("lkd,ld->lk", taken, grad_out)
        picked_grad = gates * (gate_grad - jnp.sum(gates * gate_grad, axis=-1, keepdims=True))
        logit_grad = jnp.einsum("lk,lke->le", picked_grad, chosen).astype(b16)
        routed_grad = routed_grad + jnp.einsum(
            "le,de->ld", logit_grad, route_proj, preferred_element_type=f32
        )
        sent_grad = (
            (gates[..., None] * grad_out[:, None, :]).astype(b16).reshape(length * picks, width)
        )
        outgoing_grad = jnp.zeros((experts * capacity, width), b16).at[places].set(sent_grad)
        arrived_grad = lax.all_to_all(
            outgoing_grad.reshape(experts, capacity, width),
            "expert",
            split_axis=0,
            concat_axis=0,
            tiled=True,
        )
        arrived_grad = arrived_grad.reshape(-1, local_experts, capacity, width)
        hidden_grad = jnp.einsum(
            "secd,efd->secf", arrived_grad, down_bank, preferred_element_type=f32
        )
        gate_pre_grad = (hidden_grad * pre_up * silu_slope(pre_gate)).astype(b16)
        up_pre_grad = (hidden_grad * jax.nn.silu(pre_gate)).astype(b16)
        expert_in_grad = jnp.einsum(
            "secf,edf->secd", gate_pre_grad, gate_bank, preferred_element_type=f32
        )
        expert_in_grad = expert_in_grad + jnp.einsum(
            "secf,edf->secd", up_pre_grad, up_bank, preferred_element_type=f32
        )
        back_grad = lax.all_to_all(
            expert_in_grad.astype(b16).reshape(experts, capacity, width),
            "expert",
            split_axis=0,
            concat_axis=0,
            tiled=True,
        )
        route_back = back_grad.reshape(experts * capacity, width)[places].astype(f32)
        routed_grad = routed_grad + jnp.sum(route_back.reshape(length, picks, width), axis=1)
        middle_part, gain_mid_grad = norm_mid_back(routed_grad)
        gain_mid_sum = gain_mid_sum + gain_mid_grad
        middle_grad = grad_out + middle_part
        middle_low = middle_grad.astype(b16)
        mixed_grad = jnp.einsum("ld,zd->lz", middle_low, proj_out, preferred_element_type=f32)
        merged_grad, kernel_grad, shift_grad, step_grad, rate_grad, skip_grad, mix_gain_grad = (
            mixer_back(mixed_grad)
        )
        small_sums[0] = small_sums[0] + kernel_grad
        small_sums[1] = small_sums[1] + shift_grad
        small_sums[2] = small_sums[2] + step_grad
        small_sums[3] = small_sums[3] + rate_grad
        small_sums[4] = small_sums[4] + skip_grad
        gain_mix_sum = gain_mix_sum + mix_gain_grad
        merged_low = merged_grad.astype(b16)
        normed_grad = jnp.einsum("lz,dz->ld", merged_low, proj_in, preferred_element_type=f32)
        input_part, gain_in_grad = norm_in_back(normed_grad)
        gain_in_sum = gain_in_sum + gain_in_grad
        input_grads.append(middle_grad + input_part)
        kept_normed.append(normed_low)
        kept_merged.append(merged_low)
        kept_mixed.append(mixed_low)
        kept_middle.append(middle_low)
        kept_routed.append(routed)
        kept_logit.append(logit_grad)
        kept_spre.append(shared_pre_grad)
        kept_slin.append(shared_lin_grad)
        kept_shid.append(shared_hidden)
        kept_dout.append(grad_low)
        kept_arrived.append(arrived)
        kept_gpre.append(gate_pre_grad)
        kept_upre.append(up_pre_grad)
        kept_ehid.append(expert_hidden)
        kept_agrad.append(arrived_grad)
    normed_all = jnp.concatenate(kept_normed, axis=0)
    routed_all = jnp.concatenate(kept_routed, axis=0)
    in_proj_grad = jnp.einsum(
        "ld,lz->dz", normed_all, jnp.concatenate(kept_merged, axis=0), preferred_element_type=f32
    )
    out_proj_grad = jnp.einsum(
        "lz,ld->zd",
        jnp.concatenate(kept_mixed, axis=0),
        jnp.concatenate(kept_middle, axis=0),
        preferred_element_type=f32,
    )
    router_grad = jnp.einsum(
        "ld,le->de", routed_all, jnp.concatenate(kept_logit, axis=0), preferred_element_type=f32
    )
    shared_gate_grad = jnp.einsum(
        "ld,lf->df", routed_all, jnp.concatenate(kept_spre, axis=0), preferred_element_type=f32
    )
    shared_up_grad = jnp.einsum(
        "ld,lf->df", routed_all, jnp.concatenate(kept_slin, axis=0), preferred_element_type=f32
    )
    shared_down_grad = jnp.einsum(
        "lf,ld->fd",
        jnp.concatenate(kept_shid, axis=0),
        jnp.concatenate(kept_dout, axis=0),
        preferred_element_type=f32,
    )
    arrived_all = jnp.concatenate(kept_arrived, axis=0)
    bank_gate_grad = jnp.einsum(
        "secd,secf->def",
        arrived_all,
        jnp.concatenate(kept_gpre, axis=0),
        preferred_element_type=f32,
    )
    bank_up_grad = jnp.einsum(
        "secd,secf->def",
        arrived_all,
        jnp.concatenate(kept_upre, axis=0),
        preferred_element_type=f32,
    )
    bank_down_grad = jnp.einsum(
        "secf,secd->fed",
        jnp.concatenate(kept_ehid, axis=0),
        jnp.concatenate(kept_agrad, axis=0),
        preferred_element_type=f32,
    )
    dense_out = (
        lax.psum_scatter(gain_in_sum, ("dp", "expert"), scatter_dimension=0, tiled=True),
        lax.psum_scatter(in_proj_grad, ("dp", "expert"), scatter_dimension=0, tiled=True),
        lax.psum_scatter(gain_mix_sum, ("dp", "expert"), scatter_dimension=0, tiled=True),
        lax.psum_scatter(out_proj_grad, ("dp", "expert"), scatter_dimension=0, tiled=True),
        lax.psum_scatter(gain_mid_sum, ("dp", "expert"), scatter_dimension=0, tiled=True),
        lax.psum_scatter(router_grad, ("dp", "expert"), scatter_dimension=0, tiled=True),
        lax.psum_scatter(shared_gate_grad, ("dp", "expert"), scatter_dimension=0, tiled=True),
        lax.psum_scatter(shared_up_grad, ("dp", "expert"), scatter_dimension=0, tiled=True),
        lax.psum_scatter(shared_down_grad, ("dp", "expert"), scatter_dimension=0, tiled=True),
    )
    bank_out = (
        lax.psum_scatter(
            bank_gate_grad.astype(jnp.bfloat16), "dp", scatter_dimension=0, tiled=True
        ).astype(jnp.float32),
        lax.psum_scatter(
            bank_up_grad.astype(jnp.bfloat16), "dp", scatter_dimension=0, tiled=True
        ).astype(jnp.float32),
        lax.psum_scatter(
            bank_down_grad.astype(jnp.bfloat16), "dp", scatter_dimension=0, tiled=True
        ).astype(jnp.float32),
    )
    small_out = lax.psum(
        (small_sums[0], small_sums[1], small_sums[2], small_sums[3], small_sums[4]),
        ("dp", "expert"),
    )
    return (
        jnp.stack(outputs),
        jnp.stack(input_grads),
        dense_out[0],
        dense_out[1],
        small_out[0],
        small_out[1],
        small_out[2],
        small_out[3],
        small_out[4],
        dense_out[2],
        dense_out[3],
        dense_out[4],
        dense_out[5],
        dense_out[6],
        dense_out[7],
        dense_out[8],
        bank_out[0].transpose(1, 0, 2),
        bank_out[1].transpose(1, 0, 2),
        bank_out[2].transpose(1, 0, 2),
    )


def solution(mesh):
    in_specs = (
        P(None, ("dp", "expert"), None),
        P(None, ("dp", "expert"), None),
        P(None, ("dp", "expert"), None),
        P(("dp", "expert")),
        P(("dp", "expert"), None),
        P(),
        P(),
        P(),
        P(),
        P(),
        P(("dp", "expert")),
        P(("dp", "expert"), None),
        P(("dp", "expert")),
        P(("dp", "expert"), None),
        P(("dp", "expert"), None),
        P(("dp", "expert"), None),
        P(("dp", "expert"), None),
        P("expert", "dp", None),
        P("expert", "dp", None),
        P("expert", "dp", None),
    )
    out_specs = (
        P(None, ("dp", "expert"), None),
        P(None, ("dp", "expert"), None),
        P(("dp", "expert")),
        P(("dp", "expert"), None),
        P(),
        P(),
        P(),
        P(),
        P(),
        P(("dp", "expert")),
        P(("dp", "expert"), None),
        P(("dp", "expert")),
        P(("dp", "expert"), None),
        P(("dp", "expert"), None),
        P(("dp", "expert"), None),
        P(("dp", "expert"), None),
        P("expert", "dp", None),
        P("expert", "dp", None),
        P("expert", "dp", None),
    )
    return jax.shard_map(body, mesh=mesh, in_specs=in_specs, out_specs=out_specs, check_vma=False)
```

profile of v0, /device:TPU:0, one launch (start us, length us, event | category | flops | bytes accessed | tf_op | source)
XLA Modules:
  0.0 2899.6 jit_solution(10605026215633880718)
XLA Ops:
  14.3 43.0 %all-reduce.41 = (bf16[1536]{0:T(1024)(128)(2,1)S(1)}, bf16[3072]{0:T(1024)(128)(2,1)S(1)}, bf16[1536]{0:T(1024)(128)(2,1)S(1)}) all-reduce(bf16[1536]{0:T(1024)(128)(2,1)S(1)} %dynamic-update-slice, bf16[3072]{0:T(1024)(128)(2,1)S(1)} %dynamic-update-slice.1, ...), channel_id=1, replica_groups=mesh['dp'=4,'expert'=8] {'dp','expert'}, use_global_device_ids=true, to_apply=%add.34 | all-reduce | flops 6144 | bytes 24576
  64.3 80.9 %all-gather.10.cloned.1.call-done = bf16[1536,6448]{1,0:T(8,128)(2,1)} async-done(((bf16[48,6448]{1,0:T(8,128)(2,1)}), bf16[1536,6448]{1,0:T(8,128)(2,1)}) %all-gather.10.cloned.1.call-update) | async-done | bytes 19808272 | tf_op jit(solution)/shard_map/all_gather | solution.py:138
  145.2 12.4 fusion.411
  157.8 14.1 fusion.417
  205.1 20.1 while.68
  225.7 13.4 fusion.413
  244.8 8.9 fusion.107
  283.3 20.0 while.69
  304.0 13.2 fusion.419
  321.9 8.9 fusion.106
  355.1 19.0 scatter_custom_fusion
  385.1 45.5 %all-to-all-done = bf16[32,36,1536]{2,1,0:T(8,128)(2,1)} async-done(((bf16[32,36,1536]{2,1,0:T(8,128)(2,1)}), bf16[32,36,1536]{2,1,0:T(8,128)(2,1)}, u32[]{:S(2)}, u32[]{:S(2)}) %all-to-all-start) | async-done | bytes 3538976 | tf_op jit(solution)/shard_map/all_to_all | solution.py:196
  438.4 20.4 all-gather.16.cloned.1.call-done
  467.3 106.4 %all-gather.18.cloned.1.call-done = bf16[4,512,1536]{2,1,0:T(8,128)(2,1)} async-done(((bf16[4,128,1536]{2,1,0:T(8,128)(2,1)}), bf16[4,512,1536]{2,1,0:T(8,128)(2,1)}) %all-gather.18.cloned.1.call-update) | async-done | bytes 6291472 | tf_op jit(solution)/shard_map/all_gather | solution.py:150
  597.2 68.2 %all-gather = bf16[32,48,32]{1,2,0:T(8,128)(2,1)S(1)} all-gather(bf16[1,48,32]{1,2,0:T(8,128)(2,1)S(1)} %bitcast.715), channel_id=1, replica_groups=mesh['dp'=4,'expert'=8] {'dp','expert'}, dimensions={0}, use_global_device_ids=true | all-gather | bytes 101376 | tf_op jit(solution)/shard_map/all_gather | solution.py:142
  684.0 12.4 scatter_custom_fusion.2
  707.1 43.6 %all-to-all-done.4 = bf16[32,36,1536]{2,1,0:T(8,128)(2,1)} async-done(((bf16[32,36,1536]{2,1,0:T(8,128)(2,1)}), bf16[32,36,1536]{2,1,0:T(8,128)(2,1)}, u32[]{:S(2)}, u32[]{:S(2)}) %all-to-all-start.4) | async-done | bytes 3538976 | tf_op jit(solution)/shard_map/all_to_all | solution.py:275
  750.7 9.9 fusion.141
  803.4 23.9 all-to-all-done.5
  850.9 19.3 scatter_custom_fusion.1
  876.1 50.6 %all_to_all.40 = bf16[32,36,1536]{2,1,0:T(8,128)(2,1)S(1)} all-to-all(bf16[32,36,1536]{2,1,0:T(8,128)(2,1)} %reshape.698), channel_id=1, replica_groups=mesh['dp'=4,'expert'=8] {'expert'}, dimensions={0} | all-to-all | bytes 7077888 | tf_op jit(solution)/shard_map/all_to_all | solution.py:196
  954.4 34.9 %all-to-all-done.3 = bf16[32,36,1536]{2,1,0:T(8,128)(2,1)} async-done(((bf16[32,36,1536]{2,1,0:T(8,128)(2,1)}), bf16[32,36,1536]{2,1,0:T(8,128)(2,1)}, u32[]{:S(2)}, u32[]{:S(2)}) %all-to-all-start.3) | async-done | bytes 3538976 | tf_op jit(solution)/shard_map/all_to_all | solution.py:210
  1007.3 9.1 scatter_custom_fusion.3
  1019.1 50.5 %all_to_all.41 = bf16[32,36,1536]{2,1,0:T(8,128)(2,1)S(1)} all-to-all(bf16[32,36,1536]{2,1,0:T(8,128)(2,1)} %reshape.715), channel_id=1, replica_groups=mesh['dp'=4,'expert'=8] {'expert'}, dimensions={0} | all-to-all | bytes 7077888 | tf_op jit(solution)/shard_map/all_to_all | solution.py:275
  1069.5 9.4 fusion.138
  1110.4 35.1 %all-to-all-done.7 = bf16[32,36,1536]{2,1,0:T(8,128)(2,1)} async-done(((bf16[32,36,1536]{2,1,0:T(8,128)(2,1)}), bf16[32,36,1536]{2,1,0:T(8,128)(2,1)}, u32[]{:S(2)}, u32[]{:S(2)}) %all-to-all-start.7) | async-done | bytes 3538976 | tf_op jit(solution)/shard_map/all_to_all | solution.py:294
  1203.0 25.5 while.70
  1279.4 25.8 while.71
  1305.2 9.0 multiply_reduce_fusion.2
  1314.2 9.1 fusion.284
  1390.0 10.0 fusion.192
  1452.1 9.8 fusion.427
  1462.1 12.6 fusion.296
  1481.2 10.9 bitcast_convert_fusion.2
  1492.1 8.7 copy.564
  1500.9 10.5 bitcast_convert_fusion.1
  1520.2 10.4 bitcast_convert_fusion
  1530.6 8.7 copy.568
  1554.6 10.7 fusion.209
  1565.5 16.9 fusion.78
  1605.1 111.8 %reduce-scatter.30.cloned.1.call-done = bf16[384,2048]{1,0:T(8,128)(2,1)} async-done(((bf16[1536,2048]{1,0:T(8,128)(2,1)}), bf16[384,2048]{1,0:T(8,128)(2,1)}) %reduce-scatter.30.cloned.1.call-update) | async-done | bytes 1572880
  1723.4 107.0 %reduce-scatter.32.cloned.1.call-done = bf16[384,2048]{1,0:T(8,128)(2,1)} async-done(((bf16[1536,2048]{1,0:T(8,128)(2,1)}), bf16[384,2048]{1,0:T(8,128)(2,1)}) %reduce-scatter.32.cloned.1.call-update) | async-done | bytes 1572880
  1837.0 107.2 %reduce-scatter.34.cloned.1.call-done = bf16[128,6144]{1,0:T(8,128)(2,1)} async-done(((bf16[512,6144]{1,0:T(8,128)(2,1)}), bf16[128,6144]{1,0:T(8,128)(2,1)}) %reduce-scatter.34.cloned.1.call-update) | async-done | bytes 1572880
  1950.7 115.3 %reduce-scatter.22.cloned.1.call-done = f32[48,1024]{1,0:T(8,128)} async-done(((f32[1536,1024]{1,0:T(8,128)}), f32[48,1024]{1,0:T(8,128)}) %reduce-scatter.22.cloned.1.call-update) | async-done | bytes 196624 | tf_op jit(solution)/shard_map/reduce_scatter | solution.py:389
  2066.0 119.6 %reduce-scatter.24.cloned.1.call-done = f32[48,1024]{1,0:T(8,128)} async-done(((f32[1536,1024]{1,0:T(8,128)}), f32[48,1024]{1,0:T(8,128)}) %reduce-scatter.24.cloned.1.call-update) | async-done | bytes 196624 | tf_op jit(solution)/shard_map/reduce_scatter | solution.py:390
  2185.6 120.5 %reduce-scatter.26.cloned.1.call-done = f32[32,1536]{1,0:T(8,128)} async-done(((f32[1024,1536]{1,0:T(8,128)}), f32[32,1536]{1,0:T(8,128)}) %reduce-scatter.26.cloned.1.call-update) | async-done | bytes 196624 | tf_op jit(solution)/shard_map/reduce_scatter | solution.py:391
  2306.1 212.8 %reduce-scatter.20.cloned.1.call-done = f32[96,1536]{1,0:T(8,128)} async-done(((f32[3072,1536]{1,0:T(8,128)}), f32[96,1536]{1,0:T(8,128)}) %reduce-scatter.20.cloned.1.call-update) | async-done | bytes 589840 | tf_op jit(solution)/shard_map/reduce_scatter | solution.py:386
  2518.9 370.8 %reduce-scatter.18.cloned.1.call-done = f32[48,6448]{1,0:T(8,128)} async-done(((f32[1536,6448]{1,0:T(8,128)}), f32[48,6448]{1,0:T(8,128)}) %reduce-scatter.18.cloned.1.call-update) | async-done | bytes 1238032 | tf_op jit(solution)/shard_map/reduce_scatter | solution.py:384
  (986 shorter events, 735.9 us)
Async XLA Ops:
  7.2 137.9 %all-gather.10.cloned.1.call-start = ((), (), s32[]{:S(2)}) async-start(), calls=%async_computation.17 | async-start | bytes 20680704 | tf_op jit(solution)/shard_map/all_gather | solution.py:138
  8.0 339.8 %all-gather.12.cloned.1.call-start = ((), (), s32[]{:S(2)}) async-start(), calls=%async_computation.18 | async-start | bytes 9732096 | tf_op jit(solution)/shard_map/all_gather | solution.py:140
  8.8 376.3 %all-gather.14.cloned.1.call-start = ((), (), s32[]{:S(2)}) async-start(), calls=%async_computation.19 | async-start | bytes 7864320 | tf_op jit(solution)/shard_map/all_gather | solution.py:148
  9.5 449.3 %all-gather.16.cloned.1.call-start = ((), (), s32[]{:S(2)}) async-start(), calls=%async_computation.20 | async-start | bytes 7864320 | tf_op jit(solution)/shard_map/all_gather | solution.py:149
  10.1 563.7 %all-gather.18.cloned.1.call-start = ((), (), s32[]{:S(2)}) async-start(), calls=%async_computation.21 | async-start | bytes 7864320 | tf_op jit(solution)/shard_map/all_gather | solution.py:150
  10.7 778.4 %all-gather.20.cloned.1.call-start = ((), (), s32[]{:S(2)}) async-start(), calls=%async_computation.22 | async-start | bytes 3244032 | tf_op jit(solution)/shard_map/all_gather | solution.py:143
  11.3 310.0 %copy-start.100 = (f32[64,64]{1,0:T(8,128)}, f32[64,64]{1,0:T(8,128)S(1)}, u32[]{:S(2)}) copy-start(f32[64,64]{1,0:T(8,128)S(1)} %fusion.356) | copy-start | bytes 49156
  57.4 100.2 %copy-start.159 = (f32[1536]{0:T(1024)}, f32[1536]{0:T(1024)S(1)}, u32[]{:S(2)}) copy-start(f32[1536]{0:T(1024)S(1)} %convert_element_type.244) | copy-start | bytes 18436
  57.6 100.0 %copy-start.213 = (f32[128]{0:T(128)}, f32[128]{0:T(128)S(1)}, u32[]{:S(2)}) copy-start(f32[128]{0:T(128)S(1)} %fusion.369) | copy-start | bytes 1540
  57.7 99.9 %copy-start.215 = (f32[128]{0:T(128)}, f32[128]{0:T(128)S(1)}, u32[]{:S(2)}) copy-start(f32[128]{0:T(128)S(1)} %fusion.372) | copy-start | bytes 1540
  58.2 122.0 %copy-start.221 = (f32[48]{0:T(128)}, f32[48]{0:T(128)S(1)}, u32[]{:S(2)}) copy-start(f32[48]{0:T(128)S(1)} %fusion.368) | copy-start | bytes 580
  58.2 122.0 %copy-start.223 = (f32[48]{0:T(128)}, f32[48]{0:T(128)S(1)}, u32[]{:S(2)}) copy-start(f32[48]{0:T(128)S(1)} %convert_element_type.247) | copy-start | bytes 580
  58.4 113.6 %copy-start.167 = (f32[3328]{0:T(1024)}, f32[3328]{0:T(1024)S(1)}, u32[]{:S(2)}) copy-start(f32[3328]{0:T(1024)S(1)} %get-tuple-element.687) | copy-start | bytes 39940
  58.4 113.6 %copy-start.169 = (f32[3328]{0:T(1024)}, f32[3328]{0:T(1024)S(1)}, u32[]{:S(2)}) copy-start(f32[3328]{0:T(1024)S(1)} %get-tuple-element.688) | copy-start | bytes 39940
  58.4 113.6 %copy-start.171 = (f32[3328]{0:T(1024)}, f32[3328]{0:T(1024)S(1)}, u32[]{:S(2)}) copy-start(f32[3328]{0:T(1024)S(1)} %get-tuple-element.689) | copy-start | bytes 39940
  58.4 113.6 %copy-start.173 = (f32[3328]{0:T(1024)}, f32[3328]{0:T(1024)S(1)}, u32[]{:S(2)}) copy-start(f32[3328]{0:T(1024)S(1)} %get-tuple-element.690) | copy-start | bytes 39940
  64.3 93.3 %copy-start.79 = (bf16[128,1536]{1,0:T(8,128)(2,1)}, bf16[128,1536]{1,0:T(8,128)(2,1)S(1)}, u32[]{:S(2)}) copy-start(bf16[128,1536]{1,0:T(8,128)(2,1)S(1)} %get-tuple-element.813) | copy-start | bytes 1179652
  64.3 93.5 %copy-start.80 = (bf16[128,1536]{1,0:T(8,128)(2,1)}, bf16[128,1536]{1,0:T(8,128)(2,1)S(1)}, u32[]{:S(2)}) copy-start(bf16[128,1536]{1,0:T(8,128)(2,1)S(1)} %get-tuple-element.814) | copy-start | bytes 1179652
  185.2 136.0 %copy-start.108 = (f32[2,64,48]{1,2,0:T(8,128)}, f32[2,64,48]{1,2,0:T(8,128)S(1)}, u32[]{:S(2)}) copy-start(f32[2,64,48]{1,2,0:T(8,128)S(1)} %copy.367) | copy-start | bytes 73732
  355.1 310.8 %copy-start.35 = (bf16[128,1536]{1,0:T(8,128)(2,1)}, bf16[128,1536]{1,0:T(8,128)(2,1)S(1)}, u32[]{:S(2)}) copy-start(bf16[128,1536]{1,0:T(8,128)(2,1)S(1)} %multiply_convert_fusion.7) | copy-start | bytes 1179652
  379.8 50.9 %all-to-all-start = ((bf16[32,36,1536]{2,1,0:T(8,128)(2,1)}), bf16[32,36,1536]{2,1,0:T(8,128)(2,1)}, u32[]{:S(2)}, u32[]{:S(2)}) async-start(bf16[32,36,1536]{2,1,0:T(8,128)(2,1)} %reshape.687), calls=%async_computation | async-start | bytes 7864320 | tf_op jit(solution)/shard_map/all_to_all | solution.py:196
  384.3 408.0 %all-gather.22.cloned.1.call-start = ((), (), s32[]{:S(2)}) async-start(), calls=%async_computation.23 | async-start | bytes 3244032 | tf_op jit(solution)/shard_map/all_gather | solution.py:144
  467.3 111.4 %copy-start.104 = (bf16[8,4,36,512]{3,2,0,1:T(8,128)(2,1)}, bf16[8,4,36,512]{3,2,0,1:T(8,128)(2,1)S(1)}, u32[]{:S(2)}) copy-start(bf16[8,4,36,512]{3,2,0,1:T(8,128)(2,1)S(1)} %get-tuple-element.854) | copy-start | bytes 3538948
  581.1 85.6 %all-to-all-start.1 = ((bf16[32,36,1536]{2,1,0:T(8,128)(2,1)}), bf16[32,36,1536]{2,1,0:T(8,128)(2,1)}, u32[]{:S(2)}, u32[]{:S(2)}) async-start(bf16[32,36,1536]{2,1,0:T(8,128)(2,1)} %bitcast.665), calls=%async_computation.1 | async-start | bytes 7864320 | tf_op jit(solution)/shard_map/all_to_all | solution.py:210
  590.7 75.4 %copy-start.188 = (s32[128,6]{0,1:T(8,128)S(1)}, s32[128,6]{0,1:T(8,128)}, u32[]{:S(2)}) copy-start(s32[128,6]{0,1:T(8,128)} %get-tuple-element.843) | copy-start | bytes 9220
  699.0 67.1 %slice-start.9 = ((s8[6291456]{0:T(1024)(128)(4,1)}), s8[2097152]{0:T(1024)(128)(4,1)S(1)}, s32[]{:S(2)}) async-start(s8[6291456]{0:T(1024)(128)(4,1)} %bitcast.653), calls=%async_computation.44 | async-start | bytes 4194304
  699.0 51.7 %all-to-all-start.4 = ((bf16[32,36,1536]{2,1,0:T(8,128)(2,1)}), bf16[32,36,1536]{2,1,0:T(8,128)(2,1)}, u32[]{:S(2)}, u32[]{:S(2)}) async-start(bf16[32,36,1536]{2,1,0:T(8,128)(2,1)} %reshape.703), calls=%async_computation.4 | async-start | bytes 7864320 | tf_op jit(solution)/shard_map/all_to_all | solution.py:275
  703.7 92.0 %all-gather.24.cloned.1.call-start = ((), (), s32[]{:S(2)}) async-start(), calls=%async_computation.24 | async-start | bytes 3244032 | tf_op jit(solution)/shard_map/all_gather | solution.py:145
  776.1 51.2 %all-to-all-start.5 = ((bf16[32,36,1536]{2,1,0:T(8,128)(2,1)}), bf16[32,36,1536]{2,1,0:T(8,128)(2,1)}, u32[]{:S(2)}, u32[]{:S(2)}) async-start(bf16[32,36,1536]{2,1,0:T(8,128)(2,1)} %bitcast.663), calls=%async_computation.5 | async-start | bytes 7864320 | tf_op jit(solution)/shard_map/all_to_all | solution.py:294
  850.9 102.7 %copy-start.33 = (bf16[128,1536]{1,0:T(8,128)(2,1)}, bf16[128,1536]{1,0:T(8,128)(2,1)S(1)}, u32[]{:S(2)}) copy-start(bf16[128,1536]{1,0:T(8,128)(2,1)S(1)} %get-tuple-element.840) | copy-start | bytes 1179652
  938.3 51.0 %all-to-all-start.3 = ((bf16[32,36,1536]{2,1,0:T(8,128)(2,1)}), bf16[32,36,1536]{2,1,0:T(8,128)(2,1)}, u32[]{:S(2)}, u32[]{:S(2)}) async-start(bf16[32,36,1536]{2,1,0:T(8,128)(2,1)} %bitcast.666), calls=%async_computation.3 | async-start | bytes 7864320 | tf_op jit(solution)/shard_map/all_to_all | solution.py:210
  1019.1 65.3 %slice-start.13 = ((s8[6291456]{0:T(1024)(128)(4,1)}), s8[4194304]{0:T(1024)(128)(4,1)S(1)}, s32[]{:S(2)}) async-start(s8[6291456]{0:T(1024)(128)(4,1)} %bitcast.657), calls=%async_computation.48 | async-start | bytes 8388608
  1094.3 51.1 %all-to-all-start.7 = ((bf16[32,36,1536]{2,1,0:T(8,128)(2,1)}), bf16[32,36,1536]{2,1,0:T(8,128)(2,1)}, u32[]{:S(2)}, u32[]{:S(2)}) async-start(bf16[32,36,1536]{2,1,0:T(8,128)(2,1)} %bitcast.664), calls=%async_computation.7 | async-start | bytes 7864320 | tf_op jit(solution)/shard_map/all_to_all | solution.py:294
  1099.2 494.6 %reduce-scatter.28.cloned.1.call-start = ((), (), s32[]{:S(2)}) async-start(), calls=%async_computation.30 | async-start | bytes 811008
  1108.3 492.9 %all-reduce.44.cloned.1.call-start = ((), (), s32[]{:S(2)}) async-start(), calls=%async_computation.34 | async-start | bytes 199680
  1481.1 235.7 %reduce-scatter.30.cloned.1.call-start = ((), (), s32[]{:S(2)}) async-start(), calls=%async_computation.31 | async-start | bytes 7864320
  1500.9 329.5 %reduce-scatter.32.cloned.1.call-start = ((), (), s32[]{:S(2)}) async-start(), calls=%async_computation.32 | async-start | bytes 7864320
  1520.1 424.0 %reduce-scatter.34.cloned.1.call-start = ((), (), s32[]{:S(2)}) async-start(), calls=%async_computation.33 | async-start | bytes 7864320
  1539.4 526.6 %reduce-scatter.22.cloned.1.call-start = ((), (), s32[]{:S(2)}) async-start(), calls=%async_computation.27 | async-start | bytes 6488064 | tf_op jit(solution)/shard_map/reduce_scatter | solution.py:389
  1544.4 641.1 %reduce-scatter.24.cloned.1.call-start = ((), (), s32[]{:S(2)}) async-start(), calls=%async_computation.28 | async-start | bytes 6488064 | tf_op jit(solution)/shard_map/reduce_scatter | solution.py:390
  1549.4 756.7 %reduce-scatter.26.cloned.1.call-start = ((), (), s32[]{:S(2)}) async-start(), calls=%async_computation.29 | async-start | bytes 6488064 | tf_op jit(solution)/shard_map/reduce_scatter | solution.py:391
  1554.5 964.4 %reduce-scatter.20.cloned.1.call-start = ((), (), s32[]{:S(2)}) async-start(), calls=%async_computation.26 | async-start | bytes 19464192 | tf_op jit(solution)/shard_map/reduce_scatter | solution.py:386
  1565.3 1324.5 %reduce-scatter.18.cloned.1.call-start = ((), (), s32[]{:S(2)}) async-start(), calls=%async_computation.25 | async-start | bytes 41361408 | tf_op jit(solution)/shard_map/reduce_scatter | solution.py:384
  1948.3 941.4 %copy-start.177 = (f32[4,3328]{1,0:T(4,128)S(1)}, f32[4,3328]{1,0:T(4,128)}, u32[]{:S(2)}) copy-start(f32[4,3328]{1,0:T(4,128)} %get-tuple-element.1145) | copy-start | bytes 159748
  1948.3 942.0 %copy-start.200 = (f32[3328]{0:T(1024)S(1)}, f32[3328]{0:T(1024)}, u32[]{:S(2)}) copy-start(f32[3328]{0:T(1024)} %get-tuple-element.1146) | copy-start | bytes 39940
  1948.3 942.6 %copy-start.257 = (f32[48]{0:T(128)S(1)}, f32[48]{0:T(128)}, u32[]{:S(2)}) copy-start(f32[48]{0:T(128)} %get-tuple-element.1147) | copy-start | bytes 580
  1948.4 943.2 %copy-start.256 = (f32[48]{0:T(128)S(1)}, f32[48]{0:T(128)}, u32[]{:S(2)}) copy-start(f32[48]{0:T(128)} %get-tuple-element.1148) | copy-start | bytes 580
  1948.4 943.7 %copy-start.255 = (f32[48]{0:T(128)S(1)}, f32[48]{0:T(128)}, u32[]{:S(2)}) copy-start(f32[48]{0:T(128)} %get-tuple-element.1149) | copy-start | bytes 580
  (261 other events, 2482.0 us)
Sparse Core Ops, SparseCore 0:
  11.0 134.1 all-gather.9
  148.1 80.1 all-gather.11
  229.8 113.9 all-gather.13
  345.2 113.5 all-gather.15
  460.2 113.5 all-gather.17
  576.5 75.1 all-gather.19
  654.6 59.6 all-gather.21
  717.1 67.6 all-gather.23
  1108.4 93.9 reduce-scatter.27
  1481.3 119.9 all-reduce.43
  1605.0 111.8 reduce-scatter.29
  1719.1 111.2 reduce-scatter.31
  1832.8 111.2 reduce-scatter.33
  1951.1 114.8 reduce-scatter.21
  2072.0 113.4 reduce-scatter.23
  2192.6 113.4 reduce-scatter.25
  2312.9 205.9 reduce-scatter.19
  2525.8 363.9 reduce-scatter.17
where the time goes:
time: 2920 us; the launch traced here: 2900 us
  waiting for transfers between devices  1660 us (57%)
  matrix products  422 us (14%)
  local copies, waits for them, and re-layouts  364 us (12%)
  blocking collectives  212 us (7%)
  other arithmetic  191 us (7%)
  starting transfers between devices  29.5 us (1%)
    reduce_scatter x1, waiting for transfers between devices, body(): lax.psum_scatter(in_proj_grad, ('dp', 'expert'), scatter_dimension=0, til...  371 us
    unnamed x23, waiting for transfers between devices  333 us
    reduce_scatter x1, waiting for transfers between devices, body(): lax.psum_scatter(out_proj_grad, ('dp', 'expert'), scatter_dimension=0, ti...  213 us
    reduce_scatter x1, waiting for transfers between devices, body(): lax.psum_scatter(shared_down_grad, ('dp', 'expert'), scatter_dimension=0,...  121 us
    reduce_scatter x1, waiting for transfers between devices, body(): lax.psum_scatter(shared_up_grad, ('dp', 'expert'), scatter_dimension=0, t...  120 us
    reduce_scatter x1, waiting for transfers between devices, body(): lax.psum_scatter(shared_gate_grad, ('dp', 'expert'), scatter_dimension=0,...  115 us
    all_gather x1, waiting for transfers between devices, body(): lax.all_gather(expert_down, 'dp', axis=1, tiled=True)  106 us
    all_gather x1, waiting for transfers between devices, body(): lax.all_gather(in_proj, ('dp', 'expert'), axis=0, tiled=True)  80.9 us
  transfers between devices with their start and end apart: 24, of which 17 were waited for; matrix products, arithmetic and copies ran while one was open for 29% of the time, Pallas kernels for 0%

commit v1 on v0

v1 whole, which is shorter than its diff:
```python
from functools import partial

import jax
import jax.numpy as jnp
from jax import lax
from jax.experimental import pallas as pl
from jax.experimental.pallas import tpu as pltpu
from jax.sharding import PartitionSpec as P

H = 48
LEN = 128
LANES = 128
epsilon = 1e-05
f32 = jnp.float32
b16 = jnp.bfloat16
highest = lax.Precision.HIGHEST
NT = (((1,), (1,)), ((), ()))


def sigmoid(value):
    return 0.5 * jnp.tanh(0.5 * value) + 0.5


def grids():
    row = lax.broadcasted_iota(jnp.int32, (LEN, LANES), 0)
    lane = lax.broadcasted_iota(jnp.int32, (LEN, LANES), 1)
    return row, lane


def shifted(signal, row):
    return [signal] + [jnp.where(row >= k, pltpu.roll(signal, k, 0), 0.0) for k in (1, 2, 3)]


def convolved(parts, weight_ref, bias_ref, block):
    weight = weight_ref[:, block]
    total = bias_ref[:, block] + weight[3:4] * parts[0]
    for k in (1, 2, 3):
        total = total + weight[3 - k : 4 - k] * parts[k]
    return total


def pick(value, lane):
    low = lane < LANES // 2
    return jnp.concatenate([jnp.where(low, value, 0.0), jnp.where(low, 0.0, value)], axis=0)


def step_terms(merged_ref, step_ref, rate_ref, tail):
    raw = merged_ref[:, tail] + step_ref[...]
    step = jnp.maximum(raw, 0.0) + jnp.log1p(jnp.exp(-jnp.abs(raw)))
    decay = -jnp.exp(rate_ref[...]) * step
    row, lane = grids()
    cumul = jnp.dot(
        (row >= lane).astype(f32), decay, precision=highest, preferred_element_type=f32
    )
    return raw, step, decay, cumul


def forward_kernel(
    pairs,
    merged_ref,
    weight_ref,
    bias_ref,
    step_ref,
    rate_ref,
    skip_ref,
    gain_ref,
    mixed_ref,
    joined_ref,
    square_ref,
    cross_ref,
):
    row, lane = grids()
    tail = pl.ds((2 * pairs + 2) * LANES, LANES)
    raw, step, decay, cumul = step_terms(merged_ref, step_ref, rate_ref, tail)
    cross_ref[...] = cumul.T
    maps = []
    for at in (0, 1):
        signal = merged_ref[:, pl.ds((2 * pairs + at) * LANES, LANES)]
        block = pl.ds((pairs + at) * LANES, LANES)
        conv = convolved(shifted(signal, row), weight_ref, bias_ref, block)
        maps.append((conv * sigmoid(conv)).astype(b16))
    inner = lax.dot_general(maps[1], maps[0], NT, preferred_element_type=f32)
    square = jnp.zeros((LEN, LANES), f32)
    for pair in range(pairs):
        block = pl.ds(pair * LANES, LANES)
        signal = merged_ref[:, pl.ds((pairs + pair) * LANES, LANES)]
        conv = convolved(shifted(signal, row), weight_ref, bias_ref, block)
        values = conv * sigmoid(conv)
        steps, parts = [], []
        for head in (2 * pair, 2 * pair + 1):
            steps.append(step[:, head : head + 1])
            spread = cumul[:, head : head + 1] - cross_ref[head : head + 1, :]
            parts.append(inner * jnp.exp(jnp.where(row >= lane, spread, -1e30)))
        scaled = values * jnp.where(lane < LANES // 2, steps[0], steps[1])
        scanned = jnp.dot(
            jnp.concatenate(parts, axis=1).astype(b16),
            pick(scaled, lane).astype(b16),
            preferred_element_type=f32,
        )
        joined = scanned + skip_ref[:, block] * values
        joined_ref[:, block] = joined
        gate = merged_ref[:, block]
        gated = joined * (gate * sigmoid(gate))
        mixed_ref[:, block] = (gated * gain_ref[:, block]).astype(b16)
        square = square + gated * gated
    square_ref[...] = square


def backward_kernel(
    pairs,
    merged_ref,
    joined_ref,
    grad_ref,
    inward_ref,
    weight_ref,
    bias_ref,
    step_ref,
    rate_ref,
    skip_ref,
    gain_ref,
    out_ref,
    weight_out,
    bias_out,
    skip_out,
    head_out,
    cross_ref,
):
    row, lane = grids()
    low = lane < LANES // 2

    @pl.when(pl.program_id(0) == 0)
    def _():
        weight_out[...] = jnp.zeros_like(weight_out)
        bias_out[...] = jnp.zeros_like(bias_out)
        skip_out[...] = jnp.zeros_like(skip_out)
        head_out[...] = jnp.zeros_like(head_out)

    inward = inward_ref[...]
    tail = pl.ds((2 * pairs + 2) * LANES, LANES)
    raw, step, decay, cumul = step_terms(merged_ref, step_ref, rate_ref, tail)
    cross_ref[...] = cumul.T
    convs, slopes, shifts, maps = [], [], [], []
    for at in (0, 1):
        signal = merged_ref[:, pl.ds((2 * pairs + at) * LANES, LANES)]
        parts = shifted(signal, row)
        conv = convolved(parts, weight_ref, bias_ref, pl.ds((pairs + at) * LANES, LANES))
        sigma = sigmoid(conv)
        shifts.append(parts)
        slopes.append(sigma * (1.0 + conv * (1.0 - sigma)))
        maps.append((conv * sigma).astype(b16))
    flipped = lax.dot_general(maps[0], maps[1], NT, preferred_element_type=f32)
    dinner = jnp.zeros((LEN, LEN), f32)
    dstep = jnp.zeros((LEN, LANES), f32)
    dcum = jnp.zeros((LEN, LANES), f32)

    def back_conv(grad, parts, block, out_block):
        bias_out[:, block] += jnp.sum(grad, axis=0, keepdims=True)
        weight = weight_ref[:, block]
        total = weight[3:4] * grad
        taps = [jnp.sum(grad * parts[3 - k], axis=0, keepdims=True) for k in range(4)]
        weight_out[:, block] += jnp.concatenate(taps, axis=0)
        for k in (1, 2, 3):
            later = jnp.where(row < LEN - k, pltpu.roll(grad, LEN - k, 0), 0.0)
            total = total + weight[3 - k : 4 - k] * later
        out_ref[:, out_block] = total.astype(b16)

    for pair in range(pairs):
        block = pl.ds(pair * LANES, LANES)
        other = pl.ds((pairs + pair) * LANES, LANES)
        gate = merged_ref[:, block]
        joined = joined_ref[:, block]
        sigma = sigmoid(gate)
        soft = gate * sigma
        dgated = grad_ref[:, block] * gain_ref[:, block] - joined * soft * inward
        djoined = dgated * soft
        out_ref[:, block] = (dgated * joined * (sigma + soft * (1.0 - sigma))).astype(b16)

        parts = shifted(merged_ref[:, other], row)
        conv = convolved(parts, weight_ref, bias_ref, block)
        csig = sigmoid(conv)
        values = conv * csig
        skip = skip_ref[:, block]
        skip_out[:, block] += jnp.sum(djoined * values, axis=0, keepdims=True)
        scanned = joined - skip * values
        steps, blends, spreads = [], [], []
        for head in (2 * pair, 2 * pair + 1):
            steps.append(step[:, head : head + 1])
            spread = cumul[:, head : head + 1] - cross_ref[head : head + 1, :]
            spreads.append(jnp.exp(jnp.where(row >= lane, spread, -1e30)))
            blends.append(flipped * jnp.exp(jnp.where(row <= lane, -spread, -1e30)))
        widened = jnp.where(low, steps[0], steps[1])
        scaled = (values * widened).astype(b16)
        dlow = djoined.astype(b16)
        both = pick(djoined, lane).astype(b16)
        dweights = lax.dot_general(both, scaled, NT, preferred_element_type=f32)
        dinner = dinner + dweights[:LEN] * spreads[0] + dweights[LEN:] * spreads[1]
        dscaled = jnp.dot(
            jnp.concatenate(blends, axis=1).astype(b16), both, preferred_element_type=f32
        )
        dvalues = skip * djoined + dscaled * widened
        first = dscaled * values
        second = dlow.astype(f32) * scanned - scaled.astype(f32) * dscaled
        for at in (0, 1):
            mine = low if at == 0 else jnp.logical_not(low)
            here = lane == 2 * pair + at
            total = jnp.sum(jnp.where(mine, first, 0.0), axis=1, keepdims=True)
            dstep = jnp.where(here, total, dstep)
            total = jnp.sum(jnp.where(mine, second, 0.0), axis=1, keepdims=True)
            dcum = jnp.where(here, total, dcum)
        back_conv(dvalues * (csig * (1.0 + conv * (1.0 - csig))), parts, block, other)
    dmaps = (
        jnp.dot(dinner.T.astype(b16), maps[1], preferred_element_type=f32),
        jnp.dot(dinner.astype(b16), maps[0], preferred_element_type=f32),
    )
    for at in (0, 1):
        back_conv(
            dmaps[at] * slopes[at],
            shifts[at],
            pl.ds((pairs + at) * LANES, LANES),
            pl.ds((2 * pairs + at) * LANES, LANES),
        )
    ddecay = jnp.dot(
        (row <= lane).astype(f32), dcum, precision=highest, preferred_element_type=f32
    )
    dstep = dstep - ddecay * jnp.exp(rate_ref[...])
    draw = jnp.where(lane < 2 * pairs, dstep * sigmoid(raw), 0.0)
    out_ref[:, tail] = draw.astype(b16)
    head_out[0:1, :] += jnp.sum(draw, axis=0, keepdims=True)
    head_out[1:2, :] += jnp.sum(ddecay * decay, axis=0, keepdims=True)


def rows_of(columns):
    return pl.BlockSpec((LEN, columns), lambda s: (s, 0))


def fixed(rows, columns):
    return pl.BlockSpec((rows, columns), lambda s: (0, 0))


def mix_forward(merged, params):
    tokens, columns = merged.shape
    width = params[-1].shape[1]
    return pl.pallas_call(
        partial(forward_kernel, width // LANES),
        grid=(tokens // LEN,),
        in_specs=[rows_of(columns)] + [fixed(*p.shape) for p in params],
        out_specs=[rows_of(width), rows_of(width), rows_of(LANES)],
        out_shape=[
            jax.ShapeDtypeStruct((tokens, width), b16),
            jax.ShapeDtypeStruct((tokens, width), f32),
            jax.ShapeDtypeStruct((tokens, LANES), f32),
        ],
        scratch_shapes=[pltpu.VMEM((LANES, LEN), f32)],
        compiler_params=pltpu.CompilerParams(vmem_limit_bytes=32 << 20),
        cost_estimate=pl.CostEstimate(
            flops=tokens * width * 9000, bytes_accessed=tokens * columns * 8, transcendentals=0
        ),
    )(merged, *params)


def mix_backward(merged, joined, grad, inward, params):
    tokens, columns = merged.shape
    width = params[-1].shape[1]
    conv = params[0].shape[1]
    return pl.pallas_call(
        partial(backward_kernel, width // LANES),
        grid=(tokens // LEN,),
        in_specs=[rows_of(columns), rows_of(width), rows_of(width), rows_of(1)]
        + [fixed(*p.shape) for p in params],
        out_specs=[
            rows_of(columns),
            fixed(4, conv),
            fixed(1, conv),
            fixed(1, width),
            fixed(8, LANES),
        ],
        out_shape=[
            jax.ShapeDtypeStruct((tokens, columns), b16),
            jax.ShapeDtypeStruct((4, conv), f32),
            jax.ShapeDtypeStruct((1, conv), f32),
            jax.ShapeDtypeStruct((1, width), f32),
            jax.ShapeDtypeStruct((8, LANES), f32),
        ],
        scratch_shapes=[pltpu.VMEM((LANES, LEN), f32)],
        compiler_params=pltpu.CompilerParams(vmem_limit_bytes=32 << 20),
        cost_estimate=pl.CostEstimate(
            flops=tokens * width * 18000, bytes_accessed=tokens * columns * 12, transcendentals=0
        ),
    )(merged, joined, grad, inward, *params)


MESH = pl.DeviceIdType.MESH


def neighbours(me):
    core, column, line = me % 2, (me // 2) % 2, me // 4
    return 1 - 2 * core, 2 - 4 * column, 4 - 8 * line


def greet(peers):
    barrier = pltpu.get_barrier_semaphore()
    for peer in peers:
        pl.semaphore_signal(barrier, inc=1, device_id={"expert": peer}, device_id_type=MESH)
    pl.semaphore_wait(barrier, len(peers))


def gather_kernel(own_ref, out_ref, send_sem, recv_sem, copy_sem):
    me = lax.axis_index("expert")
    core, column, line = neighbours(me)
    rows = own_ref.shape[0]
    top, bottom = pl.ds(0, rows // 2), pl.ds(rows // 2, rows // 2)
    greet((me + core, me + column, me + line))

    def copy(at, src, dst, peer):
        return pltpu.make_async_remote_copy(
            src_ref=src,
            dst_ref=dst,
            send_sem=send_sem.at[at],
            recv_sem=recv_sem.at[at],
            device_id={"expert": peer},
            device_id_type=MESH,
        )

    here = pltpu.make_async_copy(own_ref, out_ref.at[me], copy_sem)
    to_x = copy(0, own_ref, out_ref.at[me], me + column)
    to_y = copy(1, own_ref, out_ref.at[me], me + line)
    to_core = copy(2, own_ref, out_ref.at[me], me + core)
    to_x.start()
    to_y.start()
    to_core.start()
    here.start()
    x_block, y_block = out_ref.at[me + column], out_ref.at[me + line]
    diagonal = out_ref.at[me + column + line]
    to_x.wait_recv()
    x_relay = copy(3, x_block.at[top], x_block.at[top], me + line)
    x_relay.start()
    x_core = copy(5, x_block, x_block, me + core)
    x_core.start()
    to_y.wait_recv()
    y_relay = copy(4, y_block.at[bottom], y_block.at[bottom], me + column)
    y_relay.start()
    y_core = copy(6, y_block, y_block, me + core)
    y_core.start()
    x_relay.wait_recv()
    y_relay.wait_recv()
    d_core = copy(7, diagonal, diagonal, me + core)
    d_core.start()
    here.wait()
    to_core.wait_recv()
    x_core.wait_recv()
    y_core.wait_recv()
    d_core.wait_recv()
    for sent in (to_x, to_y, to_core, x_relay, x_core, y_relay, y_core, d_core):
        sent.wait_send()


def plane_gather(own, number):
    if lax.axis_size("expert") != 8:
        return lax.all_gather(own, "expert", axis=0, tiled=True)
    rows, columns = own.shape
    out = pl.pallas_call(
        gather_kernel,
        out_shape=jax.ShapeDtypeStruct((8, rows, columns), own.dtype),
        in_specs=[pl.BlockSpec(memory_space=pl.ANY)],
        out_specs=pl.BlockSpec(memory_space=pl.ANY),
        scratch_shapes=[
            pltpu.SemaphoreType.DMA((8,)),
            pltpu.SemaphoreType.DMA((8,)),
            pltpu.SemaphoreType.DMA,
        ],
        compiler_params=pltpu.CompilerParams(collective_id=number, has_side_effects=True),
        cost_estimate=pl.CostEstimate(
            flops=0, bytes_accessed=rows * columns * 96, transcendentals=0
        ),
    )(own)
    return out.reshape(8 * rows, columns)


def scatter_kernel(
    parts_ref, out_ref, mine, theirs, x_in, y_in, dx_in, dy_in, send_sem, recv_sem, copy_sem
):
    me = lax.axis_index("expert")
    core, column, line = neighbours(me)
    rows = out_ref.shape[0]
    half = rows // 2
    top, bottom = pl.ds(0, half), pl.ds(half, half)
    greet((me + core, me + column, me + line))

    def copy(at, src, dst, peer):
        return pltpu.make_async_remote_copy(
            src_ref=src,
            dst_ref=dst,
            send_sem=send_sem.at[at],
            recv_sem=recv_sem.at[at],
            device_id={"expert": peer},
            device_id_type=MESH,
        )

    chips = (me + column + line, me + column, me + line, me)
    swaps = [copy(k, parts_ref.at[chips[k] + core], theirs.at[k], me + core) for k in range(4)]
    loads = [
        pltpu.make_async_copy(parts_ref.at[chips[k]], mine.at[k], copy_sem.at[k]) for k in range(4)
    ]
    for k in range(4):
        swaps[k].start()
        loads[k].start()

    def each(first, count, step):
        def body(i, carry):
            step(pl.ds(pl.multiple_of(first + i * 16, 16), 16))
            return carry

        lax.fori_loop(0, count // 16, body, 0)

    def pair_sum(k):
        loads[k].wait()
        swaps[k].wait_recv()

        def step(block):
            total = mine[k, block].astype(f32) + theirs[k, block].astype(f32)
            if k == 3:
                out_ref[block, :] = total
            else:
                mine[k, block] = total.astype(b16)

        each(0, rows, step)

    pair_sum(0)
    d_x = copy(4, mine.at[0, top], dx_in, me + column)
    d_y = copy(5, mine.at[0, bottom], dy_in, me + line)
    d_x.start()
    d_y.start()
    pair_sum(1)
    x_top = copy(6, mine.at[1, top], x_in.at[top], me + column)
    x_top.start()
    pair_sum(2)
    y_bottom = copy(7, mine.at[2, bottom], y_in.at[bottom], me + line)
    y_bottom.start()
    pair_sum(3)

    d_x.wait_recv()

    def add_y(block):
        mine[2, block] = (mine[2, block].astype(f32) + dx_in[block, :].astype(f32)).astype(b16)

    each(0, half, add_y)
    y_top = copy(8, mine.at[2, top], y_in.at[top], me + line)
    y_top.start()
    d_y.wait_recv()

    def add_x(block):
        low = pl.ds(pl.multiple_of(block.start - half, 16), 16)
        mine[1, block] = (mine[1, block].astype(f32) + dy_in[low, :].astype(f32)).astype(b16)

    each(half, half, add_x)
    x_bottom = copy(9, mine.at[1, bottom], x_in.at[bottom], me + column)
    x_bottom.start()
    x_top.wait_recv()
    y_bottom.wait_recv()
    y_top.wait_recv()
    x_bottom.wait_recv()

    def finish(block):
        out_ref[block, :] = (
            out_ref[block, :] + x_in[block, :].astype(f32) + y_in[block, :].astype(f32)
        )

    each(0, rows, finish)
    for sent in swaps + [d_x, d_y, x_top, y_bottom, y_top, x_bottom]:
        sent.wait_send()


def plane_scatter(parts, number):
    if lax.axis_size("expert") != 8:
        return lax.psum_scatter(parts, "expert", scatter_dimension=0, tiled=True).astype(f32)
    rows, columns = parts.shape[0] // 8, parts.shape[1]
    return pl.pallas_call(
        scatter_kernel,
        out_shape=jax.ShapeDtypeStruct((rows, columns), f32),
        in_specs=[pl.BlockSpec(memory_space=pl.ANY)],
        out_specs=pl.BlockSpec(memory_space=pltpu.VMEM),
        scratch_shapes=[
            pltpu.VMEM((4, rows, columns), b16),
            pltpu.VMEM((4, rows, columns), b16),
            pltpu.VMEM((rows, columns), b16),
            pltpu.VMEM((rows, columns), b16),
            pltpu.VMEM((rows // 2, columns), b16),
            pltpu.VMEM((rows // 2, columns), b16),
            pltpu.SemaphoreType.DMA((10,)),
            pltpu.SemaphoreType.DMA((10,)),
            pltpu.SemaphoreType.DMA((4,)),
        ],
        compiler_params=pltpu.CompilerParams(
            collective_id=number, has_side_effects=True, vmem_limit_bytes=32 << 20
        ),
        cost_estimate=pl.CostEstimate(
            flops=0, bytes_accessed=rows * columns * 128, transcendentals=0
        ),
    )(parts.reshape(8, rows, columns))


def rms_scale(value, gain):
    return value * lax.rsqrt(jnp.mean(value * value, axis=-1, keepdims=True) + epsilon) * gain


def rms_back(value, gain, grad):
    scale = lax.rsqrt(jnp.mean(value * value, axis=-1, keepdims=True) + epsilon)
    unit = value * scale
    inward = grad * gain
    back = scale * (inward - unit * jnp.mean(inward * unit, axis=-1, keepdims=True))
    return back, jnp.sum(grad * unit, axis=0)


def dot(a, b):
    return jnp.dot(a, b, preferred_element_type=f32)


def dot_nt(a, b):
    return lax.dot_general(a, b, NT, preferred_element_type=f32)


def dot_tn(a, b):
    return lax.dot_general(a, b, (((0,), (0,)), ((), ())), preferred_element_type=f32)


def silu_parts(value):
    sigma = jax.nn.sigmoid(value)
    return value * sigma, sigma * (1.0 + value * (1.0 - sigma))


def dense_gates(logits, route_ids):
    experts = logits.shape[1]
    ids = jnp.arange(experts, dtype=jnp.int32)
    named = jnp.any(route_ids[:, :, None] == ids, axis=1)
    top = jnp.max(jnp.where(named, logits, -jnp.inf), axis=1, keepdims=True)
    weight = jnp.where(named, jnp.exp(jnp.where(named, logits - top, 0.0)), 0.0)
    return weight / jnp.sum(weight, axis=1, keepdims=True)


def exchange(value, axis, distance):
    size = lax.axis_size(axis)
    return lax.ppermute(value, axis, [(i, i ^ distance) for i in range(size)])


def total_of(value, axes):
    for axis in axes:
        distance = 1
        while distance < lax.axis_size(axis):
            value = value + exchange(value, axis, distance)
            distance *= 2
    return value


class Heads:
    def __init__(self, planes, plane, out_rows, width):
        self.planes, self.plane, self.width = planes, plane, width
        self.each = H // plane
        self.padded = -(-self.each // 2) * 2
        own = 2 * out_rows
        self.owned = own % width == 0 and planes % 2 == 0 and self.padded == self.each
        self.run = own // width if self.owned else self.each

    def group(self, value, size):
        lead = value.shape[:-1]
        if self.owned:
            value = value.reshape(lead + (2, self.planes // 2, self.plane // 2, self.run * size))
            n = len(lead)
            value = jnp.transpose(value, tuple(range(n)) + (n + 2, n, n + 1, n + 3))
        value = value.reshape(lead + (self.plane, self.each * size))
        pad = (self.padded - self.each) * size
        return jnp.pad(value, [(0, 0)] * (len(lead) + 1) + [(0, pad)]) if pad else value

    def ungroup(self, value, size):
        lead = value.shape[:-2]
        value = value[..., : self.each * size]
        if self.owned:
            value = value.reshape(lead + (self.plane // 2, 2, self.planes // 2, self.run * size))
            n = len(lead)
            value = jnp.transpose(value, tuple(range(n)) + (n + 1, n + 2, n, n + 3))
        return value.reshape(lead + (H * size,))


def body(
    block_input,
    out_grad,
    routes,
    norm_in,
    in_proj,
    conv_weight,
    conv_bias,
    step_bias,
    log_rate,
    skip_gain,
    mixer_gain,
    out_proj,
    norm_mid,
    router,
    shared_gate,
    shared_up,
    shared_down,
    expert_gate,
    expert_up,
    expert_down,
):
    both = ("dp", "expert")
    planes, plane = lax.axis_size("dp"), lax.axis_size("expert")
    at = lax.axis_index("expert")
    core = at % 2
    micro, length, width = block_input.shape
    picks = routes.shape[-1]
    local = expert_gate.shape[0]
    experts = local * plane
    capacity = 3 * length * picks // (2 * experts)
    slots = -(-capacity // 8) * 8
    tokens = micro * length
    shard = in_proj.shape[0]
    out_rows = out_proj.shape[0]
    inner = out_rows * planes * plane
    hr = shared_down.shape[0]
    fs = hr * planes
    ehidden = expert_gate.shape[2]
    gather = lambda v, axes: lax.all_gather(v, axes, axis=0, tiled=True)
    scatter = lambda v, axes: lax.psum_scatter(v, axes, scatter_dimension=0, tiled=True)
    heads = Heads(planes, plane, out_rows, inner // H)
    size = heads.width
    wide = heads.padded * size
    states = conv_weight.shape[1] - inner
    main = 2 * wide + states + LANES

    signal = in_proj[:, inner : 2 * inner]
    maps = in_proj[:, 2 * inner : 2 * inner + states]
    steps = in_proj[:, 2 * inner + states :]
    common = jnp.concatenate([norm_in[:, None], norm_mid[:, None], router], axis=1)
    spare = LANES - heads.padded - common.shape[1]
    repeat = lambda v: jnp.broadcast_to(v[:, None, :], (shard, plane, v.shape[1]))
    split = lambda v: v.reshape(shard, planes, plane, hr).transpose(0, 2, 1, 3).reshape(shard, plane, fs)
    sent = jnp.concatenate(
        [
            heads.group(in_proj[:, :inner], size),
            heads.group(signal, size),
            repeat(maps),
            heads.group(steps, 1),
            repeat(common),
            jnp.zeros((shard, plane, spare), b16),
            split(shared_gate),
            split(shared_up),
        ],
        axis=2,
    ).transpose(1, 0, 2)
    came = lax.all_to_all(sent, "expert", split_axis=0, concat_axis=0, tiled=True)
    proj = gather(came.reshape(plane * shard, -1), "dp")
    in_w = proj[:, :main]
    gate_up = proj[:, main:]
    first = 2 * wide + states + heads.padded
    gain_in = proj[:, first].astype(f32)
    gain_mid = proj[:, first + 1].astype(f32)
    route_proj = proj[:, first + 2 : first + 2 + experts]

    own_routes = jnp.pad(routes.reshape(tokens, picks).astype(b16), ((0, 0), (0, LANES - picks)))
    flat_in = block_input.reshape(tokens, width)
    grad_low = out_grad.reshape(tokens, width)
    seen = plane_gather(jnp.concatenate([flat_in, own_routes], axis=1), 0)
    all_grad = plane_gather(grad_low, 1)
    all_in = seen[:, :width].astype(f32)
    all_routes = seen[:, width : width + picks].astype(jnp.int32)
    count = all_in.shape[0]
    seqs = count // LEN

    out_shard = jnp.concatenate(
        [
            jnp.concatenate([out_proj, mixer_gain[:, None]], axis=1),
            jnp.pad(shared_down, ((0, 0), (0, 1))),
        ],
        axis=0,
    )
    out_shard = jnp.pad(out_shard, ((0, 0), (0, LANES - 1)))
    half = planes // 2
    if heads.owned:
        out_all = gather(out_shard, "dp").reshape(planes, out_rows + hr, -1)
        down_w = out_all[:, out_rows:, :width].reshape(fs, width)
        pieces = out_all[:, :out_rows].reshape(2, half, out_rows, -1)
        low = core == 0
        keep = jnp.where(low, pieces[0], pieces[1])
        other = exchange(jnp.where(low, pieces[1], pieces[0]), "expert", 1)
        out_w = jnp.stack([jnp.where(low, keep, other), jnp.where(low, other, keep)], axis=1)
        out_w = out_w.reshape(wide, -1)
    else:
        down_w = gather(shared_down, "dp")
        out_all = gather(out_shard[:out_rows], both)
        out_w = lax.dynamic_slice_in_dim(out_all, at * heads.each * size, heads.each * size, 0)
        out_w = jnp.pad(out_w, ((0, wide - heads.each * size), (0, 0)))
    gain_mix = out_w[:, width]
    out_w = out_w[:, :width]

    pick_own = lambda v: lax.dynamic_index_in_dim(v, at, v.ndim - 2, keepdims=False)
    lane_pad = lambda v: jnp.pad(v.astype(f32), (0, LANES - v.shape[0])).reshape(1, LANES)
    own_lanes = lambda v: jnp.concatenate(
        [pick_own(heads.group(v[:, :inner], size)), v[:, inner:]], axis=1
    ).astype(f32)
    params = (
        own_lanes(conv_weight),
        own_lanes(conv_bias[None]),
        lane_pad(pick_own(heads.group(step_bias, 1))),
        lane_pad(pick_own(heads.group(log_rate, 1))),
        pick_own(heads.group(jnp.repeat(skip_gain, size), size)).astype(f32).reshape(1, -1),
        gain_mix.astype(f32).reshape(1, -1),
    )

    normed = rms_scale(all_in, gain_in).astype(b16)
    merged = dot(normed, in_w)
    mixed, joined, square = mix_forward(merged, params)
    square = jnp.sum(square, axis=1, keepdims=True)
    square_high = square.astype(b16)
    square_low = (square - square_high.astype(f32)).astype(b16)
    lane = jnp.arange(LANES)[None]
    tail = jnp.where(lane == 2 * at, square_high, jnp.where(lane == 2 * at + 1, square_low, 0))
    summed = plane_scatter(
        jnp.concatenate([dot(mixed, out_w).astype(b16), tail.astype(b16)], axis=1), 2
    )
    scale = lax.rsqrt(jnp.sum(summed[:, width:], axis=1, keepdims=True) / inner + epsilon)
    mixer_out = scale * summed[:, :width]
    start = flat_in.astype(f32)
    grad_out = grad_low.astype(f32)
    middle = start + mixer_out
    routed = rms_scale(middle, gain_mid).astype(b16)
    all_routed = plane_gather(routed, 3)

    mine = at * local + jnp.arange(local, dtype=jnp.int32)
    marks = jnp.any(all_routes[:, :, None] == mine, axis=1).reshape(seqs, LEN, local)
    earlier = jnp.arange(LEN)[:, None] > jnp.arange(LEN)[None, :]
    rank = jnp.einsum(
        "ts,nse->net", earlier.astype(b16), marks.astype(b16), preferred_element_type=f32
    ).astype(jnp.int32)
    places = jnp.arange(slots, dtype=jnp.int32)
    chosen = (rank[:, :, None, :] == places[None, None, :, None]) & (
        marks.transpose(0, 2, 1)[:, :, None, :]
    )
    select = chosen.astype(b16).reshape(seqs, local * slots, LEN)
    gates_all = dense_gates(dot(all_routed, route_proj), all_routes)
    gates_mine = lax.dynamic_slice_in_dim(gates_all, at * local, local, axis=1)
    gates_mine = gates_mine.reshape(seqs, LEN, local).transpose(0, 2, 1)
    slot_gates = jnp.sum(jnp.where(chosen, gates_mine[:, :, None, :], 0.0), axis=-1)

    def spread(rows):
        return jnp.einsum(
            "nrt,ntd->nrd", select, rows.reshape(seqs, LEN, -1), preferred_element_type=f32
        ).reshape(seqs, local, slots, -1)

    rows_in = spread(all_routed).astype(b16)
    rows_grad = spread(all_grad)
    outs, backs, dgates, bank_grads = [], [], [], []
    for e in range(local):
        gu_w = gather(jnp.concatenate([expert_gate[e], expert_up[e]], axis=1), "dp")
        e_down = gather(expert_down[e], "dp")
        x = rows_in[:, e].reshape(seqs * slots, -1)
        g = slot_gates[:, e].reshape(seqs * slots, 1)
        dy = rows_grad[:, e].reshape(seqs * slots, -1)
        pre = dot(x, gu_w)
        soft, slope = silu_parts(pre[:, :ehidden])
        lin = pre[:, ehidden:]
        hid = (soft * lin).astype(b16)
        made = dot(hid, e_down).astype(b16).astype(f32)
        dgates.append(jnp.sum(made * dy, axis=1).reshape(seqs, slots))
        outs.append((made * g).astype(b16).reshape(seqs, slots, -1))
        dmade = (dy * g).astype(b16)
        dhid = dot_nt(dmade, e_down)
        dpre = jnp.concatenate([dhid * lin * slope, dhid * soft], axis=1).astype(b16)
        backs.append(dot_nt(dpre, gu_w).astype(b16).reshape(seqs, slots, -1))
        bank_grads.append(
            (
                scatter(dot_tn(x, dpre).astype(b16), "dp").astype(f32),
                scatter(dot_tn(hid, dmade).astype(b16), "dp").astype(f32),
            )
        )
    combine = lambda parts: jnp.einsum(
        "nrt,nrd->ntd", select, jnp.concatenate(parts, axis=1), preferred_element_type=f32
    ).reshape(count, -1)
    dgate_rows = jnp.sum(
        jnp.where(chosen, jnp.stack(dgates, axis=1)[:, :, :, None], 0.0), axis=2
    ).transpose(0, 2, 1)
    dgate_wide = lax.dynamic_update_slice_in_dim(
        jnp.zeros((count, experts), f32), dgate_rows.reshape(count, local), at * local, axis=1
    )
    high = dgate_wide.astype(b16)
    fine = (dgate_wide - high.astype(f32)).astype(b16)
    fill = jnp.zeros((count, -(2 * experts) % LANES), b16)

    pre = dot(all_routed, gate_up)
    soft, slope = silu_parts(pre[:, :fs])
    lin = pre[:, fs:]
    hid = (soft * lin).astype(b16)
    dhid = dot_nt(all_grad, down_w)
    dpre = jnp.concatenate([dhid * lin * slope, dhid * soft], axis=1).astype(b16)
    shared_out = dot(hid, down_w)
    shared_back = dot_nt(dpre, gate_up)

    payload = [(combine(backs) + shared_back).astype(b16), high, fine, fill]
    back = plane_scatter(jnp.concatenate(payload, axis=1), 4)
    out_sum = plane_scatter((combine(outs) + shared_out).astype(b16), 5)

    gates = dense_gates(dot(routed, route_proj), routes.reshape(tokens, picks))
    dgate = back[:, width : width + experts] + back[:, width + experts : width + 2 * experts]
    dlogits = (gates * (dgate - jnp.sum(gates * dgate, axis=1, keepdims=True))).astype(b16)
    droute = back[:, :width] + dot_nt(dlogits, route_proj)
    dmid_part, mid_gain_grad = rms_back(middle, gain_mid, droute)
    dmid = grad_out + dmid_part

    scaled = (dmid * scale).astype(b16)
    inward = scale * jnp.sum(scaled.astype(f32) * mixer_out, axis=1, keepdims=True) / inner
    inward_high = inward.astype(b16)
    inward_low = (inward - inward_high.astype(f32)).astype(b16)
    tail = jnp.where(lane == 0, inward_high, jnp.where(lane == 1, inward_low, 0)).astype(b16)
    spread_mid = plane_gather(jnp.concatenate([scaled, tail], axis=1), 6)
    all_mid = spread_mid[:, :width]
    all_inward = spread_mid[:, width : width + 1].astype(f32) + spread_mid[
        :, width + 1 : width + 2
    ].astype(f32)
    dmerged, weight_grad, bias_grad, skip_grad, head_grad = mix_backward(
        merged, joined, dot_nt(all_mid, out_w), all_inward, params
    )
    dnormed = plane_scatter(dot_nt(dmerged, in_w).astype(b16), 7)
    dstart, unused = rms_back(start, gain_in, dnormed)

    def owners(grad):
        grad = scatter(grad.astype(b16), "dp")
        grad = grad.reshape(plane, shard, -1)
        return lax.all_to_all(grad, "expert", split_axis=0, concat_axis=0, tiled=True).astype(f32)

    shared_grad = owners(dot_tn(all_routed, dpre))
    unsplit = lambda v: (
        v.reshape(plane, shard, planes, hr).transpose(1, 2, 0, 3).reshape(shard, planes * plane * hr)
    )
    out_w_grad = dot_tn(mixed, all_mid).astype(b16)
    down_grad = dot_tn(hid, all_grad).astype(b16)
    if heads.owned:
        parts = out_w_grad.reshape(half, 2, out_rows, width)
        keep = jnp.where(low, parts[:, 0], parts[:, 1])
        other = exchange(jnp.where(low, parts[:, 1], parts[:, 0]), "expert", 1)
        out_parts = jnp.concatenate([jnp.where(low, keep, other), jnp.where(low, other, keep)])
        rows = jnp.concatenate([out_parts, down_grad.reshape(planes, hr, width)], axis=1)
        rows = scatter(rows.reshape(planes * (out_rows + hr), width), "dp").astype(f32)
        out_w_grad, down_grad = rows[:out_rows], rows[out_rows:]
    else:
        rows = lax.dynamic_update_slice_in_dim(
            jnp.zeros((inner, width), b16), out_w_grad[: heads.each * size], at * heads.each * size, 0
        )
        out_w_grad = scatter(rows, both).astype(f32)
        down_grad = scatter(down_grad, "dp").astype(f32)

    extra = jnp.concatenate(
        [
            jnp.zeros((width, heads.padded + 1), f32),
            mid_gain_grad[:, None],
            dot_tn(routed, dlogits),
            jnp.zeros((width, spare), f32),
        ],
        axis=1,
    )
    in_w_grad = dot_tn(normed, dmerged)
    in_w_grad = jnp.concatenate([in_w_grad[:, :-LANES], in_w_grad[:, -LANES:] + extra], axis=1)
    in_w_grad = owners(in_w_grad)
    by_row = in_w_grad.transpose(1, 0, 2)
    step_part = 2 * wide + states
    in_grad = jnp.concatenate(
        [
            heads.ungroup(by_row[:, :, :wide], size),
            heads.ungroup(by_row[:, :, wide : 2 * wide], size),
            jnp.sum(by_row[:, :, 2 * wide : step_part], axis=1),
            heads.ungroup(by_row[:, :, step_part : step_part + heads.padded], 1),
        ],
        axis=1,
    )
    shared_common = jnp.sum(by_row[:, :, first:], axis=1)
    gain_in_grad = jnp.sum(in_proj.astype(f32) * in_grad, axis=1) / norm_in.astype(f32)
    gain_mix_grad = jnp.sum(out_proj.astype(f32) * out_w_grad, axis=1) / mixer_gain.astype(f32)

    place = lambda v, size: heads.ungroup(
        lax.dynamic_update_slice_in_dim(
            jnp.zeros(v.shape[:-1] + (plane, v.shape[-1]), f32), v[..., None, :], at, v.ndim - 1
        ),
        size,
    )
    taps = jnp.concatenate([weight_grad, bias_grad], axis=0)
    taps = jnp.concatenate([place(taps[:, :wide], size), taps[:, wide:]], axis=1)
    skip_grad = jnp.sum(skip_grad.reshape(heads.padded, size), axis=1)
    head_rows = jnp.concatenate([head_grad[:2, : heads.padded], skip_grad[None]], axis=0)
    head_rows = place(head_rows, 1).reshape(1, -1)
    head_rows = jnp.pad(head_rows, ((0, 0), (0, taps.shape[1] - head_rows.shape[1])))
    small = total_of(jnp.concatenate([taps, head_rows], axis=0), ("dp", "expert"))

    shape = block_input.shape
    return (
        (middle + out_sum).astype(b16).reshape(shape),
        (dmid + dstart).reshape(shape),
        gain_in_grad,
        in_grad,
        small[:4],
        small[4],
        small[5, :H],
        small[5, H : 2 * H],
        small[5, 2 * H : 3 * H],
        gain_mix_grad,
        out_w_grad,
        shared_common[:, 1],
        shared_common[:, 2 : 2 + experts],
        unsplit(shared_grad[:, :, :fs].transpose(0, 1, 2)),
        unsplit(shared_grad[:, :, fs:]),
        down_grad,
        jnp.stack([a[:, :ehidden] for a, _ in bank_grads]),
        jnp.stack([a[:, ehidden:] for a, _ in bank_grads]),
        jnp.stack([b for _, b in bank_grads]),
    )


def solution(mesh):
    both = ("dp", "expert")
    rows, matrix, bank = P(both), P(both, None), P("expert", "dp", None)
    token = P(None, both, None)
    in_specs = (token, token, token, rows, matrix, P(), P(), P(), P(), P(), rows, matrix, rows)
    in_specs = in_specs + (matrix, matrix, matrix, matrix, bank, bank, bank)
    out_specs = (token, token, rows, matrix, P(), P(), P(), P(), P(), rows, matrix, rows)
    out_specs = out_specs + (matrix, matrix, matrix, matrix, bank, bank, bank)
    return jax.shard_map(body, mesh=mesh, in_specs=in_specs, out_specs=out_specs, check_vma=False)
```

time: 2920 us -> 1140 us (0.39)
  waiting for transfers between devices: 1660 us -> 348 us
  Pallas kernels: 0 us -> 296 us
  local copies, waits for them, and re-layouts: 364 us -> 117 us
  matrix products: 422 us -> 223 us
  blocking collectives: 212 us -> 20.8 us
  other arithmetic: 191 us -> 93.9 us
    reduce_scatter x5 -> x11, waiting for transfers between devices: 939 us -> 139 us  [body(): lax.psum_scatter(v, axes, scatter_dimension=0, tiled=True)]
    unnamed x23 -> x21, waiting for transfers between devices: 333 us -> 2.2 us
    pallas_call x0 -> x10, Pallas kernels: none -> 296 us  [the longest x4 134 us: plane_gather(): pl.pallas_call(gather_kernel, out_shape=jax.ShapeDtypeStruct((8, rows, co...]
    dot_general x70 -> x45, matrix products: 421 us -> 223 us  [the longest x14 77.3 us: dot(): return jnp.dot(a, b, preferred_element_type=f32)]
    all_to_all x6 -> x2, waiting for transfers between devices: 183 us -> 5.57 us  [owners(): lax.all_to_all(grad, 'expert', split_axis=0, concat_axis=0, tiled=True)]
    reshape x44 -> x36, local copies, waits for them, and re-layouts: 114 us -> 21.8 us  [the longest x1 12.7 us: body(): combine = lambda parts: jnp.einsum('nrt,nrd->ntd', select, jnp.concatenat...]
    all_to_all x2 -> x1, blocking collectives: 101 us -> 20.8 us  [body(): lax.all_to_all(sent, 'expert', split_axis=0, concat_axis=0, tiled=True)]
    all_gather x1 -> x0, blocking collectives: 68.2 us -> none  [body(): lax.all_gather(router, ('dp', 'expert'), axis=0, tiled=True)]
  transfers between devices with their start and end apart: 24 -> 30, of which waited for: 17 -> 12; matrix products, arithmetic and copies ran while one was open for 29% -> 35% of each run, Pallas kernels for 0% -> 26%
where the time goes in v1:
time: 1140 us; the launch traced here: 1130 us
  waiting for transfers between devices  348 us (31%)
  Pallas kernels  296 us (26%)
  matrix products  223 us (20%)
  local copies, waits for them, and re-layouts  117 us (10%)
  other arithmetic  93.9 us (8%)
  blocking collectives  20.8 us (2%)
  between operations  17 us (1%)
  starting transfers between devices  13.7 us (1%)
    all_gather x10, waiting for transfers between devices, body(): gather = lambda v, axes: lax.all_gather(v, axes, axis=0, tiled=True)  199 us
    reduce_scatter x11, waiting for transfers between devices, body(): lax.psum_scatter(v, axes, scatter_dimension=0, tiled=True)  139 us
    pallas_call x4, Pallas kernels, plane_gather(): pl.pallas_call(gather_kernel, out_shape=jax.ShapeDtypeStruct((8, rows, co...  134 us
    pallas_call x4, Pallas kernels, plane_scatter(): pl.pallas_call(scatter_kernel, out_shape=jax.ShapeDtypeStruct((rows, colu...  130 us
    dot_general x14, matrix products, dot(): return jnp.dot(a, b, preferred_element_type=f32)  77.3 us
    dot_general x13, matrix products, dot_tn(): lax.dot_general(a, b, (((0,), (0,)), ((), ())), preferred_element_type=f32)  61.4 us
    dot_general x13, matrix products, dot_nt(): return lax.dot_general(a, b, NT, preferred_element_type=f32)  56.4 us
    unnamed x257, local copies, waits for them, and re-layouts  37.4 us
  transfers between devices with their start and end apart: 30, of which 12 were waited for; matrix products, arithmetic and copies ran while one was open for 35% of the time, Pallas kernels for 26%

profile of v1, /device:TPU:0, one launch (start us, length us, event | category | flops | bytes accessed | tf_op | source)
XLA Modules:
  0.0 1129.0 jit_solution(8380084428225063689)
XLA Ops:
  15.1 20.8 %all_to_all.15 = bf16[8,48,1408]{2,1,0:T(8,128)(2,1)} all-to-all(bf16[8,48,1408]{2,1,0:T(8,128)(2,1)S(1)} %copy.365), channel_id=1, replica_groups=mesh['dp'=4,'expert'=8] {'expert'}, dimensions={0} | all-to-all | bytes 2162688 | tf_op jit(solution)/shard_map/all_to_all | solution.py:650
  47.5 34.2 %shard_map.339 = bf16[8,256,1664]{2,1,0:T(8,128)(2,1)} custom-call(bf16[256,1664]{1,0:T(8,128)(2,1)} %fusion.74.own_ref), custom_call_target="tpu_custom_call" | custom-call | bytes 40894464 | tf_op jit(solution)/shard_map/pallas_call | solution.py:361
  85.7 32.9 %shard_map.344 = bf16[8,256,1536]{2,1,0:T(8,128)(2,1)} custom-call(bf16[256,1536]{1,0:T(8,128)(2,1)} %bitcast.379), custom_call_target="tpu_custom_call" | custom-call | bytes 37748736 | tf_op jit(solution)/shard_map/pallas_call | solution.py:361
  118.9 10.5 fusion.127
  129.5 11.6 %fusion.117 = (f32[16,1,40,1536]{3,2,1,0:T(8,128)}, f32[16,1,40,1536]{3,2,1,0:T(8,128)}, f32[16,1,40,1536]{3,2,1,0:T(8,128)}, f32[16,1,40,1536]{3,2,1,0:T(8,128)}) fusion(f32[16,4,40,1536]{3,2,1,0:T(8,128)} %bitcast.357), kind=kLoop, calls=%fused_computation.311 | loop fusion | bytes 31457280 | tf_op jit(solution)/shard_map/slice | solution.py:757
  152.4 11.8 %fusion.37.merged_ref = f32[2048,1152]{1,0:T(8,128)S(1)} fusion(bf16[1536,1408]{1,0:T(8,128)(2,1)} %all-gather.15.cloned.1.call-done, f32[1536]{0:T(1024)S(1)} %get-tuple-element.112, f32[2048]{0:T(1024)S(1)} %add_rsqrt_fusion, bf16[2048,1664]{1,0:T(8,128)(2,1)} %bitcast.372), kind=kOutput, calls=%fused_computation.74 | convolution fusion | flops 7260340224 | bytes 19281920 | tf_op jit(solution)/shard_map/dot_general | solution.py:515
  164.2 10.7 shard_map.340
  177.0 6.9 convolution_convert_fusion.1
  184.0 6.8 pad_maximum_fusion
  190.8 9.8 copy.373
  203.5 33.5 %shard_map.341 = f32[256,1664]{1,0:T(8,128)S(1)} custom-call(bf16[8,256,1664]{2,1,0:T(8,128)(2,1)S(1)} %bitcast.353), custom_call_target="tpu_custom_call" | custom-call | bytes 54525952 | tf_op jit(solution)/shard_map/pallas_call | solution.py:477
  239.3 32.3 %shard_map.342 = bf16[8,256,1536]{2,1,0:T(8,128)(2,1)} custom-call(bf16[256,1536]{1,0:T(8,128)(2,1)} %multiply_convert_fusion.1.own_ref), custom_call_target="tpu_custom_call" | custom-call | bytes 37748736 | tf_op jit(solution)/shard_map/pallas_call | solution.py:361
  271.7 5.4 convolution_convert_fusion.2
  295.7 5.4 select_reduce_fusion.2
  301.1 26.5 %all-gather.23.cloned.1.call-done = bf16[1536,1024]{1,0:T(8,128)(2,1)} async-done(((bf16[384,1024]{1,0:T(8,128)(2,1)}), bf16[1536,1024]{1,0:T(8,128)(2,1)}) %all-gather.23.cloned.1.call-update) | async-done | bytes 3145744 | tf_op jit(solution)/shard_map/all_gather | solution.py:622
  327.5 6.2 fusion.125
  333.7 57.4 %all-gather.21.cloned.1.call-done = bf16[1536,1024]{1,0:T(8,128)(2,1)} async-done(((bf16[384,1024]{1,0:T(8,128)(2,1)}), bf16[1536,1024]{1,0:T(8,128)(2,1)}) %all-gather.21.cloned.1.call-update) | async-done | bytes 3145744 | tf_op jit(solution)/shard_map/all_gather | solution.py:622
  410.5 18.0 %all-gather.27.cloned.1.call-done = bf16[1,512,1536]{2,1,0:T(8,128)(2,1)} async-done(((bf16[1,128,1536]{2,1,0:T(8,128)(2,1)}), bf16[1,512,1536]{2,1,0:T(8,128)(2,1)}) %all-gather.27.cloned.1.call-update) | async-done | bytes 1572880 | tf_op jit(solution)/shard_map/all_gather | solution.py:622
  433.8 32.3 %all-gather.31.cloned.1.call-done = bf16[1,512,1536]{2,1,0:T(8,128)(2,1)} async-done(((bf16[1,128,1536]{2,1,0:T(8,128)(2,1)}), bf16[1,512,1536]{2,1,0:T(8,128)(2,1)}) %all-gather.31.cloned.1.call-update) | async-done | bytes 1572880 | tf_op jit(solution)/shard_map/all_gather | solution.py:622
  466.1 5.3 fusion.29
  471.3 32.3 %all-gather.29.cloned.1.call-done = bf16[1,512,1536]{2,1,0:T(8,128)(2,1)} async-done(((bf16[1,128,1536]{2,1,0:T(8,128)(2,1)}), bf16[1,512,1536]{2,1,0:T(8,128)(2,1)}) %all-gather.29.cloned.1.call-update) | async-done | bytes 1572880 | tf_op jit(solution)/shard_map/all_gather | solution.py:622
  508.9 32.2 %all-gather.33.cloned.1.call-done = bf16[1,512,1536]{2,1,0:T(8,128)(2,1)} async-done(((bf16[1,128,1536]{2,1,0:T(8,128)(2,1)}), bf16[1,512,1536]{2,1,0:T(8,128)(2,1)}) %all-gather.33.cloned.1.call-update) | async-done | bytes 1572880 | tf_op jit(solution)/shard_map/all_gather | solution.py:622
  568.3 5.7 fusion.35
  607.9 6.0 fusion.12
  613.9 12.7 %copy.389 = f32[2048,1536]{0,1:T(8,128)} copy(f32[2048,1536]{1,0:T(8,128)} %bitcast.375) | data formatting | bytes 25165824 | tf_op jit(solution)/shard_map/reshape | solution.py:777
  631.8 7.1 add_convert_fusion
  638.8 9.6 maximum_maximum_fusion
  648.4 9.8 copy.390
  661.2 33.8 %shard_map.345 = f32[256,1664]{1,0:T(8,128)S(1)} custom-call(bf16[8,256,1664]{2,1,0:T(8,128)(2,1)S(1)} %bitcast.354), custom_call_target="tpu_custom_call" | custom-call | bytes 54525952 | tf_op jit(solution)/shard_map/pallas_call | solution.py:477
  705.0 34.3 %shard_map.346 = bf16[8,256,1664]{2,1,0:T(8,128)(2,1)} custom-call(bf16[256,1664]{1,0:T(8,128)(2,1)} %pad_maximum_fusion.12.own_ref), custom_call_target="tpu_custom_call" | custom-call | bytes 40894464 | tf_op jit(solution)/shard_map/pallas_call | solution.py:361
  739.3 5.4 fusion.39
  751.1 5.9 convolution_convert_fusion.5
  758.1 6.0 convolution_convert_fusion.4
  765.2 6.0 convolution_convert_fusion.3
  773.2 6.0 fusion.22.grad_ref
  783.0 21.6 %shard_map.347 = (bf16[2048,1152]{1,0:T(8,128)(2,1)S(1)}, f32[4,640]{1,0:T(4,128)S(1)}, f32[1,640]{1,0:T(1,128)S(1)}, f32[1,384]{1,0:T(1,128)S(1)}, f32[8,128]{1,0:T(8,128)S(1)}) custom-call(f32[2048,1152]{1,0:T(8,128)S(1)} %copy-done.17, f32[2048,384]{1,0:T(8,128)S(1)} %copy-done.19, f32[2048,384]{1,0:T(8,128)S(1)} %fusion.22.grad_ref, ...), custom_call_target="tpu_custom_call" | custom-call | flops 14155776000 | bytes 28311552 | tf_op jit(solution)/shard_map/pallas_call | solution.py:265
  804.7 12.8 %fusion.68 = f32[1536,1152]{0,1:T(8,128)S(1)} fusion(bf16[2048,1152]{1,0:T(8,128)(2,1)S(1)} %get-tuple-element.30, f32[1536]{0:T(1024)S(1)} %copy-done.80, f32[2048]{0:T(1024)S(1)} %copy-done.93, bf16[2048,1664]{1,0:T(8,128)(2,1)} %bitcast.373), kind=kOutput, calls=%fused_computation.157 | convolution fusion | flops 7260340224 | bytes 18102272 | tf_op jit(solution)/shard_map/dot_general | solution.py:523
  821.1 5.8 copy.417
  830.8 6.1 convolution_convert_fusion.6
  837.0 11.7 %convolution_convert_fusion = bf16[2048,1536]{1,0:T(8,128)(2,1)S(1)} fusion(bf16[2048,1152]{1,0:T(8,128)(2,1)} %copy-done.20, bf16[1536,1408]{1,0:T(8,128)(2,1)} %all-gather.15.cloned.1.call-done), kind=kOutput, calls=%fused_computation.24 | convolution fusion | flops 7250903040 | bytes 14548992 | tf_op jit(solution)/shard_map/dot_general | solution.py:519
  848.7 5.9 fusion.4
  856.3 7.0 fusion.3
  863.3 31.4 %shard_map.348 = f32[256,1536]{1,0:T(8,128)S(1)} custom-call(bf16[8,256,1536]{2,1,0:T(8,128)(2,1)S(1)} %bitcast.356), custom_call_target="tpu_custom_call" | custom-call | bytes 50331648 | tf_op jit(solution)/shard_map/pallas_call | solution.py:477
  897.2 31.2 %shard_map.343 = f32[256,1536]{1,0:T(8,128)S(1)} custom-call(bf16[8,256,1536]{2,1,0:T(8,128)(2,1)S(1)} %bitcast.355), custom_call_target="tpu_custom_call" | custom-call | bytes 50331648 | tf_op jit(solution)/shard_map/pallas_call | solution.py:477
  939.0 5.6 all-to-all-done.2
  959.8 16.3 %reduce-scatter.24.cloned.1.call-done = bf16[384,1024]{1,0:T(8,128)(2,1)} async-done(((bf16[1536,1024]{1,0:T(8,128)(2,1)}), bf16[384,1024]{1,0:T(8,128)(2,1)}) %reduce-scatter.24.cloned.1.call-update) | async-done | bytes 786448 | tf_op jit(solution)/shard_map/reduce_scatter | solution.py:623
  980.4 64.3 %reduce-scatter.34.cloned.1.call-done = bf16[384,1152]{1,0:T(8,128)(2,1)} async-done(((bf16[1536,1152]{1,0:T(8,128)(2,1)}), bf16[384,1152]{1,0:T(8,128)(2,1)}) %reduce-scatter.34.cloned.1.call-update) | async-done | bytes 884752 | tf_op jit(solution)/shard_map/reduce_scatter | solution.py:623
  1049.6 58.0 %reduce-scatter.18.cloned.1.call-done = bf16[384,1024]{1,0:T(8,128)(2,1)} async-done(((bf16[1536,1024]{1,0:T(8,128)(2,1)}), bf16[384,1024]{1,0:T(8,128)(2,1)}) %reduce-scatter.18.cloned.1.call-update) | async-done | bytes 786448 | tf_op jit(solution)/shard_map/reduce_scatter | solution.py:623
  (577 shorter events, 243.5 us)
Async XLA Ops:
  7.2 133.9 %all-gather.17.cloned.1.call-start = ((), (), s32[]{:S(2)}) async-start(), calls=%async_computation.15 | async-start | bytes 2129920 | tf_op jit(solution)/shard_map/all_gather | solution.py:622
  10.0 140.1 %all-gather.15.cloned.1.call-start = ((), (), s32[]{:S(2)}) async-start(), calls=%async_computation.14 | async-start | bytes 5406720 | tf_op jit(solution)/shard_map/all_gather | solution.py:622
  35.9 244.8 %all-gather.25.cloned.1.call-start = ((), (), s32[]{:S(2)}) async-start(), calls=%async_computation.19 | async-start | bytes 3932160 | tf_op jit(solution)/shard_map/all_gather | solution.py:622
  39.0 249.2 %all-gather.19.cloned.1.call-start = ((), (), s32[]{:S(2)}) async-start(), calls=%async_computation.16 | async-start | bytes 3932160 | tf_op jit(solution)/shard_map/all_gather | solution.py:622
  40.0 287.5 %all-gather.23.cloned.1.call-start = ((), (), s32[]{:S(2)}) async-start(), calls=%async_computation.18 | async-start | bytes 3932160 | tf_op jit(solution)/shard_map/all_gather | solution.py:622
  41.1 350.1 %all-gather.21.cloned.1.call-start = ((), (), s32[]{:S(2)}) async-start(), calls=%async_computation.17 | async-start | bytes 3932160 | tf_op jit(solution)/shard_map/all_gather | solution.py:622
  42.2 386.3 %all-gather.27.cloned.1.call-start = ((), (), s32[]{:S(2)}) async-start(), calls=%async_computation.30 | async-start | bytes 1966080 | tf_op jit(solution)/shard_map/all_gather | solution.py:622
  44.0 422.1 %all-gather.31.cloned.1.call-start = ((), (), s32[]{:S(2)}) async-start(), calls=%async_computation.32 | async-start | bytes 1966080 | tf_op jit(solution)/shard_map/all_gather | solution.py:622
  44.7 458.9 %all-gather.29.cloned.1.call-start = ((), (), s32[]{:S(2)}) async-start(), calls=%async_computation.31 | async-start | bytes 1966080 | tf_op jit(solution)/shard_map/all_gather | solution.py:622
  45.5 495.6 %all-gather.33.cloned.1.call-start = ((), (), s32[]{:S(2)}) async-start(), calls=%async_computation.33 | async-start | bytes 1966080 | tf_op jit(solution)/shard_map/all_gather | solution.py:622
  46.1 888.8 %reduce-scatter.16.cloned.1.call-start = ((), (), s32[]{:S(2)}) async-start(), calls=%async_computation.21 | async-start | bytes 983040 | tf_op jit(solution)/shard_map/reduce_scatter | solution.py:623
  46.3 35.4 %copy-start.81 = (bf16[1,3328]{1,0:T(2,128)(2,1)}, bf16[1,3328]{1,0:T(2,128)(2,1)S(1)}, u32[]{:S(2)}) copy-start(bf16[1,3328]{1,0:T(2,128)(2,1)S(1)} %broadcast_in_dim.208) | copy-start | bytes 19972
  46.5 35.2 %copy-start.67 = (s32[2,128,6]{2,1,0:T(8,128)}, s32[2,128,6]{2,1,0:T(8,128)S(1)}, u32[]{:S(2)}) copy-start(s32[2,128,6]{2,1,0:T(8,128)S(1)} %copy.354) | copy-start | bytes 18436
  84.8 79.4 %copy-start.10 = (f32[1,128]{1,0:T(1,128)}, f32[1,128]{1,0:T(1,128)S(1)}, u32[]{:S(2)}) copy-start(f32[1,128]{1,0:T(1,128)S(1)} %bitcast_convert_fusion.1.step_ref) | copy-start | bytes 1540
  84.8 79.4 %copy-start.12 = (f32[1,128]{1,0:T(1,128)}, f32[1,128]{1,0:T(1,128)S(1)}, u32[]{:S(2)}) copy-start(f32[1,128]{1,0:T(1,128)S(1)} %bitcast_convert_fusion.rate_ref) | copy-start | bytes 1540
  85.2 79.0 %copy-start.6 = (f32[1,384]{1,0:T(1,128)}, f32[1,384]{1,0:T(1,128)S(1)}, u32[]{:S(2)}) copy-start(f32[1,384]{1,0:T(1,128)S(1)} %fusion.100.skip_ref) | copy-start | bytes 4612
  85.7 32.9 %copy-start.75 = (s32[16,4,128]{2,1,0:T(4,128)}, s32[16,4,128]{2,1,0:T(4,128)S(1)}, u32[]{:S(2)}) copy-start(s32[16,4,128]{2,1,0:T(4,128)S(1)} %copy.375) | copy-start | bytes 98308
  141.1 23.1 %copy-start.4 = (f32[1,640]{1,0:T(1,128)}, f32[1,640]{1,0:T(1,128)S(1)}, u32[]{:S(2)}) copy-start(f32[1,640]{1,0:T(1,128)S(1)} %maximum_convert_fusion.2.bias_ref) | copy-start | bytes 7684
  141.2 23.0 %copy-start.2 = (f32[4,640]{1,0:T(4,128)}, f32[4,640]{1,0:T(4,128)S(1)}, u32[]{:S(2)}) copy-start(f32[4,640]{1,0:T(4,128)S(1)} %maximum_convert_fusion.1.weight_ref) | copy-start | bytes 30724
  142.6 6.0 collective-permute-start
  150.0 14.2 %copy-start.8 = (f32[1,384]{1,0:T(1,128)}, f32[1,384]{1,0:T(1,128)S(1)}, u32[]{:S(2)}) copy-start(f32[1,384]{1,0:T(1,128)S(1)} %reshape.536.gain_ref) | copy-start | bytes 4612
  203.5 34.2 %copy-start.23 = (bf16[2,128,1536]{2,1,0:T(8,128)(2,1)S(1)}, bf16[2,128,1536]{2,1,0:T(8,128)(2,1)}, u32[]{:S(2)}) copy-start(bf16[2,128,1536]{2,1,0:T(8,128)(2,1)} %param.20) | copy-start | bytes 2359300
  238.2 33.4 %copy-start.84 = (f32[256]{0:T(256)}, f32[256]{0:T(256)S(1)}, u32[]{:S(2)}) copy-start(f32[256]{0:T(256)S(1)} %add_rsqrt_fusion.1) | copy-start | bytes 3076
  410.4 538.1 %reduce-scatter.28.cloned.1.call-start = ((), (), s32[]{:S(2)}) async-start(), calls=%async_computation.27 | async-start | bytes 1966080 | tf_op jit(solution)/shard_map/reduce_scatter | solution.py:623
  557.6 390.9 %reduce-scatter.30.cloned.1.call-start = ((), (), s32[]{:S(2)}) async-start(), calls=%async_computation.28 | async-start | bytes 1966080 | tf_op jit(solution)/shard_map/reduce_scatter | solution.py:623
  577.1 371.4 %reduce-scatter.32.cloned.1.call-start = ((), (), s32[]{:S(2)}) async-start(), calls=%async_computation.29 | async-start | bytes 1966080 | tf_op jit(solution)/shard_map/reduce_scatter | solution.py:623
  631.7 316.8 %reduce-scatter.26.cloned.1.call-start = ((), (), s32[]{:S(2)}) async-start(), calls=%async_computation.26 | async-start | bytes 1966080 | tf_op jit(solution)/shard_map/reduce_scatter | solution.py:623
  661.2 33.8 %copy-start.74 = (pred[256,32]{1,0:T(8,128)(4,1)S(1)}, pred[256,32]{1,0:T(8,128)(4,1)}, u32[]{:S(2)}) copy-start(pred[256,32]{1,0:T(8,128)(4,1)} %copy.394) | copy-start | bytes 24580
  661.2 34.5 %copy-start.85 = (f32[256]{0:T(256)S(1)}, f32[256]{0:T(256)}, u32[]{:S(2)}) copy-start(f32[256]{0:T(256)} %copy-done.84) | copy-start | bytes 3076
  701.2 250.7 %reduce-scatter.14.cloned.1.call-start = ((), (), s32[]{:S(2)}) async-start(), calls=%async_computation.20 | async-start | bytes 1966080 | tf_op jit(solution)/shard_map/reduce_scatter | solution.py:623
  705.0 34.3 %copy-start.15 = (bf16[2048,384]{1,0:T(8,128)(2,1)S(1)}, bf16[2048,384]{1,0:T(8,128)(2,1)}, u32[]{:S(2)}) copy-start(bf16[2048,384]{1,0:T(8,128)(2,1)} %copy-done.14) | copy-start | bytes 4718596
  744.8 4.7 collective-permute-start.6
  751.0 205.0 %reduce-scatter.20.cloned.1.call-start = ((), (), s32[]{:S(2)}) async-start(), calls=%async_computation.23 | async-start | bytes 3932160 | tf_op jit(solution)/shard_map/reduce_scatter | solution.py:623
  757.0 200.3 %reduce-scatter.22.cloned.1.call-start = ((), (), s32[]{:S(2)}) async-start(), calls=%async_computation.24 | async-start | bytes 3932160 | tf_op jit(solution)/shard_map/reduce_scatter | solution.py:623
  764.1 212.0 %reduce-scatter.24.cloned.1.call-start = ((), (), s32[]{:S(2)}) async-start(), calls=%async_computation.25 | async-start | bytes 3932160 | tf_op jit(solution)/shard_map/reduce_scatter | solution.py:623
  771.2 273.4 %reduce-scatter.34.cloned.1.call-start = ((), (), s32[]{:S(2)}) async-start(), calls=%async_computation.34 | async-start | bytes 4423680 | tf_op jit(solution)/shard_map/reduce_scatter | solution.py:623
  783.0 21.6 %copy-start.80 = (f32[1536]{0:T(1024)S(1)}, f32[1536]{0:T(1024)}, u32[]{:S(2)}) copy-start(f32[1536]{0:T(1024)} %copy-done.79) | copy-start | bytes 18436
  783.0 21.6 %copy-start.93 = (f32[2048]{0:T(1024)S(1)}, f32[2048]{0:T(1024)}, u32[]{:S(2)}) copy-start(f32[2048]{0:T(1024)} %copy-done.92) | copy-start | bytes 24580
  826.9 280.6 %reduce-scatter.18.cloned.1.call-start = ((), (), s32[]{:S(2)}) async-start(), calls=%async_computation.22 | async-start | bytes 3932160 | tf_op jit(solution)/shard_map/reduce_scatter | solution.py:623
  830.2 24.5 %collective-permute-start.1 = (f32[6,3328]{1,0:T(8,128)}, f32[6,3328]{1,0:T(8,128)S(1)}, u32[]{:S(2)}, u32[]{:S(2)}) collective-permute-start(f32[6,3328]{1,0:T(8,128)} %select_maximum_fusion), channel_id=1, source_target_pairs={{0,8},{8,0},{16,24},{24,16},{1,9},{9,1},{17,25},{25,17},{2,10},{10... | collective-permute-start | bytes 239624 | tf_op jit(solution)/shard_map/ppermute | solution.py:542
  854.7 39.9 %collective-permute-start.2 = (f32[6,3328]{1,0:T(8,128)S(1)}, f32[6,3328]{1,0:T(8,128)S(1)}, u32[]{:S(2)}, u32[]{:S(2)}) collective-permute-start(f32[6,3328]{1,0:T(8,128)S(1)} %fusion.184), channel_id=1, source_target_pairs={{0,16},{8,24},{16,0},{24,8},{1,17},{9,25},{17,1},{25,9},{2,18},{10... | collective-permute-start | bytes 239624 | tf_op jit(solution)/shard_map/ppermute | solution.py:542
  894.7 1.4 collective-permute-start.3
  896.1 32.2 %collective-permute-start.4 = (f32[6,3328]{1,0:T(8,128)S(1)}, f32[6,3328]{1,0:T(8,128)S(1)}, u32[]{:S(2)}, u32[]{:S(2)}) collective-permute-start(f32[6,3328]{1,0:T(8,128)S(1)} %add.219), channel_id=1, source_target_pairs={{0,2},{1,3},{2,0},{3,1},{4,6},{5,7},{6,4},{7,5},{8,10},{9,11},{10,... | collective-permute-start | bytes 239624 | tf_op jit(solution)/shard_map/ppermute | solution.py:542
  897.2 31.9 %copy-start.25 = (f32[256,1536]{1,0:T(8,128)S(1)}, f32[256,1536]{1,0:T(8,128)}, u32[]{:S(2)}) copy-start(f32[256,1536]{1,0:T(8,128)} %get-tuple-element.211) | copy-start | bytes 4718596
  897.2 31.9 %copy-start.29 = (bf16[2,128,1536]{2,1,0:T(8,128)(2,1)S(1)}, bf16[2,128,1536]{2,1,0:T(8,128)(2,1)}, u32[]{:S(2)}) copy-start(bf16[2,128,1536]{2,1,0:T(8,128)(2,1)} %param.21) | copy-start | bytes 2359300
  928.4 5.2 collective-permute-start.5
  934.9 9.7 all-to-all-start.2
  1044.7 69.7 %all-to-all-start.1 = ((bf16[8,48,1152]{2,1,0:T(8,128)(2,1)}), bf16[8,48,1152]{2,1,0:T(8,128)(2,1)S(1)}, u32[]{:S(2)}, u32[]{:S(2)}) async-start(bf16[8,48,1152]{2,1,0:T(8,128)(2,1)} %bitcast.418), calls=%async_computation.1 | async-start | bytes 1769472 | tf_op jit(solution)/shard_map/all_to_all | solution.py:827
  (113 other events, 479.6 us)
Sparse Core Ops, SparseCore 0:
  10.2 41.9 all-gather.16
  53.8 81.7 all-gather.14
  137.7 62.0 all-gather.24
  201.2 62.1 all-gather.18
  265.4 62.1 all-gather.22
  329.0 62.1 all-gather.20
  392.7 35.7 all-gather.26
  430.1 35.9 all-gather.30
  467.6 35.9 all-gather.28
  505.0 35.9 all-gather.32
  543.3 22.1 reduce-scatter.15
  567.7 34.5 reduce-scatter.27
  604.6 34.2 reduce-scatter.29
  641.0 34.2 reduce-scatter.31
  701.3 33.7 reduce-scatter.25
  751.1 33.4 reduce-scatter.13
  786.8 61.4 reduce-scatter.19
  851.0 61.3 reduce-scatter.21
  915.3 60.7 reduce-scatter.23
  978.2 66.3 reduce-scatter.33
  1047.0 60.5 reduce-scatter.17

commit v2 on v1

--- a/solution.py
+++ b/solution.py
@@ -252,9 +252,7 @@
         ],
         scratch_shapes=[pltpu.VMEM((LANES, LEN), f32)],
         compiler_params=pltpu.CompilerParams(vmem_limit_bytes=32 << 20),
-        cost_estimate=pl.CostEstimate(
-            flops=tokens * width * 9000, bytes_accessed=tokens * columns * 8, transcendentals=0
-        ),
+        cost_estimate=pl.CostEstimate(flops=0, bytes_accessed=1024, transcendentals=0),
     )(merged, *params)
 
 
@@ -283,9 +281,7 @@
         ],
         scratch_shapes=[pltpu.VMEM((LANES, LEN), f32)],
         compiler_params=pltpu.CompilerParams(vmem_limit_bytes=32 << 20),
-        cost_estimate=pl.CostEstimate(
-            flops=tokens * width * 18000, bytes_accessed=tokens * columns * 12, transcendentals=0
-        ),
+        cost_estimate=pl.CostEstimate(flops=0, bytes_accessed=1024, transcendentals=0),
     )(merged, joined, grad, inward, *params)
 
 
@@ -297,206 +293,461 @@
     return 1 - 2 * core, 2 - 4 * column, 4 - 8 * line
 
 
+def other_plane(me):
+    place = lax.axis_index("dp")
+    return {"dp": place + 1 - 2 * (place % 2), "expert": me}
+
+
 def greet(peers):
     barrier = pltpu.get_barrier_semaphore()
     for peer in peers:
-        pl.semaphore_signal(barrier, inc=1, device_id={"expert": peer}, device_id_type=MESH)
+        pl.semaphore_signal(barrier, inc=1, device_id=peer, device_id_type=MESH)
     pl.semaphore_wait(barrier, len(peers))
 
 
-def gather_kernel(own_ref, out_ref, send_sem, recv_sem, copy_sem):
+def far_plane(me):
+    place = lax.axis_index("dp")
+    return {"dp": place + 2 - 4 * (place // 2), "expert": me}
+
+
+def peers_of(me, across, along=0):
+    core, column, line = neighbours(me)
+    peers = [{"expert": me + core}, {"expert": me + column}, {"expert": me + line}]
+    peers = peers + ([other_plane(me)] if across else [])
+    return peers + ([far_plane(me)] if along else [])
+
+
+def begin_swaps(refs, swaps, first, send_sem, recv_sem, peer):
+    found = []
+    for i in range(swaps):
+        found.append(remote(send_sem, recv_sem, first + i, refs[i], refs[swaps + i], peer[0]))
+        found[-1].start()
+    return found
+
+
+def remote(send_sem, recv_sem, at, src, dst, peer):
+    return pltpu.make_async_remote_copy(
+        src_ref=src,
+        dst_ref=dst,
+        send_sem=send_sem.at[at],
+        recv_sem=recv_sem.at[at],
+        device_id=peer,
+        device_id_type=MESH,
+    )
+
+
+def gather_kernel(sets, count, swaps, lines, waits, *refs):
+    total = count + swaps + lines
+    owns, give, block = refs[:count], refs[count : count + swaps], refs[count + swaps : total]
+    refs = refs[total + waits :]
+    outs, take, line_out = refs[:count], refs[count : count + swaps], refs[count + swaps : total]
+    send_sem, recv_sem, copy_sem = refs[total:]
     me = lax.axis_index("expert")
     core, column, line = neighbours(me)
-    rows = own_ref.shape[0]
-    top, bottom = pl.ds(0, rows // 2), pl.ds(rows // 2, rows // 2)
-    greet((me + core, me + column, me + line))
-
-    def copy(at, src, dst, peer):
-        return pltpu.make_async_remote_copy(
-            src_ref=src,
-            dst_ref=dst,
-            send_sem=send_sem.at[at],
-            recv_sem=recv_sem.at[at],
-            device_id={"expert": peer},
-            device_id_type=MESH,
+    half = owns[0].shape[0] // 2
+    top, bottom = pl.ds(0, half), pl.ds(half, half)
+    peers = peers_of(me, max(sets) == 2 or swaps or lines, lines)
+    greet(peers)
+    copy = partial(remote, send_sem, recv_sem)
+    arrays = range(count)
+    place = lax.axis_index("dp")
+    distant = place + 2 - 4 * (place // 2)
+    along = []
+    for i in range(lines):
+        base = 17 * count + swaps + 3 * i
+        own, out = block[i], line_out[i]
+        along.append(
+            (
+                pltpu.make_async_copy(own, out.at[place], copy_sem.at[count + i]),
+                copy(base, own, out.at[place], peers[4]),
+                copy(base + 1, own, out.at[place], peers[3]),
+                copy(base + 2, out.at[distant], out.at[distant], peers[3]),
+            )
         )
-
-    here = pltpu.make_async_copy(own_ref, out_ref.at[me], copy_sem)
-    to_x = copy(0, own_ref, out_ref.at[me], me + column)
-    to_y = copy(1, own_ref, out_ref.at[me], me + line)
-    to_core = copy(2, own_ref, out_ref.at[me], me + core)
-    to_x.start()
-    to_y.start()
-    to_core.start()
-    here.start()
-    x_block, y_block = out_ref.at[me + column], out_ref.at[me + line]
-    diagonal = out_ref.at[me + column + line]
-    to_x.wait_recv()
-    x_relay = copy(3, x_block.at[top], x_block.at[top], me + line)
-    x_relay.start()
-    x_core = copy(5, x_block, x_block, me + core)
-    x_core.start()
-    to_y.wait_recv()
-    y_relay = copy(4, y_block.at[bottom], y_block.at[bottom], me + column)
-    y_relay.start()
-    y_core = copy(6, y_block, y_block, me + core)
-    y_core.start()
-    x_relay.wait_recv()
-    y_relay.wait_recv()
-    d_core = copy(7, diagonal, diagonal, me + core)
-    d_core.start()
-    here.wait()
-    to_core.wait_recv()
-    x_core.wait_recv()
-    y_core.wait_recv()
-    d_core.wait_recv()
-    for sent in (to_x, to_y, to_core, x_relay, x_core, y_relay, y_core, d_core):
-        sent.wait_send()
-
-
-def plane_gather(own, number):
-    if lax.axis_size("expert") != 8:
-        return lax.all_gather(own, "expert", axis=0, tiled=True)
-    rows, columns = own.shape
-    out = pl.pallas_call(
-        gather_kernel,
-        out_shape=jax.ShapeDtypeStruct((8, rows, columns), own.dtype),
-        in_specs=[pl.BlockSpec(memory_space=pl.ANY)],
-        out_specs=pl.BlockSpec(memory_space=pl.ANY),
+    steps = []
+    here, across = [], []
+    for i in arrays:
+        here.append(pltpu.make_async_copy(owns[i], outs[i].at[me], copy_sem.at[i]))
+        if sets[i] == 2:
+            across.append(copy(17 * i + 16, owns[i], outs[i].at[8 + me], peers[3]))
+    for g in range(2):
+        for i in arrays:
+            if sets[i] <= g:
+                continue
+            out = lambda at: outs[i].at[8 * g + at]
+            own = owns[i] if g == 0 else out(me)
+            at_x, at_y, at_d = out(me + column), out(me + line), out(me + column + line)
+            base = 17 * i + 8 * g
+            steps.append(
+                (
+                    copy(base, own, out(me), peers[1]),
+                    copy(base + 1, own, out(me), peers[2]),
+                    copy(base + 2, own, out(me), peers[0]),
+                    copy(base + 3, at_x.at[top], at_x.at[top], peers[2]),
+                    copy(base + 4, at_y.at[bottom], at_y.at[bottom], peers[1]),
+                    copy(base + 5, at_x, at_x, peers[0]),
+                    copy(base + 6, at_y, at_y, peers[0]),
+                    copy(base + 7, at_d, at_d, peers[0]),
+                )
+            )
+
+    def begin(group):
+        for to_x, to_y, to_core, *unused in group:
+            to_x.start()
+            to_y.start()
+            to_core.start()
+
+    def relay(group):
+        for to_x, to_y, to_core, x_relay, y_relay, x_core, y_core, d_core in group:
+            to_x.wait_recv()
+            x_relay.start()
+            x_core.start()
+            to_y.wait_recv()
+            y_relay.start()
+            y_core.start()
+
+    def close(group):
+        for to_x, to_y, to_core, x_relay, y_relay, x_core, y_core, d_core in group:
+            x_relay.wait_recv()
+            y_relay.wait_recv()
+            d_core.start()
+
+    first, second = steps[:count], steps[count:]
+    for here_block, to_far, to_near, relayed in along:
+        to_far.start()
+        to_near.start()
+        here_block.start()
+    for copied in across:
+        copied.start()
+    begin(first)
+    swapped = begin_swaps(give + take, swaps, 17 * count, send_sem, recv_sem, peers[3:4])
+    for here_block, to_far, to_near, relayed in along:
+        to_far.wait_recv()
+        relayed.start()
+    for copied in here:
+        copied.start()
+    for copied in across:
+        copied.wait_recv()
+    begin(second)
+    relay(first)
+    close(first)
+    relay(second)
+    close(second)
+    for copied in here:
+        copied.wait()
+    for copied in across:
+        copied.wait_send()
+    for copied in swapped:
+        copied.wait()
+    for here_block, to_far, to_near, relayed in along:
+        here_block.wait()
+        to_near.wait_recv()
+        relayed.wait_recv()
+        for copied in (to_far, to_near, relayed):
+            copied.wait_send()
+    for group in steps:
+        for at in (2, 5, 6, 7):
+            group[at].wait_recv()
+        for sent in group:
+            sent.wait_send()
+
+
+def plane_gather(number, *owns, sets=1, swaps=(), lines=(), after=()):
+    if lax.axis_size("expert") != 8 or (lines and lax.axis_size("dp") != 4):
+        return [lax.all_gather(own, "expert", axis=0, tiled=True) for own in owns] + [
+            lax.all_gather(line, "dp", axis=0, tiled=True) for line in lines
+        ]
+    count = len(owns)
+    sets = (sets,) * count if isinstance(sets, int) else sets
+    total = count + len(swaps) + len(lines)
+    anywhere = pl.BlockSpec(memory_space=pl.ANY)
+    outs = pl.pallas_call(
+        partial(gather_kernel, sets, count, len(swaps), len(lines), len(after)),
+        out_shape=[
+            jax.ShapeDtypeStruct((8 * n,) + own.shape, own.dtype) for n, own in zip(sets, owns)
+        ]
+        + [jax.ShapeDtypeStruct(v.shape, v.dtype) for v in swaps]
+        + [jax.ShapeDtypeStruct((4,) + v.shape, v.dtype) for v in lines],
+        in_specs=[anywhere] * (total + len(after)),
+        out_specs=[anywhere] * total,
         scratch_shapes=[
-            pltpu.SemaphoreType.DMA((8,)),
-            pltpu.SemaphoreType.DMA((8,)),
-            pltpu.SemaphoreType.DMA,
+            pltpu.SemaphoreType.DMA((17 * count + len(swaps) + 3 * len(lines),)),
+            pltpu.SemaphoreType.DMA((17 * count + len(swaps) + 3 * len(lines),)),
+            pltpu.SemaphoreType.DMA((count + len(lines),)),
         ],
         compiler_params=pltpu.CompilerParams(collective_id=number, has_side_effects=True),
-        cost_estimate=pl.CostEstimate(
-            flops=0, bytes_accessed=rows * columns * 96, transcendentals=0
-        ),
-    )(own)
-    return out.reshape(8 * rows, columns)
-
-
-def scatter_kernel(
-    parts_ref, out_ref, mine, theirs, x_in, y_in, dx_in, dy_in, send_sem, recv_sem, copy_sem
-):
+        cost_estimate=pl.CostEstimate(flops=0, bytes_accessed=1024, transcendentals=0),
+    )(*owns, *swaps, *lines, *after)
+    gathered = [out.reshape(-1, out.shape[2]) for out in outs[:count]]
+    spread = [out.reshape(4 * out.shape[1], out.shape[2]) for out in outs[total - len(lines) :]]
+    return gathered + list(outs[count : total - len(lines)]) + spread
+
+
+def scatter_kernel(sets, count, extra, gathers, lines, waits, *refs):
+    parts, give = refs[:count], refs[count : count + extra]
+    refs = refs[count + extra :]
+    owns, blocks = refs[:gathers], refs[gathers : gathers + lines]
+    refs = refs[gathers + lines + waits :]
+    outs, take = refs[:count], refs[count : count + extra]
+    refs = refs[count + extra :]
+    gathered, line_outs = refs[:gathers], refs[gathers : gathers + lines]
+    refs = refs[gathers + lines :]
+    per = 6 * sets + (3 if sets == 2 else 0)
+    held = [refs[per * i : per * (i + 1)] for i in range(count)]
+    send_sem, recv_sem, copy_sem = refs[per * count :]
     me = lax.axis_index("expert")
     core, column, line = neighbours(me)
-    rows = out_ref.shape[0]
+    rows = outs[0].shape[0]
     half = rows // 2
     top, bottom = pl.ds(0, half), pl.ds(half, half)
-    greet((me + core, me + column, me + line))
-
-    def copy(at, src, dst, peer):
-        return pltpu.make_async_remote_copy(
-            src_ref=src,
-            dst_ref=dst,
-            send_sem=send_sem.at[at],
-            recv_sem=recv_sem.at[at],
-            device_id={"expert": peer},
-            device_id_type=MESH,
+    peers = peers_of(me, sets == 2 or extra or lines, lines)
+    greet(peers)
+    copy = partial(remote, send_sem, recv_sem)
+    arrays = range(count)
+    chips = (me + column + line, me + column, me + line, me)
+    order = range(sets - 1, -1, -1)
+    keep = lambda g, i, at: held[i][6 * g + at]
+    total_ref = lambda g, i: outs[i] if g == 0 else held[i][12]
+    swaps, loads = {}, {}
+    for g in order:
+        for k in range(4):
+            for i in arrays:
+                base = 21 * i + 10 * g + k
+                swaps[g, i, k] = copy(
+                    base, parts[i].at[8 * g + chips[k] + core], keep(g, i, 1).at[k], peers[0]
+                )
+                loads[g, i, k] = pltpu.make_async_copy(
+                    parts[i].at[8 * g + chips[k]],
+                    keep(g, i, 0).at[k],
+                    copy_sem.at[8 * i + 4 * g + k],
+                )
+                swaps[g, i, k].start()
+                loads[g, i, k].start()
+
+    swapped = begin_swaps(give + take, extra, 21 * count, send_sem, recv_sem, peers[3:4])
+    base = 21 * count + extra
+    place = lax.axis_index("dp")
+    distant = place + 2 - 4 * (place // 2)
+    here, small, along = [], [], []
+    for i in range(gathers):
+        own, out = owns[i], lambda at: gathered[i].at[at]
+        at_x, at_y, at_d = out(me + column), out(me + line), out(me + column + line)
+        low, high = pl.ds(0, own.shape[0] // 2), pl.ds(own.shape[0] // 2, own.shape[0] // 2)
+        here.append(pltpu.make_async_copy(own, out(me), copy_sem.at[8 * count + i]))
+        small.append(
+            (
+                copy(base, own, out(me), peers[1]),
+                copy(base + 1, own, out(me), peers[2]),
+                copy(base + 2, own, out(me), peers[0]),
+                copy(base + 3, at_x.at[low], at_x.at[low], peers[2]),
+                copy(base + 4, at_y.at[high], at_y.at[high], peers[1]),
+                copy(base + 5, at_x, at_x, peers[0]),
+                copy(base + 6, at_y, at_y, peers[0]),
+                copy(base + 7, at_d, at_d, peers[0]),
+            )
         )
-
-    chips = (me + column + line, me + column, me + line, me)
-    swaps = [copy(k, parts_ref.at[chips[k] + core], theirs.at[k], me + core) for k in range(4)]
-    loads = [
-        pltpu.make_async_copy(parts_ref.at[chips[k]], mine.at[k], copy_sem.at[k]) for k in range(4)
-    ]
-    for k in range(4):
-        swaps[k].start()
-        loads[k].start()
-
-    def each(first, count, step):
-        def body(i, carry):
-            step(pl.ds(pl.multiple_of(first + i * 16, 16), 16))
+        base += 8
+        for begun in [here[-1]] + list(small[-1][:3]):
+            begun.start()
+    for i in range(lines):
+        own, out = blocks[i], line_outs[i]
+        here.append(pltpu.make_async_copy(own, out.at[place], copy_sem.at[8 * count + gathers + i]))
+        along.append(
+            (
+                copy(base, own, out.at[place], peers[4]),
+                copy(base + 1, own, out.at[place], peers[3]),
+                copy(base + 2, out.at[distant], out.at[distant], peers[3]),
+            )
+        )
+        base += 3
+        for begun in [here[-1]] + list(along[-1][:2]):
+            begun.start()
+
+    def each(first, amount, step):
+        def body(at, carry):
+            step(pl.ds(pl.multiple_of(first + at * 16, 16), 16))
             return carry
 
-        lax.fori_loop(0, count // 16, body, 0)
-
-    def pair_sum(k):
-        loads[k].wait()
-        swaps[k].wait_recv()
+        lax.fori_loop(0, amount // 16, body, 0)
+
+    def pair_sum(g, k):
+        for i in arrays:
+            loads[g, i, k].wait()
+            swaps[g, i, k].wait_recv()
 
         def step(block):
-            total = mine[k, block].astype(f32) + theirs[k, block].astype(f32)
-            if k == 3:
-                out_ref[block, :] = total
-            else:
-                mine[k, block] = total.astype(b16)
+            for i in arrays:
+                mine, theirs = keep(g, i, 0), keep(g, i, 1)
+                total = mine[k, block].astype(f32) + theirs[k, block].astype(f32)
+                if k == 3:
+                    total_ref(g, i)[block, :] = total
+                else:
+                    mine[k, block] = total.astype(b16)
 
         each(0, rows, step)
 
-    pair_sum(0)
-    d_x = copy(4, mine.at[0, top], dx_in, me + column)
-    d_y = copy(5, mine.at[0, bottom], dy_in, me + line)
-    d_x.start()
-    d_y.start()
-    pair_sum(1)
-    x_top = copy(6, mine.at[1, top], x_in.at[top], me + column)
-    x_top.start()
-    pair_sum(2)
-    y_bottom = copy(7, mine.at[2, bottom], y_in.at[bottom], me + line)
-    y_bottom.start()
-    pair_sum(3)
-
-    d_x.wait_recv()
-
-    def add_y(block):
-        mine[2, block] = (mine[2, block].astype(f32) + dx_in[block, :].astype(f32)).astype(b16)
-
-    each(0, half, add_y)
-    y_top = copy(8, mine.at[2, top], y_in.at[top], me + line)
-    y_top.start()
-    d_y.wait_recv()
-
-    def add_x(block):
-        low = pl.ds(pl.multiple_of(block.start - half, 16), 16)
-        mine[1, block] = (mine[1, block].astype(f32) + dy_in[low, :].astype(f32)).astype(b16)
-
-    each(half, half, add_x)
-    x_bottom = copy(9, mine.at[1, bottom], x_in.at[bottom], me + column)
-    x_bottom.start()
-    x_top.wait_recv()
-    y_bottom.wait_recv()
-    y_top.wait_recv()
-    x_bottom.wait_recv()
-
-    def finish(block):
-        out_ref[block, :] = (
-            out_ref[block, :] + x_in[block, :].astype(f32) + y_in[block, :].astype(f32)
-        )
-
-    each(0, rows, finish)
-    for sent in swaps + [d_x, d_y, x_top, y_bottom, y_top, x_bottom]:
-        sent.wait_send()
-
-
-def plane_scatter(parts, number):
+    sent = []
+
+    def sends(g, at, k, area, into, peer):
+        found = []
+        for i in arrays:
+            target = keep(g, i, into)
+            target = target if into > 3 else target.at[area]
+            source = keep(g, i, 0).at[k, area]
+            found.append(copy(21 * i + 10 * g + at, source, target, peer))
+            found[-1].start()
+        sent.extend(found)
+        return found
+
+    legs = {}
+    for g in order:
+        pair_sum(g, 0)
+        d_x = sends(g, 4, 0, top, 4, peers[1])
+        d_y = sends(g, 5, 0, bottom, 5, peers[2])
+        pair_sum(g, 1)
+        x_top = sends(g, 6, 1, top, 2, peers[1])
+        pair_sum(g, 2)
+        y_bottom = sends(g, 7, 2, bottom, 3, peers[2])
+        pair_sum(g, 3)
+        legs[g] = [d_x, d_y, x_top, y_bottom]
+
+    for to_x, to_y, to_core, x_relay, y_relay, x_core, y_core, d_core in small:
+        to_x.wait_recv()
+        x_relay.start()
+        x_core.start()
+        to_y.wait_recv()
+        y_relay.start()
+        y_core.start()
+    for to_far, to_near, relayed in along:
+        to_far.wait_recv()
+        relayed.start()
+
+    for g in order:
+        d_x, d_y, x_top, y_bottom = legs[g]
+        for i in arrays:
+            d_x[i].wait_recv()
+
+        def add_y(block):
+            for i in arrays:
+                mine, extra = keep(g, i, 0), keep(g, i, 4)
+                mine[2, block] = (
+                    mine[2, block].astype(f32) + extra[block, :].astype(f32)
+                ).astype(b16)
+
+        each(0, half, add_y)
+        y_top = sends(g, 8, 2, top, 3, peers[2])
+        for i in arrays:
+            d_y[i].wait_recv()
+
+        def add_x(block):
+            low = pl.ds(pl.multiple_of(block.start - half, 16), 16)
+            for i in arrays:
+                mine, extra = keep(g, i, 0), keep(g, i, 5)
+                mine[1, block] = (
+                    mine[1, block].astype(f32) + extra[low, :].astype(f32)
+                ).astype(b16)
+
+        each(half, half, add_x)
+        x_bottom = sends(g, 9, 1, bottom, 2, peers[1])
+        legs[g] = [x_top, y_bottom, y_top, x_bottom]
+
+    for to_x, to_y, to_core, x_relay, y_relay, x_core, y_core, d_core in small:
+        x_relay.wait_recv()
+        y_relay.wait_recv()
+        d_core.start()
+    across = []
+    for g in order:
+        for i in arrays:
+            for came in legs[g]:
+                came[i].wait_recv()
+
+        def finish(block):
+            for i in arrays:
+                total = (
+                    total_ref(g, i)[block, :]
+                    + keep(g, i, 2)[block, :].astype(f32)
+                    + keep(g, i, 3)[block, :].astype(f32)
+                )
+                if g == 0:
+                    outs[i][block, :] = total
+                else:
+                    held[i][13][block, :] = total.astype(b16)
+
+        each(0, rows, finish)
+        if g == 1:
+            for i in arrays:
+                across.append(copy(21 * i + 20, held[i][13], held[i][14], peers[3]))
+                across[-1].start()
+    if sets == 2:
+        for i in arrays:
+            across[i].wait_recv()
+
+        def add_z(block):
+            for i in arrays:
+                outs[i][block, :] = outs[i][block, :] + held[i][14][block, :].astype(f32)
+
+        each(0, rows, add_z)
+    for done in list(swaps.values()) + sent + across:
+        done.wait_send()
+    for copied in swapped + here:
+        copied.wait()
+    for group in small:
+        for at in (2, 5, 6, 7):
+            group[at].wait_recv()
+        for copied in group:
+            copied.wait_send()
+    for to_far, to_near, relayed in along:
+        to_near.wait_recv()
+        relayed.wait_recv()
+        for copied in (to_far, to_near, relayed):
+            copied.wait_send()
+
+
+def plane_scatter(number, *parts, sets=1, swaps=(), gathers=(), lines=(), after=()):
     if lax.axis_size("expert") != 8:
-        return lax.psum_scatter(parts, "expert", scatter_dimension=0, tiled=True).astype(f32)
-    rows, columns = parts.shape[0] // 8, parts.shape[1]
+        return [
+            lax.psum_scatter(part, "expert", scatter_dimension=0, tiled=True).astype(f32)
+            for part in parts
+        ] + [lax.all_gather(v, "expert", axis=0) for v in gathers] + [
+            lax.all_gather(v, "dp", axis=0) for v in lines
+        ]
+    count = len(parts)
+    others = list(swaps) + list(gathers) + list(lines) + list(after)
+    moved = len(others) - len(after)
+    sems = 21 * count + len(swaps) + 8 * len(gathers) + 3 * len(lines)
+    rows = parts[0].shape[0] // (8 * sets)
+    scratch = []
+    for part in parts:
+        columns = part.shape[1]
+        for g in range(sets):
+            scratch += [pltpu.VMEM((4, rows, columns), b16)] * 2
+            scratch += [pltpu.VMEM((rows, columns), b16)] * 2
+            scratch += [pltpu.VMEM((rows // 2, columns), b16)] * 2
+        if sets == 2:
+            scratch += [pltpu.VMEM((rows, columns), f32)]
+            scratch += [pltpu.VMEM((rows, columns), b16)] * 2
     return pl.pallas_call(
-        scatter_kernel,
-        out_shape=jax.ShapeDtypeStruct((rows, columns), f32),
-        in_specs=[pl.BlockSpec(memory_space=pl.ANY)],
-        out_specs=pl.BlockSpec(memory_space=pltpu.VMEM),
-        scratch_shapes=[
-            pltpu.VMEM((4, rows, columns), b16),
-            pltpu.VMEM((4, rows, columns), b16),
-            pltpu.VMEM((rows, columns), b16),
-            pltpu.VMEM((rows, columns), b16),
-            pltpu.VMEM((rows // 2, columns), b16),
-            pltpu.VMEM((rows // 2, columns), b16),
-            pltpu.SemaphoreType.DMA((10,)),
-            pltpu.SemaphoreType.DMA((10,)),
-            pltpu.SemaphoreType.DMA((4,)),
+        partial(
+            scatter_kernel, sets, count, len(swaps), len(gathers), len(lines), len(after)
+        ),
+        out_shape=[jax.ShapeDtypeStruct((rows, part.shape[1]), f32) for part in parts]
+        + [jax.ShapeDtypeStruct(v.shape, v.dtype) for v in swaps]
+        + [jax.ShapeDtypeStruct((8,) + v.shape, v.dtype) for v in gathers]
+        + [jax.ShapeDtypeStruct((4,) + v.shape, v.dtype) for v in lines],
+        in_specs=[pl.BlockSpec(memory_space=pl.ANY)] * (count + len(others)),
+        out_specs=[pl.BlockSpec(memory_space=pltpu.VMEM)] * count
+        + [pl.BlockSpec(memory_space=pl.ANY)] * moved,
+        scratch_shapes=scratch
+        + [
+            pltpu.SemaphoreType.DMA((sems,)),
+            pltpu.SemaphoreType.DMA((sems,)),
+            pltpu.SemaphoreType.DMA((8 * count + len(gathers) + len(lines),)),
         ],
         compiler_params=pltpu.CompilerParams(
-            collective_id=number, has_side_effects=True, vmem_limit_bytes=32 << 20
+            collective_id=number, has_side_effects=True, vmem_limit_bytes=(16 + 24 * sets) << 20
         ),
-        cost_estimate=pl.CostEstimate(
-            flops=0, bytes_accessed=rows * columns * 128, transcendentals=0
-        ),
-    )(parts.reshape(8, rows, columns))
+        cost_estimate=pl.CostEstimate(flops=0, bytes_accessed=1024, transcendentals=0),
+    )(*[part.reshape(8 * sets, rows, part.shape[1]) for part in parts], *others)
 
 
 def rms_scale(value, gain):
@@ -537,6 +788,10 @@
     return weight / jnp.sum(weight, axis=1, keepdims=True)
 
 
+def tie(*values):
+    return lax.optimization_barrier(values)
+
+
 def exchange(value, axis, distance):
     size = lax.axis_size(axis)
     return lax.ppermute(value, axis, [(i, i ^ distance) for i in range(size)])
@@ -549,6 +804,108 @@
             value = value + exchange(value, axis, distance)
             distance *= 2
     return value
+
+
+def merge_kernel(near, parts, select_ref, *refs):
+    rows_refs, (small_ref, weight_ref), out_ref = refs[:parts], refs[parts : parts + 2], refs[-1]
+    slots = select_ref.shape[1] // parts
+    total = None
+    for k in range(parts):
+        term = lax.dot_general(
+            select_ref[0, k * slots : (k + 1) * slots, :],
+            rows_refs[k][0],
+            (((0,), (0,)), ((), ())),
+            preferred_element_type=f32,
+        )
+        total = term if total is None else total + term
+    first = pl.program_id(0) < near
+
+    @pl.when(first)
+    def _():
+        out_ref[...] = (total + dot(small_ref[...], weight_ref[...])).astype(b16)
+
+    @pl.when(jnp.logical_not(first))
+    def _():
+        out_ref[...] = total.astype(b16)
+
+
+def merge(select, parts, small, weight, after=()):
+    seqs, slots, unused = select.shape
+    slots = slots // len(parts)
+    width = weight.shape[1]
+    near = small.shape[0] // LEN
+    return pl.pallas_call(
+        partial(merge_kernel, near, len(parts)),
+        grid=(seqs,),
+        in_specs=[pl.BlockSpec((1,) + select.shape[1:], lambda s: (s, 0, 0))]
+        + [pl.BlockSpec((1, slots, width), lambda s: (s, 0, 0))] * len(parts)
+        + [
+            pl.BlockSpec((LEN, small.shape[1]), lambda s: (jnp.minimum(s, near - 1), 0)),
+            fixed(*weight.shape),
+        ]
+        + [pl.BlockSpec(memory_space=pl.ANY)] * len(after),
+        out_specs=rows_of(width),
+        out_shape=jax.ShapeDtypeStruct((seqs * LEN, width), b16),
+        compiler_params=pltpu.CompilerParams(vmem_limit_bytes=32 << 20),
+        cost_estimate=pl.CostEstimate(flops=0, bytes_accessed=1024, transcendentals=0),
+    )(select, *[v.reshape(seqs, slots, width) for v in parts], small, weight, *after)
+
+
+def spread_kernel(parts, select_ref, rows_ref, *out_refs):
+    slots = select_ref.shape[1] // parts
+    rows = dot(select_ref[0], rows_ref[...]).astype(b16)
+    for k in range(parts):
+        out_refs[k][0] = rows[k * slots : (k + 1) * slots]
+
+
+def spread(select, rows, parts):
+    seqs, slots, unused = select.shape
+    slots = slots // parts
+    width = rows.shape[1]
+    outs = pl.pallas_call(
+        partial(spread_kernel, parts),
+        grid=(seqs,),
+        in_specs=[
+            pl.BlockSpec((1,) + select.shape[1:], lambda s: (s, 0, 0)),
+            rows_of(width),
+        ],
+        out_specs=[pl.BlockSpec((1, slots, width), lambda s: (s, 0, 0))] * parts,
+        out_shape=[jax.ShapeDtypeStruct((seqs, slots, width), b16)] * parts,
+        compiler_params=pltpu.CompilerParams(vmem_limit_bytes=32 << 20),
+        cost_estimate=pl.CostEstimate(flops=0, bytes_accessed=1024, transcendentals=0),
+    )(select, rows)
+    return [v.reshape(seqs * slots, width) for v in outs]
+
+
+def bank_kernel(parity_ref, gate_ref, up_ref, down_ref, out_ref):
+    columns = gate_ref.shape[2]
+    rows = down_ref.shape[1]
+    out_ref[0, 0, :, :columns] = gate_ref[0]
+    out_ref[0, 0, :, columns : 2 * columns] = up_ref[0]
+    for k in range(3):
+        out_ref[0, 0, k * rows : (k + 1) * rows, 2 * columns :] = down_ref[
+            0, :, k * columns : (k + 1) * columns
+        ]
+
+
+def bank_rows(parity, gate, up, down):
+    local, rows, columns = gate.shape
+    half = local // 2
+    which = lambda side, e, p: ((p[0] + side) % 2 * half + e, 0, 0)
+    block = lambda v: pl.BlockSpec((1,) + v.shape[1:], which)
+    return pl.pallas_call(
+        bank_kernel,
+        grid_spec=pltpu.PrefetchScalarGridSpec(
+            num_scalar_prefetch=1,
+            grid=(2, half),
+            in_specs=[block(gate), block(up), block(down)],
+            out_specs=pl.BlockSpec(
+                (1, 1, rows, 3 * columns), lambda side, e, p: (side, e, 0, 0)
+            ),
+        ),
+        out_shape=jax.ShapeDtypeStruct((2, half, rows, 3 * columns), b16),
+        cost_estimate=pl.CostEstimate(flops=0, bytes_accessed=1024, transcendentals=0),
+    )(parity.reshape(1), gate, up, down)
 
 
 class Heads:
@@ -610,6 +967,10 @@
     picks = routes.shape[-1]
     local = expert_gate.shape[0]
     experts = local * plane
+    sets = 2 if planes == 4 and plane == 8 else 1
+    place = lax.axis_index("dp")
+    odd = place % 2 == 1
+    taken = local // sets
     capacity = 3 * length * picks // (2 * experts)
     slots = -(-capacity // 8) * 8
     tokens = micro * length
@@ -648,6 +1009,37 @@
         axis=2,
     ).transpose(1, 0, 2)
     came = lax.all_to_all(sent, "expert", split_axis=0, concat_axis=0, tiled=True)
+
+    third = width // 3
+    part = expert_down.shape[1]
+    stacked = lambda v: jnp.concatenate([v[:, k * third : (k + 1) * third] for k in range(3)], axis=0)
+    ends, gives = None, []
+    if sets == 2:
+        ends = [[0, 2], [1, 3]]
+        sides = bank_rows((place % 2).astype(jnp.int32), expert_gate, expert_up, expert_down)
+        banks = [sides[0, e] for e in range(taken)]
+        gives = [sides[1, e] for e in range(taken)]
+    else:
+        banks = [
+            jnp.concatenate([expert_gate[e], expert_up[e], stacked(expert_down[e])], axis=1)
+            for e in range(local)
+        ]
+
+    def settle(e, came):
+        rows = came.shape[0]
+        both = jnp.zeros((2 * rows, came.shape[1]), b16)
+        both = lax.dynamic_update_slice_in_dim(both, banks[e], place % 2 * rows, 0)
+        banks[e] = lax.dynamic_update_slice_in_dim(both, came, (1 - place % 2) * rows, 0)
+
+    own_routes = jnp.pad(routes.reshape(tokens, picks).astype(b16), ((0, 0), (0, LANES - picks)))
+    flat_in = block_input.reshape(tokens, width)
+    grad_low = out_grad.reshape(tokens, width)
+    flat_in, came = tie(flat_in, came)
+    all_in, all_grad, all_routes, *swapped = plane_gather(
+        0, flat_in, grad_low, own_routes, sets=(1, sets, sets), swaps=gives
+    )
+    for e, other in enumerate(swapped):
+        settle(e, other)
     proj = gather(came.reshape(plane * shard, -1), "dp")
     in_w = proj[:, :main]
     gate_up = proj[:, main:]
@@ -655,15 +1047,9 @@
     gain_in = proj[:, first].astype(f32)
     gain_mid = proj[:, first + 1].astype(f32)
     route_proj = proj[:, first + 2 : first + 2 + experts]
-
-    own_routes = jnp.pad(routes.reshape(tokens, picks).astype(b16), ((0, 0), (0, LANES - picks)))
-    flat_in = block_input.reshape(tokens, width)
-    grad_low = out_grad.reshape(tokens, width)
-    seen = plane_gather(jnp.concatenate([flat_in, own_routes], axis=1), 0)
-    all_grad = plane_gather(grad_low, 1)
-    all_in = seen[:, :width].astype(f32)
-    all_routes = seen[:, width : width + picks].astype(jnp.int32)
-    count = all_in.shape[0]
+    all_routes = all_routes[:, :picks].astype(jnp.int32)
+    near = all_in.shape[0]
+    count = all_grad.shape[0]
     seqs = count // LEN
 
     out_shard = jnp.concatenate(
@@ -706,7 +1092,7 @@
         gain_mix.astype(f32).reshape(1, -1),
     )
 
-    normed = rms_scale(all_in, gain_in).astype(b16)
+    normed = rms_scale(all_in.astype(f32), gain_in).astype(b16)
     merged = dot(normed, in_w)
     mixed, joined, square = mix_forward(merged, params)
     square = jnp.sum(square, axis=1, keepdims=True)
@@ -714,19 +1100,24 @@
     square_low = (square - square_high.astype(f32)).astype(b16)
     lane = jnp.arange(LANES)[None]
     tail = jnp.where(lane == 2 * at, square_high, jnp.where(lane == 2 * at + 1, square_low, 0))
-    summed = plane_scatter(
-        jnp.concatenate([dot(mixed, out_w).astype(b16), tail.astype(b16)], axis=1), 2
-    )
-    scale = lax.rsqrt(jnp.sum(summed[:, width:], axis=1, keepdims=True) / inner + epsilon)
-    mixer_out = scale * summed[:, :width]
+    summed, squares = plane_scatter(2, dot(mixed, out_w).astype(b16), tail.astype(b16))
+    scale = lax.rsqrt(jnp.sum(squares, axis=1, keepdims=True) / inner + epsilon)
+    mixer_out = scale * summed
     start = flat_in.astype(f32)
     grad_out = grad_low.astype(f32)
     middle = start + mixer_out
     routed = rms_scale(middle, gain_mid).astype(b16)
-    all_routed = plane_gather(routed, 3)
-
-    mine = at * local + jnp.arange(local, dtype=jnp.int32)
-    marks = jnp.any(all_routes[:, :, None] == mine, axis=1).reshape(seqs, LEN, local)
+    whole = [
+        lax.all_gather(banks[e], "dp", axis=0, tiled=True, axis_index_groups=ends)
+        for e in range(taken)
+    ]
+    if sets == 2:
+        routed, whole[0] = tie(routed, whole[0])
+    (all_routed,) = plane_gather(3, routed, sets=sets)
+
+    lowest = at * local + (place % sets) * taken
+    mine = lowest + jnp.arange(taken, dtype=jnp.int32)
+    marks = jnp.any(all_routes[:, :, None] == mine, axis=1).reshape(seqs, LEN, taken)
     earlier = jnp.arange(LEN)[:, None] > jnp.arange(LEN)[None, :]
     rank = jnp.einsum(
         "ts,nse->net", earlier.astype(b16), marks.astype(b16), preferred_element_type=f32
@@ -735,103 +1126,143 @@
     chosen = (rank[:, :, None, :] == places[None, None, :, None]) & (
         marks.transpose(0, 2, 1)[:, :, None, :]
     )
-    select = chosen.astype(b16).reshape(seqs, local * slots, LEN)
+    select = chosen.astype(b16)
     gates_all = dense_gates(dot(all_routed, route_proj), all_routes)
-    gates_mine = lax.dynamic_slice_in_dim(gates_all, at * local, local, axis=1)
-    gates_mine = gates_mine.reshape(seqs, LEN, local).transpose(0, 2, 1)
+    gates_mine = lax.dynamic_slice_in_dim(gates_all, lowest, taken, axis=1)
+    gates_mine = gates_mine.reshape(seqs, LEN, taken).transpose(0, 2, 1)
     slot_gates = jnp.sum(jnp.where(chosen, gates_mine[:, :, None, :], 0.0), axis=-1)
 
-    def spread(rows):
-        return jnp.einsum(
-            "nrt,ntd->nrd", select, rows.reshape(seqs, LEN, -1), preferred_element_type=f32
-        ).reshape(seqs, local, slots, -1)
-
-    rows_in = spread(all_routed).astype(b16)
-    rows_grad = spread(all_grad)
-    outs, backs, dgates, bank_grads = [], [], [], []
-    for e in range(local):
-        gu_w = gather(jnp.concatenate([expert_gate[e], expert_up[e]], axis=1), "dp")
-        e_down = gather(expert_down[e], "dp")
-        x = rows_in[:, e].reshape(seqs * slots, -1)
+    select = select.reshape(seqs, taken * slots, LEN)
+    rows_in = spread(select, all_routed, taken)
+    rows_grad = spread(select, all_grad, taken)
+    outs, backs, dgates, sums = [], [], [], []
+    tied = []
+    made_grads = []
+
+    def weight_grads(x, depre, ehid, dmade):
+        made_grads[:] = [dot_tn(x, depre).astype(b16), dot_tn(ehid, dmade).astype(b16)]
+        sums.append(
+            [
+                lax.psum_scatter(
+                    v, "dp", scatter_dimension=0, tiled=True, axis_index_groups=ends
+                )
+                for v in made_grads
+            ]
+        )
+
+    for e in range(taken):
+        bank = whole[e]
+        x, dy = rows_in[e], rows_grad[e]
+        x, bank, *tied = tie(x, bank, *tied)
+        gu_w = bank[:, : 2 * ehidden]
+        e_down = bank[:, 2 * ehidden :].reshape(planes, 3, part, third)
+        e_down = e_down.transpose(0, 2, 1, 3).reshape(ehidden, width)
         g = slot_gates[:, e].reshape(seqs * slots, 1)
-        dy = rows_grad[:, e].reshape(seqs * slots, -1)
-        pre = dot(x, gu_w)
-        soft, slope = silu_parts(pre[:, :ehidden])
-        lin = pre[:, ehidden:]
-        hid = (soft * lin).astype(b16)
-        made = dot(hid, e_down).astype(b16).astype(f32)
+        epre = dot(x, gu_w)
+        esoft, eslope = silu_parts(epre[:, :ehidden])
+        elin = epre[:, ehidden:]
+        ehid = (esoft * elin).astype(b16)
+        made = dot(ehid, e_down).astype(b16).astype(f32)
+        dy = dy.astype(f32)
         dgates.append(jnp.sum(made * dy, axis=1).reshape(seqs, slots))
-        outs.append((made * g).astype(b16).reshape(seqs, slots, -1))
+        outs.append((made * g).astype(b16))
         dmade = (dy * g).astype(b16)
-        dhid = dot_nt(dmade, e_down)
-        dpre = jnp.concatenate([dhid * lin * slope, dhid * soft], axis=1).astype(b16)
-        backs.append(dot_nt(dpre, gu_w).astype(b16).reshape(seqs, slots, -1))
-        bank_grads.append(
-            (
-                scatter(dot_tn(x, dpre).astype(b16), "dp").astype(f32),
-                scatter(dot_tn(hid, dmade).astype(b16), "dp").astype(f32),
-            )
-        )
-    combine = lambda parts: jnp.einsum(
-        "nrt,nrd->ntd", select, jnp.concatenate(parts, axis=1), preferred_element_type=f32
-    ).reshape(count, -1)
+        dehid = dot_nt(dmade, e_down)
+        depre = jnp.concatenate([dehid * elin * eslope, dehid * esoft], axis=1).astype(b16)
+        backs.append(dot_nt(depre, gu_w).astype(b16))
+        weight_grads(x, depre, ehid, dmade)
+        tied = tied + made_grads
+        if e == 0:
+            tied = list(tie(all_routed, *tied))
+            near_routed, near_grad = tied[0][:near], all_grad[:near]
+            pre = dot(near_routed, gate_up)
+            soft, slope = silu_parts(pre[:, :fs])
+            lin = pre[:, fs:]
+            hid = (soft * lin).astype(b16)
+            dhid = dot_nt(near_grad, down_w)
+            dpre = jnp.concatenate([dhid * lin * slope, dhid * soft], axis=1).astype(b16)
+            shared_grad = dot_tn(near_routed, dpre).astype(b16)
+            down_grad = dot_tn(hid, near_grad).astype(b16)
+            tied = [shared_grad, down_grad, hid, dpre] + tied[1:]
+    shared_grad, down_grad, hid, dpre = tied[:4]
     dgate_rows = jnp.sum(
         jnp.where(chosen, jnp.stack(dgates, axis=1)[:, :, :, None], 0.0), axis=2
     ).transpose(0, 2, 1)
     dgate_wide = lax.dynamic_update_slice_in_dim(
-        jnp.zeros((count, experts), f32), dgate_rows.reshape(count, local), at * local, axis=1
+        jnp.zeros((count, experts), f32), dgate_rows.reshape(count, taken), lowest, axis=1
     )
     high = dgate_wide.astype(b16)
     fine = (dgate_wide - high.astype(f32)).astype(b16)
     fill = jnp.zeros((count, -(2 * experts) % LANES), b16)
-
-    pre = dot(all_routed, gate_up)
-    soft, slope = silu_parts(pre[:, :fs])
-    lin = pre[:, fs:]
-    hid = (soft * lin).astype(b16)
-    dhid = dot_nt(all_grad, down_w)
-    dpre = jnp.concatenate([dhid * lin * slope, dhid * soft], axis=1).astype(b16)
-    shared_out = dot(hid, down_w)
-    shared_back = dot_nt(dpre, gate_up)
-
-    payload = [(combine(backs) + shared_back).astype(b16), high, fine, fill]
-    back = plane_scatter(jnp.concatenate(payload, axis=1), 4)
-    out_sum = plane_scatter((combine(outs) + shared_out).astype(b16), 5)
+    back_part = merge(select, backs, dpre, gate_up.T)
+    back, back_gates = plane_scatter(
+        4, back_part, jnp.concatenate([high, fine, fill], axis=1), sets=sets, after=made_grads
+    )
 
     gates = dense_gates(dot(routed, route_proj), routes.reshape(tokens, picks))
-    dgate = back[:, width : width + experts] + back[:, width + experts : width + 2 * experts]
+    dgate = back_gates[:, :experts] + back_gates[:, experts : 2 * experts]
     dlogits = (gates * (dgate - jnp.sum(gates * dgate, axis=1, keepdims=True))).astype(b16)
-    droute = back[:, :width] + dot_nt(dlogits, route_proj)
+    droute = back + dot_nt(dlogits, route_proj)
     dmid_part, mid_gain_grad = rms_back(middle, gain_mid, droute)
     dmid = grad_out + dmid_part
+
+    def small_rows(weight_grad, bias_grad, skip_grad, head_grad):
+        spot = lambda v, size: heads.ungroup(
+            lax.dynamic_update_slice_in_dim(
+                jnp.zeros(v.shape[:-1] + (plane, v.shape[-1]), f32), v[..., None, :], at, v.ndim - 1
+            ),
+            size,
+        )
+        taps = jnp.concatenate([weight_grad, bias_grad], axis=0)
+        taps = jnp.concatenate([spot(taps[:, :wide], size), taps[:, wide:]], axis=1)
+        skip_grad = jnp.sum(skip_grad.reshape(heads.padded, size), axis=1)
+        head_rows = jnp.concatenate([head_grad[:2, : heads.padded], skip_grad[None]], axis=0)
+        head_rows = spot(head_rows, 1).reshape(1, -1)
+        head_rows = jnp.pad(head_rows, ((0, 0), (0, taps.shape[1] - head_rows.shape[1])))
+        rows = jnp.concatenate([taps, head_rows], axis=0)
+        return jnp.pad(rows, ((0, 16 - rows.shape[0]), (0, 0)))
+
+    def owners(grad):
+        grad = scatter(grad.astype(b16), "dp").reshape(plane, shard, -1)
+        return lax.all_to_all(grad, "expert", split_axis=0, concat_axis=0, tiled=True).astype(f32)
 
     scaled = (dmid * scale).astype(b16)
     inward = scale * jnp.sum(scaled.astype(f32) * mixer_out, axis=1, keepdims=True) / inner
     inward_high = inward.astype(b16)
     inward_low = (inward - inward_high.astype(f32)).astype(b16)
     tail = jnp.where(lane == 0, inward_high, jnp.where(lane == 1, inward_low, 0)).astype(b16)
-    spread_mid = plane_gather(jnp.concatenate([scaled, tail], axis=1), 6)
-    all_mid = spread_mid[:, :width]
-    all_inward = spread_mid[:, width : width + 1].astype(f32) + spread_mid[
-        :, width + 1 : width + 2
-    ].astype(f32)
+    shared_rows = owners(shared_grad)
+    all_mid, all_inward = plane_gather(6, scaled, tail, after=sums[0])
+    kept, sent = [], []
+    if sets == 2:
+        for group in sums:
+            for v in group:
+                rows = v.shape[0] // 2
+                kept.append(jnp.where(odd, v[rows:], v[:rows]))
+                sent.append(jnp.where(odd, v[:rows], v[rows:]))
+    swapped = [exchange(v, "dp", 1) for v in sent]
+    all_inward = all_inward[:, :1].astype(f32) + all_inward[:, 1:2].astype(f32)
     dmerged, weight_grad, bias_grad, skip_grad, head_grad = mix_backward(
         merged, joined, dot_nt(all_mid, out_w), all_inward, params
     )
-    dnormed = plane_scatter(dot_nt(dmerged, in_w).astype(b16), 7)
-    dstart, unused = rms_back(start, gain_in, dnormed)
-
-    def owners(grad):
-        grad = scatter(grad.astype(b16), "dp")
-        grad = grad.reshape(plane, shard, -1)
-        return lax.all_to_all(grad, "expert", split_axis=0, concat_axis=0, tiled=True).astype(f32)
-
-    shared_grad = owners(dot_tn(all_routed, dpre))
+    taps_of = small_rows(weight_grad, bias_grad, skip_grad, head_grad)
+    dnormed, taps_of = plane_scatter(
+        7,
+        dot_nt(dmerged, in_w).astype(b16),
+        gathers=[taps_of],
+        after=[shared_rows] + swapped,
+    )
+    taps_of = jnp.sum(taps_of, axis=0)
+    out_part = merge(select, outs, hid, down_w, after=[dmerged])
+    out_part, dnormed = tie(out_part, dnormed)
+    out_sum, small = plane_scatter(5, out_part, sets=sets, lines=[taps_of])
+    small = jnp.sum(small, axis=0)
+
+    shared_grad = shared_rows
     unsplit = lambda v: (
         v.reshape(plane, shard, planes, hr).transpose(1, 2, 0, 3).reshape(shard, planes * plane * hr)
     )
     out_w_grad = dot_tn(mixed, all_mid).astype(b16)
-    down_grad = dot_tn(hid, all_grad).astype(b16)
     if heads.owned:
         parts = out_w_grad.reshape(half, 2, out_rows, width)
         keep = jnp.where(low, parts[:, 0], parts[:, 1])
@@ -874,20 +1305,19 @@
     gain_in_grad = jnp.sum(in_proj.astype(f32) * in_grad, axis=1) / norm_in.astype(f32)
     gain_mix_grad = jnp.sum(out_proj.astype(f32) * out_w_grad, axis=1) / mixer_gain.astype(f32)
 
-    place = lambda v, size: heads.ungroup(
-        lax.dynamic_update_slice_in_dim(
-            jnp.zeros(v.shape[:-1] + (plane, v.shape[-1]), f32), v[..., None, :], at, v.ndim - 1
-        ),
-        size,
-    )
-    taps = jnp.concatenate([weight_grad, bias_grad], axis=0)
-    taps = jnp.concatenate([place(taps[:, :wide], size), taps[:, wide:]], axis=1)
-    skip_grad = jnp.sum(skip_grad.reshape(heads.padded, size), axis=1)
-    head_rows = jnp.concatenate([head_grad[:2, : heads.padded], skip_grad[None]], axis=0)
-    head_rows = place(head_rows, 1).reshape(1, -1)
-    head_rows = jnp.pad(head_rows, ((0, 0), (0, taps.shape[1] - head_rows.shape[1])))
-    small = total_of(jnp.concatenate([taps, head_rows], axis=0), ("dp", "expert"))
-
+    bank_grads = []
+    for e in range(taken):
+        if sets == 1:
+            bank_grads.append([v.astype(f32) for v in sums[e]])
+            continue
+        pair = [
+            (jnp.where(odd, came, keep), jnp.where(odd, keep, came))
+            for keep, came in zip(kept[2 * e : 2 * e + 2], swapped[2 * e : 2 * e + 2])
+        ]
+        bank_grads.append([v.astype(f32) for v, _ in pair])
+        bank_grads.append([v.astype(f32) for _, v in pair])
+    bank_grads = bank_grads[::2] + bank_grads[1::2] if sets == 2 else bank_grads
+    dstart, unused = rms_back(start, gain_in, dnormed)
     shape = block_input.shape
     return (
         (middle + out_sum).astype(b16).reshape(shape),
@@ -906,9 +1336,9 @@
         unsplit(shared_grad[:, :, :fs].transpose(0, 1, 2)),
         unsplit(shared_grad[:, :, fs:]),
         down_grad,
-        jnp.stack([a[:, :ehidden] for a, _ in bank_grads]),
-        jnp.stack([a[:, ehidden:] for a, _ in bank_grads]),
-        jnp.stack([b for _, b in bank_grads]),
+        jnp.stack([v[:, :ehidden] for v, _ in bank_grads]),
+        jnp.stack([v[:, ehidden:] for v, _ in bank_grads]),
+        jnp.stack([v for _, v in bank_grads]),
     )
 
 

time: 1140 us -> 988 us (0.87)
  waiting for transfers between devices: 348 us -> 54.2 us
  Pallas kernels: 296 us -> 548 us
  matrix products: 223 us -> 152 us
  other arithmetic: 93.9 us -> 69.8 us
  local copies, waits for them, and re-layouts: 117 us -> 104 us
    pallas_call x8 -> x12, Pallas kernels: 263 us -> 516 us  [the longest x3 239 us: plane_gather(): pl.pallas_call(partial(gather_kernel, sets, count, len(swaps), len(lines)...]
    all_gather x10 -> x2, waiting for transfers between devices: 199 us -> 0.04 us  [body(): gather = lambda v, axes: lax.all_gather(v, axes, axis=0, tiled=True)]
    reduce_scatter x11 -> x3, waiting for transfers between devices: 139 us -> 0.01 us  [body(): lax.psum_scatter(v, axes, scatter_dimension=0, tiled=True)]
    ppermute x7 -> x6, waiting for transfers between devices: 3.02 us -> 36.9 us  [exchange(): return lax.ppermute(value, axis, [(i, i ^ distance) for i in range(size)])]
    dot_general x4 -> x0, matrix products: 27.9 us -> none  [the longest x2 15.9 us: spread(): jnp.einsum('nrt,ntd->nrd', select, rows.reshape(seqs, LEN, -1), preferred...]
    dot_general x14 -> x9, matrix products: 77.3 us -> 51.9 us  [dot(): return jnp.dot(a, b, preferred_element_type=f32)]
    concatenate x9 -> x3, other arithmetic: 22.9 us -> 3.15 us  [the longest x1 3.01 us: body(): jnp.concatenate([high, fine, fill], axis=1)]
    concatenate x3 -> x1, local copies, waits for them, and re-layouts: 19.6 us -> 0.08 us  [body(): jnp.concatenate([high, fine, fill], axis=1)]
  transfers between devices with their start and end apart: 30 -> 19, of which waited for: 12 -> 5; matrix products, arithmetic and copies ran while one was open for 35% -> 28% of each run, Pallas kernels for 26% -> 56%
where the time goes in v2:
time: 988 us; the launch traced here: 979 us
  Pallas kernels  548 us (55%)
  matrix products  152 us (15%)
  local copies, waits for them, and re-layouts  104 us (11%)
  other arithmetic  69.8 us (7%)
  waiting for transfers between devices  54.2 us (5%)
  blocking collectives  20.7 us (2%)
  between operations  16.8 us (2%)
  starting transfers between devices  13.5 us (1%)
    pallas_call x3, Pallas kernels, plane_gather(): pl.pallas_call(partial(gather_kernel, sets, count, len(swaps), len(lines)...  239 us
    pallas_call x4, Pallas kernels, plane_scatter(): pl.pallas_call(partial(scatter_kernel, sets, count, len(swaps), len(gathe...  219 us
    dot_general x8, matrix products, dot_nt(): return lax.dot_general(a, b, NT, preferred_element_type=f32)  52.6 us
    dot_general x9, matrix products, dot(): return jnp.dot(a, b, preferred_element_type=f32)  51.9 us
    unnamed x268, local copies, waits for them, and re-layouts  48.6 us
    dot_general x9, matrix products, dot_tn(): lax.dot_general(a, b, (((0,), (0,)), ((), ())), preferred_element_type=f32)  47.2 us
    pallas_call x2, Pallas kernels, merge(): pl.pallas_call(partial(merge_kernel, near, len(parts)), grid=(seqs,), in_...  38.9 us
    ppermute x6, waiting for transfers between devices, exchange(): return lax.ppermute(value, axis, [(i, i ^ distance) for i in range(size)])  36.9 us
  transfers between devices with their start and end apart: 19, of which 5 were waited for; matrix products, arithmetic and copies ran while one was open for 28% of the time, Pallas kernels for 56%

profile of v2, /device:TPU:0, one launch (start us, length us, event | category | flops | bytes accessed | tf_op | source)
XLA Modules:
  0.0 979.3 jit_solution(17271444251555414317)
XLA Ops:
  17.2 20.7 %all_to_all.15 = bf16[8,48,1408]{2,1,0:T(8,128)(2,1)S(1)} all-to-all(bf16[8,48,1408]{2,1,0:T(8,128)(2,1)S(1)} %bitcast.350), channel_id=1, replica_groups=mesh['dp'=4,'expert'=8] {'expert'}, dimensions={0} | all-to-all | bytes 2162688 | tf_op jit(solution)/shard_map/all_to_all | solution.py:1011
  40.3 5.0 shard_map.339
  49.5 142.7 %shard_map.340 = (bf16[8,256,1536]{2,1,0:T(8,128)(2,1)}, bf16[16,256,1536]{2,1,0:T(8,128)(2,1)}, bf16[16,256,128]{2,1,0:T(8,128)(2,1)}, bf16[384,1536]{1,0:T(8,128)(2,1)}, bf16[384,1536]{1,0:T(8,128)(2,1)}) custom-call(bf16[256,1536]{1,0:T(8,128)(2,1)} %bitcast.337, bf16[256,1536]{1,0:T(8,128)(2,1)} %bitcast.341, bf16[256,128]{1,0:T(8,128)(2,1)} %pad.29.refs_2_, ...), custom_call_target="tpu_custom_call" | custom-call | bytes 1024 | tf_op jit(solution)/shard_map/pallas_call | solution.py:464
  201.1 5.0 multiply_reduce_fusion
  208.2 5.9 slice.288
  215.8 4.8 copy-done.3
  220.6 6.9 shard_map.345
  234.1 4.4 fusion.1
  238.6 8.5 fusion.16.merged_ref
  247.1 10.9 %shard_map.341 = (bf16[2048,384]{1,0:T(8,128)(2,1)S(1)}, f32[2048,384]{1,0:T(8,128)S(1)}, f32[2048,128]{1,0:T(8,128)S(1)}) custom-call(f32[2048,1152]{1,0:T(8,128)S(1)} %fusion.16.merged_ref, f32[4,640]{1,0:T(4,128)S(1)} %maximum_convert_fusion.1.weight_ref, f32[1,640]{1,0:T(1,128)S(1)} %maximum_convert_fusion.2.bias_ref, ...), custom_call_target="tpu_custom_call" | custom-call | bytes 1024 | tf_op jit(solution)/shard_map/pallas_call | solution.py:243
  261.2 5.2 convolution_convert_fusion.5
  267.0 34.5 %shard_map.342 = (f32[256,1536]{1,0:T(8,128)S(1)}, f32[256,128]{1,0:T(8,128)S(1)}) custom-call(bf16[8,256,1536]{2,1,0:T(8,128)(2,1)S(1)} %bitcast.321, bf16[8,256,128]{2,1,0:T(8,128)(2,1)S(1)} %select_select_fusion.refs_1_), custom_call_target="tpu_custom_call" | custom-call | bytes 1024 | tf_op jit(solution)/shard_map/pallas_call | solution.py:729
  308.5 63.9 %shard_map.343 = bf16[16,256,1536]{2,1,0:T(8,128)(2,1)} custom-call(bf16[256,1536]{1,0:T(8,128)(2,1)} %multiply_convert_fusion.7.refs_0_), custom_call_target="tpu_custom_call" | custom-call | bytes 1024 | tf_op jit(solution)/shard_map/pallas_call | solution.py:464
  372.4 4.6 copy-done
  377.0 6.9 shard_map.344
  384.0 4.8 select_reduce_fusion.2
  392.8 8.0 fusion.22
  403.5 4.6 multiply_convert_fusion.4
  408.2 5.2 fusion.3
  413.4 3.4 convolution_convert_fusion.9
  416.8 8.5 convolution_convert_fusion.7
  425.3 4.8 fusion.12
  430.1 4.8 multiply_convert_fusion.10
  451.3 8.0 fusion.19
  459.3 4.7 multiply_convert_fusion.1
  464.1 5.7 fusion.7
  470.5 5.9 convolution_convert_fusion.8.refs_3_
  478.8 9.0 convolution_convert_fusion.1
  487.8 8.0 convolution_convert_fusion
  495.9 6.7 convolution_convert_fusion.6.refs_2_
  508.9 17.6 %shard_map.346 = bf16[4096,1536]{1,0:T(8,128)(2,1)S(1)} custom-call(bf16[32,80,128]{2,1,0:T(8,128)(2,1)S(1)} %fusion.48.select_ref, bf16[32,40,1536]{2,1,0:T(8,128)(2,1)S(1)} %bitcast.324, bf16[32,40,1536]{2,1,0:T(8,128)(2,1)S(1)} %bitcast.325, bf16[2048,256]{1,0:T(8,128)(2,1)S(1)} %pad_maximum_fusion.12.refs_2_, ...), custom_call_target="tpu_custom_call" | custom-call | bytes 1024 | tf_op jit(solution)/shard_map/pallas_call | solution.py:837
  526.6 4.6 copy-done.1
  531.2 80.6 %shard_map.347 = (f32[256,1536]{1,0:T(8,128)}, f32[256,128]{1,0:T(8,128)}) custom-call(bf16[16,256,1536]{2,1,0:T(8,128)(2,1)} %bitcast.314, bf16[16,256,128]{2,1,0:T(8,128)(2,1)} %bitcast.352, bf16[1536,1024]{1,0:T(8,128)(2,1)} %convolution_convert_fusion.6.refs_2_, bf16[512,1536]{1,0:T(8,128)(2,1)} %convolution_convert_fusion.8.refs_3_), custom_call_target="tpu_custom_call" | custom-call | bytes 1024 | tf_op jit(solution)/shard_map/pallas_call | solution.py:729
  625.2 5.3 all-to-all-done.1
  639.3 32.9 %shard_map.348 = (bf16[8,256,1536]{2,1,0:T(8,128)(2,1)}, bf16[8,256,128]{2,1,0:T(8,128)(2,1)}) custom-call(bf16[256,1536]{1,0:T(8,128)(2,1)} %get-tuple-element.190.refs_0_, bf16[256,128]{1,0:T(8,128)(2,1)} %select_select_fusion.1.refs_1_, bf16[768,1024]{1,0:T(8,128)(2,1)} %reduce-scatter.10.cloned.1.call-done.refs_2_, ...), custom_call_target="tpu_custom_call" | custom-call | bytes 1024 | tf_op jit(solution)/shard_map/pallas_call | solution.py:464
  673.7 5.7 fusion.52.grad_ref
  679.9 21.5 %shard_map.349 = (bf16[2048,1152]{1,0:T(8,128)(2,1)S(1)}, f32[4,640]{1,0:T(4,128)S(1)}, f32[1,640]{1,0:T(1,128)S(1)}, f32[1,384]{1,0:T(1,128)S(1)}, f32[8,128]{1,0:T(8,128)S(1)}) custom-call(f32[2048,1152]{1,0:T(8,128)S(1)} %bitcast.316, f32[2048,384]{1,0:T(8,128)S(1)} %copy-done.22, f32[2048,384]{1,0:T(8,128)S(1)} %fusion.52.grad_ref, ...), custom_call_target="tpu_custom_call" | custom-call | bytes 1024 | tf_op jit(solution)/shard_map/pallas_call | solution.py:263
  701.4 12.0 %fusion.92 = f32[1536,1152]{0,1:T(8,128)S(1)} fusion(bf16[2048,1536]{1,0:T(8,128)(2,1)} %copy-done.65, bf16[2048,1152]{1,0:T(8,128)(2,1)S(1)} %get-tuple-element.90.refs_4_), kind=kOutput, calls=%fused_computation.266 | convolution fusion | flops 7247757312 | bytes 18087936 | tf_op jit(solution)/shard_map/dot_general | solution.py:774
  716.3 5.8 copy.370
  724.0 24.9 %collective-permute-done.4.refs_6_ = bf16[128,1536]{1,0:T(8,128)(2,1)S(1)} collective-permute-done((bf16[128,1536]{1,0:T(8,128)(2,1)S(1)}, bf16[128,1536]{1,0:T(8,128)(2,1)S(1)}, u32[]{:S(2)}, u32[]{:S(2)}) %collective-permute-start.4) | collective-permute-done | bytes 393248 | tf_op jit(solution)/shard_map/ppermute | solution.py:797
  756.7 5.9 convolution_convert_fusion.10
  764.5 13.3 %convolution_convert_fusion.2 = bf16[2048,1536]{1,0:T(8,128)(2,1)} fusion(bf16[2048,1152]{1,0:T(8,128)(2,1)} %copy-done.10, bf16[1536,1408]{0,1:T(8,128)(2,1)} %all-gather.5.cloned.1.call-done), kind=kOutput, calls=%fused_computation.22 | convolution fusion | flops 7250903040 | bytes 14548992 | tf_op jit(solution)/shard_map/dot_general | solution.py:770
  785.4 21.3 %shard_map.350 = bf16[4096,1536]{1,0:T(8,128)(2,1)} custom-call(bf16[32,80,128]{2,1,0:T(8,128)(2,1)S(1)} %copy-done.5, bf16[32,40,1536]{2,1,0:T(8,128)(2,1)S(1)} %bitcast.322, bf16[32,40,1536]{2,1,0:T(8,128)(2,1)S(1)} %bitcast.323, bf16[2048,128]{1,0:T(8,128)(2,1)S(1)} %copy-done.26, bf16[128,1536]{1,0:T(8,128)(2,1)S(1)} %bitcast.327, ...), custom_call_target="tpu_custom_call" | custom-call | bytes 1024 | tf_op jit(solution)/shard_map/pallas_call | solution.py:837
  813.7 11.9 %collective-permute-done.3.refs_5_ = bf16[384,1024]{1,0:T(8,128)(2,1)S(1)} collective-permute-done((bf16[384,1024]{1,0:T(8,128)(2,1)}, bf16[384,1024]{1,0:T(8,128)(2,1)S(1)}, u32[]{:S(2)}, u32[]{:S(2)}) %collective-permute-start.3) | collective-permute-done | bytes 786464 | tf_op jit(solution)/shard_map/ppermute | solution.py:797
  825.7 35.8 %shard_map.351 = (f32[256,1536]{1,0:T(8,128)S(1)}, f32[8,16,3328]{2,1,0:T(8,128)S(1)}) custom-call(bf16[8,256,1536]{2,1,0:T(8,128)(2,1)S(1)} %bitcast.320, f32[16,3328]{1,0:T(8,128)S(1)} %pad.35.refs_1_, f32[8,48,256]{2,1,0:T(8,128)S(1)} %convert_element_type.385.refs_2_, bf16[384,1024]{1,0:T(8,128)(2,1)} %collective-permute-done.1.refs_3_, ...), custom_call_target="tpu_custom_call" | custom-call | bytes 1024 | tf_op jit(solution)/shard_map/pallas_call | solution.py:729
  866.1 67.7 %shard_map.352 = (f32[256,1536]{1,0:T(8,128)}, f32[4,16,3328]{2,1,0:T(8,128)}) custom-call(bf16[16,256,1536]{2,1,0:T(8,128)(2,1)} %bitcast.332, f32[16,3328]{1,0:T(8,128)} %reduce_sum.228.refs_1_), custom_call_target="tpu_custom_call" | custom-call | bytes 1024 | tf_op jit(solution)/shard_map/pallas_call | solution.py:729
  947.5 3.7 all-to-all-start.2
  956.5 8.3 all-to-all-done.2
  (543 shorter events, 161.9 us)
Async XLA Ops:
  7.2 199.2 %all-gather.7.cloned.1.call-start = ((), (), s32[]{:S(2)}) async-start(), calls=%async_computation.11 | async-start | bytes 2129920 | tf_op jit(solution)/shard_map/all_gather | solution.py:983
  10.0 222.7 %all-gather.5.cloned.1.call-start = ((), (), s32[]{:S(2)}) async-start(), calls=%async_computation.10 | async-start | bytes 5406720 | tf_op jit(solution)/shard_map/all_gather | solution.py:983
  17.2 22.2 %copy-start.107 = (s32[2,128,6]{1,0,2:T(2,128)S(1)}, s32[2,128,6]{1,0,2:T(2,128)}, u32[]{:S(2)}) copy-start(s32[2,128,6]{1,0,2:T(2,128)} %param.22) | copy-start | bytes 18436
  39.3 269.2 %all-gather.9.cloned.1.call-start = ((), (), s32[]{:S(2)}) async-start(), calls=%async_computation.12 | async-start | bytes 7077888 | tf_op jit(solution)/shard_map/all_gather | solution.py:1111
  195.1 246.6 %all-gather.11.cloned.1.call-start = ((), (), s32[]{:S(2)}) async-start(), calls=%async_computation.13 | async-start | bytes 7077888 | tf_op jit(solution)/shard_map/all_gather | solution.py:1111
  196.6 50.4 %copy-start.42 = (f32[1,128]{1,0:T(1,128)}, f32[1,128]{1,0:T(1,128)S(1)}, u32[]{:S(2)}) copy-start(f32[1,128]{1,0:T(1,128)S(1)} %bitcast_convert_fusion.1.step_ref) | copy-start | bytes 1540
  196.6 50.4 %copy-start.44 = (f32[1,128]{1,0:T(1,128)}, f32[1,128]{1,0:T(1,128)S(1)}, u32[]{:S(2)}) copy-start(f32[1,128]{1,0:T(1,128)S(1)} %bitcast_convert_fusion.rate_ref) | copy-start | bytes 1540
  196.7 50.4 %copy-start.38 = (f32[1,384]{1,0:T(1,128)}, f32[1,384]{1,0:T(1,128)S(1)}, u32[]{:S(2)}) copy-start(f32[1,384]{1,0:T(1,128)S(1)} %fusion.80.skip_ref) | copy-start | bytes 4612
  196.7 50.3 %copy-start.36 = (f32[1,640]{1,0:T(1,128)}, f32[1,640]{1,0:T(1,128)S(1)}, u32[]{:S(2)}) copy-start(f32[1,640]{1,0:T(1,128)S(1)} %maximum_convert_fusion.2.bias_ref) | copy-start | bytes 7684
  196.8 50.3 %copy-start.34 = (f32[4,640]{1,0:T(4,128)}, f32[4,640]{1,0:T(4,128)S(1)}, u32[]{:S(2)}) copy-start(f32[4,640]{1,0:T(4,128)S(1)} %maximum_convert_fusion.1.weight_ref) | copy-start | bytes 30724
  207.9 23.1 %collective-permute-start = (bf16[2,96,1664]{2,1,0:T(8,128)(2,1)S(1)}, bf16[2,96,1664]{2,1,0:T(8,128)(2,1)S(1)}, u32[]{:S(2)}, u32[]{:S(2)}) collective-permute-start(bf16[2,96,1664]{2,1,0:T(8,128)(2,1)S(1)} %broadcast_select_fusion.4), channel_id=1, source_target_pairs={{0,1},{1,0},{2,3},{3,2},{4,5},{5,4},{6,7},{7,6},{8,9},{9,8},{10,11... | collective-permute-start | bytes 1916936 | tf_op jit(solution)/shard_map/ppermute | solution.py:797
  215.2 405.8 %reduce-scatter.14.cloned.1.call-start = ((), (), s32[]{:S(2)}) async-start(), calls=%async_computation.16 | async-start | bytes 983040 | tf_op jit(solution)/shard_map/reduce_scatter | solution.py:984
  215.8 291.0 %copy-start.4 = (bf16[32,80,128]{2,1,0:T(8,128)(2,1)}, bf16[32,80,128]{2,1,0:T(8,128)(2,1)S(1)}, u32[]{:S(2)}) copy-start(bf16[32,80,128]{2,1,0:T(8,128)(2,1)S(1)} %fusion.48.select_ref) | copy-start | bytes 1966084
  220.6 10.3 %copy-start.67 = (bf16[512,1664]{1,0:T(8,128)(2,1)S(1)}, bf16[512,1664]{1,0:T(8,128)(2,1)}, u32[]{:S(2)}) copy-start(bf16[512,1664]{1,0:T(8,128)(2,1)} %all-gather.7.cloned.1.call-done) | copy-start | bytes 5111812
  231.0 199.1 %copy-start.32 = (bf16[4,32,1536]{2,1,0:T(8,128)(2,1)}, bf16[4,32,1536]{2,1,0:T(8,128)(2,1)S(1)}, u32[]{:S(2)}) copy-start(bf16[4,32,1536]{2,1,0:T(8,128)(2,1)S(1)} %slice.360) | copy-start | bytes 1179652
  232.6 14.5 %copy-start.40 = (f32[1,384]{1,0:T(1,128)}, f32[1,384]{1,0:T(1,128)S(1)}, u32[]{:S(2)}) copy-start(f32[1,384]{1,0:T(1,128)S(1)} %reshape.586.gain_ref) | copy-start | bytes 4612
  247.1 10.9 %copy-start.2 = (f32[2048,1152]{1,0:T(8,128)}, f32[2048,1152]{1,0:T(8,128)S(1)}, u32[]{:S(2)}) copy-start(f32[2048,1152]{1,0:T(8,128)S(1)} %fusion.16.merged_ref) | copy-start | bytes 28311556
  267.0 36.0 %copy-start.59 = (bf16[2,128,1536]{2,1,0:T(8,128)(2,1)S(1)}, bf16[2,128,1536]{2,1,0:T(8,128)(2,1)}, u32[]{:S(2)}) copy-start(bf16[2,128,1536]{2,1,0:T(8,128)(2,1)} %param.20) | copy-start | bytes 2359300
  304.0 68.4 %copy-start.97 = (f32[256]{0:T(256)}, f32[256]{0:T(256)S(1)}, u32[]{:S(2)}) copy-start(f32[256]{0:T(256)S(1)} %add_rsqrt_fusion.1) | copy-start | bytes 3076
  441.7 192.9 %reduce-scatter.12.cloned.1.call-start = ((), (), s32[]{:S(2)}) async-start(), calls=%async_computation.15 | async-start | bytes 2359296 | tf_op jit(solution)/shard_map/reduce_scatter | solution.py:1146
  442.3 197.0 %reduce-scatter.10.cloned.1.call-start = ((), (), s32[]{:S(2)}) async-start(), calls=%async_computation.14 | async-start | bytes 4718592 | tf_op jit(solution)/shard_map/reduce_scatter | solution.py:1146
  443.0 279.4 %reduce-scatter.18.cloned.1.call-start = ((), (), s32[]{:S(2)}) async-start(), calls=%async_computation.18 | async-start | bytes 2359296 | tf_op jit(solution)/shard_map/reduce_scatter | solution.py:1146
  476.4 275.7 %reduce-scatter.16.cloned.1.call-start = ((), (), s32[]{:S(2)}) async-start(), calls=%async_computation.17 | async-start | bytes 4718592 | tf_op jit(solution)/shard_map/reduce_scatter | solution.py:1146
  478.8 9.0 copy-start.119
  478.8 9.0 copy-start.120
  621.0 9.6 all-to-all-start.1
  624.4 323.1 %reduce-scatter.22.cloned.1.call-start = ((), (), s32[]{:S(2)}) async-start(), calls=%async_computation.20 | async-start | bytes 4423680 | tf_op jit(solution)/shard_map/reduce_scatter | solution.py:984
  634.6 44.8 %slice-start.3 = ((s8[9437184]{0:T(1024)(128)(4,1)}), s8[1048576]{0:T(1024)(128)(4,1)S(1)}, s32[]{:S(2)}) async-start(s8[9437184]{0:T(1024)(128)(4,1)} %bitcast.315), calls=%async_computation.24 | async-start | bytes 2097152
  636.7 87.2 %collective-permute-start.2 = (bf16[128,1536]{1,0:T(8,128)(2,1)}, bf16[128,1536]{1,0:T(8,128)(2,1)S(1)}, u32[]{:S(2)}, u32[]{:S(2)}) collective-permute-start(bf16[128,1536]{1,0:T(8,128)(2,1)} %broadcast_select_fusion.11), channel_id=1, source_target_pairs={{0,8},{8,0},{16,24},{24,16},{1,9},{9,1},{17,25},{25,17},{2,10},{10... | collective-permute-start | bytes 1179656 | tf_op jit(solution)/shard_map/ppermute | solution.py:797
  639.3 34.3 %copy-start.81 = (bf16[2,2,96,1664]{3,2,1,0:T(8,128)(2,1)S(1)}, bf16[2,2,96,1664]{3,2,1,0:T(8,128)(2,1)}, u32[]{:S(2)}) copy-start(bf16[2,2,96,1664]{3,2,1,0:T(8,128)(2,1)} %copy-done.80) | copy-start | bytes 3833860
  701.4 12.0 %copy-start.10 = (bf16[2048,1152]{1,0:T(8,128)(2,1)}, bf16[2048,1152]{1,0:T(8,128)(2,1)S(1)}, u32[]{:S(2)}) copy-start(bf16[2048,1152]{1,0:T(8,128)(2,1)S(1)} %get-tuple-element.90.refs_4_) | copy-start | bytes 14155780
  722.1 230.3 %reduce-scatter.20.cloned.1.call-start = ((), (), s32[]{:S(2)}) async-start(), calls=%async_computation.19 | async-start | bytes 1966080 | tf_op jit(solution)/shard_map/reduce_scatter | solution.py:984
  722.4 26.5 %copy-start.71 = (bf16[256,1536]{1,0:T(8,128)(2,1)S(1)}, bf16[256,1536]{1,0:T(8,128)(2,1)}, u32[]{:S(2)}) copy-start(bf16[256,1536]{1,0:T(8,128)(2,1)} %reduce-scatter.18.cloned.1.call-done) | copy-start | bytes 2359300
  723.6 25.3 %collective-permute-start.4 = (bf16[128,1536]{1,0:T(8,128)(2,1)S(1)}, bf16[128,1536]{1,0:T(8,128)(2,1)S(1)}, u32[]{:S(2)}, u32[]{:S(2)}) collective-permute-start(bf16[128,1536]{1,0:T(8,128)(2,1)S(1)} %broadcast_select_fusion.10), channel_id=1, source_target_pairs={{0,8},{8,0},{16,24},{24,16},{1,9},{9,1},{17,25},{25,17},{2,10},{10... | collective-permute-start | bytes 1179656 | tf_op jit(solution)/shard_map/ppermute | solution.py:797
  723.9 27.1 %copy-start.28 = (bf16[128,1536]{1,0:T(8,128)(2,1)}, bf16[128,1536]{1,0:T(8,128)(2,1)S(1)}, u32[]{:S(2)}) copy-start(bf16[128,1536]{1,0:T(8,128)(2,1)S(1)} %collective-permute-done.2.refs_4_) | copy-start | bytes 1179652
  752.1 57.2 %collective-permute-start.1 = (bf16[384,1024]{1,0:T(8,128)(2,1)}, bf16[384,1024]{1,0:T(8,128)(2,1)}, u32[]{:S(2)}, u32[]{:S(2)}) collective-permute-start(bf16[384,1024]{1,0:T(8,128)(2,1)} %broadcast_select_fusion.3), channel_id=1, source_target_pairs={{0,8},{8,0},{16,24},{24,16},{1,9},{9,1},{17,25},{25,17},{2,10},{10... | collective-permute-start | bytes 2359304 | tf_op jit(solution)/shard_map/ppermute | solution.py:797
  754.4 71.2 %collective-permute-start.3 = (bf16[384,1024]{1,0:T(8,128)(2,1)}, bf16[384,1024]{1,0:T(8,128)(2,1)S(1)}, u32[]{:S(2)}, u32[]{:S(2)}) collective-permute-start(bf16[384,1024]{1,0:T(8,128)(2,1)} %broadcast_select_fusion.2), channel_id=1, source_target_pairs={{0,8},{8,0},{16,24},{24,16},{1,9},{9,1},{17,25},{25,17},{2,10},{10... | collective-permute-start | bytes 2359304 | tf_op jit(solution)/shard_map/ppermute | solution.py:797
  764.5 14.3 %copy-start.5 = (bf16[32,80,128]{2,1,0:T(8,128)(2,1)S(1)}, bf16[32,80,128]{2,1,0:T(8,128)(2,1)}, u32[]{:S(2)}) copy-start(bf16[32,80,128]{2,1,0:T(8,128)(2,1)} %copy-done.4) | copy-start | bytes 1966084
  764.5 14.3 %copy-start.26 = (bf16[2048,128]{1,0:T(8,128)(2,1)S(1)}, bf16[2048,128]{1,0:T(8,128)(2,1)}, u32[]{:S(2)}) copy-start(bf16[2048,128]{1,0:T(8,128)(2,1)} %copy-done.25) | copy-start | bytes 1572868
  764.5 14.3 %copy-start.33 = (bf16[4,32,1536]{2,1,0:T(8,128)(2,1)S(1)}, bf16[4,32,1536]{2,1,0:T(8,128)(2,1)}, u32[]{:S(2)}) copy-start(bf16[4,32,1536]{2,1,0:T(8,128)(2,1)} %copy-done.32) | copy-start | bytes 1179652
  764.5 42.2 %collective-permute-start.5 = (bf16[2,96,1536]{2,1,0:T(8,128)(2,1)}, bf16[2,96,1536]{2,1,0:T(8,128)(2,1)}, u32[]{:S(2)}, u32[]{:S(2)}) collective-permute-start(bf16[2,96,1536]{2,1,0:T(8,128)(2,1)} %fusion.58), channel_id=1, source_target_pairs={{0,1},{1,0},{2,3},{3,2},{4,5},{5,4},{6,7},{7,6},{8,9},{9,8},{10,11... | collective-permute-start | bytes 1769480 | tf_op jit(solution)/shard_map/ppermute | solution.py:797
  785.4 21.3 %copy-start.69 = (bf16[384,1536]{1,0:T(8,128)(2,1)S(1)}, bf16[384,1536]{1,0:T(8,128)(2,1)}, u32[]{:S(2)}) copy-start(bf16[384,1536]{1,0:T(8,128)(2,1)} %copy-done.68) | copy-start | bytes 3538948
  807.9 17.7 %slice-start.6 = ((s8[6291456]{0:T(1024)(128)(4,1)}), s8[2097152]{0:T(1024)(128)(4,1)S(1)}, s32[]{:S(2)}) async-start(s8[6291456]{0:T(1024)(128)(4,1)} %bitcast.318), calls=%async_computation.27 | async-start | bytes 4194304
  809.3 16.4 %slice-start.7 = ((s8[6291456]{0:T(1024)(128)(4,1)}), s8[4194304]{0:T(1024)(128)(4,1)S(1)}, s32[]{:S(2)}) async-start(s8[6291456]{0:T(1024)(128)(4,1)} %bitcast.318), calls=%async_computation.28 | async-start | bytes 8388608
  812.4 13.3 %copy-start.29 = (bf16[128,1536]{1,0:T(8,128)(2,1)S(1)}, bf16[128,1536]{1,0:T(8,128)(2,1)}, u32[]{:S(2)}) copy-start(bf16[128,1536]{1,0:T(8,128)(2,1)} %copy-done.28) | copy-start | bytes 1179652
  812.4 13.3 %copy-start.31 = (bf16[128,1536]{1,0:T(8,128)(2,1)S(1)}, bf16[128,1536]{1,0:T(8,128)(2,1)}, u32[]{:S(2)}) copy-start(bf16[128,1536]{1,0:T(8,128)(2,1)} %copy-done.30) | copy-start | bytes 1179652
  825.7 35.8 %copy-start.23 = (bf16[384,1024]{1,0:T(8,128)(2,1)}, bf16[384,1024]{1,0:T(8,128)(2,1)S(1)}, u32[]{:S(2)}) copy-start(bf16[384,1024]{1,0:T(8,128)(2,1)S(1)} %collective-permute-done.3.refs_5_) | copy-start | bytes 2359300
  947.5 17.3 %all-to-all-start.2 = ((bf16[8,48,1152]{2,1,0:T(8,128)(2,1)}), bf16[8,48,1152]{2,1,0:T(8,128)(2,1)S(1)}, u32[]{:S(2)}, u32[]{:S(2)}) async-start(bf16[8,48,1152]{2,1,0:T(8,128)(2,1)} %bitcast.377), calls=%async_computation.7 | async-start | bytes 1769472 | tf_op jit(solution)/shard_map/all_to_all | solution.py:1227
  (107 other events, 407.5 us)
Sparse Core Ops, SparseCore 0:
  10.2 41.9 all-gather.6
  54.3 135.4 all-gather.4
  195.2 113.3 all-gather.8
  309.9 113.1 all-gather.10
  441.8 23.0 reduce-scatter.13
  467.0 43.0 reduce-scatter.11
  513.0 77.0 reduce-scatter.9
  592.3 42.9 reduce-scatter.17
  638.2 76.9 reduce-scatter.15
  722.2 103.7 reduce-scatter.21
  828.3 35.0 reduce-scatter.19

commit v3 on v2

--- a/solution.py
+++ b/solution.py
@@ -337,10 +337,11 @@
 
 
 def gather_kernel(sets, count, swaps, lines, waits, *refs):
-    total = count + swaps + lines
-    owns, give, block = refs[:count], refs[count : count + swaps], refs[count + swaps : total]
-    refs = refs[total + waits :]
-    outs, take, line_out = refs[:count], refs[count : count + swaps], refs[count + swaps : total]
+    owns, sides, block = refs[:count], refs[count : count + swaps], refs[count + swaps :][:lines]
+    refs = refs[count + swaps + lines + waits :]
+    shares = swaps * (sides[0].shape[1] if swaps else 0)
+    total = count + shares + lines
+    outs, take, line_out = refs[:count], refs[count : count + shares], refs[count + shares : total]
     send_sem, recv_sem, copy_sem = refs[total:]
     me = lax.axis_index("expert")
     core, column, line = neighbours(me)
@@ -354,7 +355,7 @@
     distant = place + 2 - 4 * (place // 2)
     along = []
     for i in range(lines):
-        base = 17 * count + swaps + 3 * i
+        base = 17 * count + shares + 3 * i
         own, out = block[i], line_out[i]
         along.append(
             (
@@ -420,7 +421,12 @@
     for copied in across:
         copied.start()
     begin(first)
-    swapped = begin_swaps(give + take, swaps, 17 * count, send_sem, recv_sem, peers[3:4])
+    swapped = []
+    for i in range(shares):
+        mine = take[i].at[place % 2]
+        here.append(pltpu.make_async_copy(sides[0].at[0, i], mine, copy_sem.at[count + lines + i]))
+        swapped.append(copy(17 * count + i, sides[0].at[1, i], mine, peers[3]))
+        swapped[-1].start()
     for here_block, to_far, to_near, relayed in along:
         to_far.wait_recv()
         relayed.start()
@@ -459,21 +465,23 @@
         ]
     count = len(owns)
     sets = (sets,) * count if isinstance(sets, int) else sets
-    total = count + len(swaps) + len(lines)
+    shares = [v for side in swaps for v in [side.shape[2:]] * side.shape[1]]
+    total = count + len(shares) + len(lines)
+    sems = 17 * count + len(shares) + 3 * len(lines)
     anywhere = pl.BlockSpec(memory_space=pl.ANY)
     outs = pl.pallas_call(
         partial(gather_kernel, sets, count, len(swaps), len(lines), len(after)),
         out_shape=[
             jax.ShapeDtypeStruct((8 * n,) + own.shape, own.dtype) for n, own in zip(sets, owns)
         ]
-        + [jax.ShapeDtypeStruct(v.shape, v.dtype) for v in swaps]
+        + [jax.ShapeDtypeStruct((2,) + v, b16) for v in shares]
         + [jax.ShapeDtypeStruct((4,) + v.shape, v.dtype) for v in lines],
-        in_specs=[anywhere] * (total + len(after)),
+        in_specs=[anywhere] * (count + len(swaps) + len(lines) + len(after)),
         out_specs=[anywhere] * total,
         scratch_shapes=[
-            pltpu.SemaphoreType.DMA((17 * count + len(swaps) + 3 * len(lines),)),
-            pltpu.SemaphoreType.DMA((17 * count + len(swaps) + 3 * len(lines),)),
-            pltpu.SemaphoreType.DMA((count + len(lines),)),
+            pltpu.SemaphoreType.DMA((sems,)),
+            pltpu.SemaphoreType.DMA((sems,)),
+            pltpu.SemaphoreType.DMA((count + len(lines) + len(shares),)),
         ],
         compiler_params=pltpu.CompilerParams(collective_id=number, has_side_effects=True),
         cost_estimate=pl.CostEstimate(flops=0, bytes_accessed=1024, transcendentals=0),
@@ -600,17 +608,54 @@
         return found
 
     legs = {}
-    for g in order:
-        pair_sum(g, 0)
-        d_x = sends(g, 4, 0, top, 4, peers[1])
-        d_y = sends(g, 5, 0, bottom, 5, peers[2])
-        pair_sum(g, 1)
-        x_top = sends(g, 6, 1, top, 2, peers[1])
-        pair_sum(g, 2)
-        y_bottom = sends(g, 7, 2, bottom, 3, peers[2])
-        pair_sum(g, 3)
-        legs[g] = [d_x, d_y, x_top, y_bottom]
-
+
+    def begin_legs(g, summed):
+        for k in range(4):
+            if not summed:
+                pair_sum(g, k)
+            if k == 0:
+                legs[g] = [
+                    sends(g, 4, 0, top, 4, peers[1]),
+                    sends(g, 5, 0, bottom, 5, peers[2]),
+                ]
+            elif k == 1:
+                legs[g].append(sends(g, 6, 1, top, 2, peers[1]))
+            elif k == 2:
+                legs[g].append(sends(g, 7, 2, bottom, 3, peers[2]))
+
+    def second_legs(g):
+        d_x, d_y, x_top, y_bottom = legs[g]
+        for i in arrays:
+            d_x[i].wait_recv()
+
+        def add_y(block):
+            for i in arrays:
+                mine, extra = keep(g, i, 0), keep(g, i, 4)
+                mine[2, block] = (
+                    mine[2, block].astype(f32) + extra[block, :].astype(f32)
+                ).astype(b16)
+
+        each(0, half, add_y)
+        y_top = sends(g, 8, 2, top, 3, peers[2])
+        for i in arrays:
+            d_y[i].wait_recv()
+
+        def add_x(block):
+            low = pl.ds(pl.multiple_of(block.start - half, 16), 16)
+            for i in arrays:
+                mine, extra = keep(g, i, 0), keep(g, i, 5)
+                mine[1, block] = (
+                    mine[1, block].astype(f32) + extra[low, :].astype(f32)
+                ).astype(b16)
+
+        each(half, half, add_x)
+        x_bottom = sends(g, 9, 1, bottom, 2, peers[1])
+        legs[g] = [x_top, y_bottom, y_top, x_bottom]
+
+    begin_legs(sets - 1, False)
+    if sets == 2:
+        for k in range(4):
+            pair_sum(0, k)
     for to_x, to_y, to_core, x_relay, y_relay, x_core, y_core, d_core in small:
         to_x.wait_recv()
         x_relay.start()
@@ -621,42 +666,17 @@
     for to_far, to_near, relayed in along:
         to_far.wait_recv()
         relayed.start()
-
-    for g in order:
-        d_x, d_y, x_top, y_bottom = legs[g]
-        for i in arrays:
-            d_x[i].wait_recv()
-
-        def add_y(block):
-            for i in arrays:
-                mine, extra = keep(g, i, 0), keep(g, i, 4)
-                mine[2, block] = (
-                    mine[2, block].astype(f32) + extra[block, :].astype(f32)
-                ).astype(b16)
-
-        each(0, half, add_y)
-        y_top = sends(g, 8, 2, top, 3, peers[2])
-        for i in arrays:
-            d_y[i].wait_recv()
-
-        def add_x(block):
-            low = pl.ds(pl.multiple_of(block.start - half, 16), 16)
-            for i in arrays:
-                mine, extra = keep(g, i, 0), keep(g, i, 5)
-                mine[1, block] = (
-                    mine[1, block].astype(f32) + extra[low, :].astype(f32)
-                ).astype(b16)
-
-        each(half, half, add_x)
-        x_bottom = sends(g, 9, 1, bottom, 2, peers[1])
-        legs[g] = [x_top, y_bottom, y_top, x_bottom]
-
+    second_legs(sets - 1)
+    if sets == 2:
+        begin_legs(0, True)
     for to_x, to_y, to_core, x_relay, y_relay, x_core, y_core, d_core in small:
         x_relay.wait_recv()
         y_relay.wait_recv()
         d_core.start()
     across = []
     for g in order:
+        if g == 0 and sets == 2:
+            second_legs(0)
         for i in arrays:
             for came in legs[g]:
                 came[i].wait_recv()
@@ -743,9 +763,7 @@
             pltpu.SemaphoreType.DMA((sems,)),
             pltpu.SemaphoreType.DMA((8 * count + len(gathers) + len(lines),)),
         ],
-        compiler_params=pltpu.CompilerParams(
-            collective_id=number, has_side_effects=True, vmem_limit_bytes=(16 + 24 * sets) << 20
-        ),
+        compiler_params=pltpu.CompilerParams(collective_id=number, has_side_effects=True),
         cost_estimate=pl.CostEstimate(flops=0, bytes_accessed=1024, transcendentals=0),
     )(*[part.reshape(8 * sets, rows, part.shape[1]) for part in parts], *others)
 
@@ -877,6 +895,151 @@
     return [v.reshape(seqs * slots, width) for v in outs]
 
 
+def expert_kernel(
+    x_ref,
+    dy_ref,
+    gate_ref,
+    bank_ref,
+    out_ref,
+    back_ref,
+    dgate_ref,
+    wide_ref,
+    tall_ref,
+    down_ref,
+    wide_sum,
+    tall_sum,
+):
+    hidden = tall_ref.shape[0]
+    third = x_ref.shape[1] // 3
+    part = hidden // 4
+
+    @pl.when(pl.program_id(0) == 0)
+    def _():
+        for i in range(4):
+            for k in range(3):
+                down_ref[i * part : (i + 1) * part, k * third : (k + 1) * third] = bank_ref[
+                    (3 * i + k) * part : (3 * i + k + 1) * part, 2 * hidden :
+                ]
+        wide_sum[...] = jnp.zeros_like(wide_sum)
+        tall_sum[...] = jnp.zeros_like(tall_sum)
+
+    x, gate = x_ref[...], gate_ref[...]
+    pre = dot(x, bank_ref[:, : 2 * hidden])
+    lin = pre[:, hidden:]
+    sigma = sigmoid(pre[:, :hidden])
+    soft = pre[:, :hidden] * sigma
+    slope = sigma * (1.0 + pre[:, :hidden] * (1.0 - sigma))
+    hid = (soft * lin).astype(b16)
+    made = dot(hid, down_ref[...]).astype(b16).astype(f32)
+    dy = dy_ref[...].astype(f32)
+    dgate_ref[...] = jnp.sum(made * dy, axis=1, keepdims=True)
+    out_ref[...] = (made * gate).astype(b16)
+    dmade = (dy * gate).astype(b16)
+    dhid = dot_nt(dmade, down_ref[...])
+    dpre = jnp.concatenate([dhid * lin * slope, dhid * soft], axis=1).astype(b16)
+    back_ref[...] = dot_nt(dpre, bank_ref[:, : 2 * hidden]).astype(b16)
+    wide_sum[...] += dot_tn(x, dpre)
+    tall_sum[...] += dot_tn(hid, dmade)
+
+    @pl.when(pl.program_id(0) == pl.num_programs(0) - 1)
+    def _():
+        wide_ref[...] = wide_sum[...].astype(b16)
+        tall_ref[...] = tall_sum[...].astype(b16)
+
+
+def expert(x, dy, gate, bank, hidden, after=()):
+    rows, width = x.shape
+    block = 256
+    per = pl.BlockSpec((block, width), lambda s: (s, 0))
+    one = pl.BlockSpec((block, 1), lambda s: (s, 0))
+
+    def kernel(*refs):
+        expert_kernel(*refs[:4], *refs[4 + len(after) :])
+
+    return pl.pallas_call(
+        kernel,
+        grid=(rows // block,),
+        in_specs=[
+            per,
+            per,
+            one,
+            pl.BlockSpec(bank.shape, lambda s: (0, 0), pipeline_mode=pl.Buffered(1)),
+        ]
+        + [pl.BlockSpec(memory_space=pl.ANY)] * len(after),
+        out_specs=[per, per, one, fixed(width, 2 * hidden), fixed(hidden, width)],
+        out_shape=[
+            jax.ShapeDtypeStruct((rows, width), b16),
+            jax.ShapeDtypeStruct((rows, width), b16),
+            jax.ShapeDtypeStruct((rows, 1), f32),
+            jax.ShapeDtypeStruct((width, 2 * hidden), b16),
+            jax.ShapeDtypeStruct((hidden, width), b16),
+        ],
+        scratch_shapes=[
+            pltpu.VMEM((hidden, width), b16),
+            pltpu.VMEM((width, 2 * hidden), f32),
+            pltpu.VMEM((hidden, width), f32),
+        ],
+        compiler_params=pltpu.CompilerParams(vmem_limit_bytes=48 << 20),
+        cost_estimate=pl.CostEstimate(flops=0, bytes_accessed=1024, transcendentals=0),
+    )(x, dy, gate, bank, *after)
+
+
+def shared_kernel(
+    x_ref, dy_ref, wide_ref, tall_ref, hid_ref, dpre_ref, wide_out, tall_out, wide_sum, tall_sum
+):
+    hidden = tall_ref.shape[0]
+
+    @pl.when(pl.program_id(0) == 0)
+    def _():
+        wide_sum[...] = jnp.zeros_like(wide_sum)
+        tall_sum[...] = jnp.zeros_like(tall_sum)
+
+    x, dy = x_ref[...], dy_ref[...]
+    pre = dot(x, wide_ref[...])
+    lin = pre[:, hidden:]
+    sigma = sigmoid(pre[:, :hidden])
+    soft = pre[:, :hidden] * sigma
+    slope = sigma * (1.0 + pre[:, :hidden] * (1.0 - sigma))
+    hid = (soft * lin).astype(b16)
+    dhid = dot_nt(dy, tall_ref[...])
+    dpre = jnp.concatenate([dhid * lin * slope, dhid * soft], axis=1).astype(b16)
+    hid_ref[...] = hid
+    dpre_ref[...] = dpre
+    wide_sum[...] += dot_tn(x, dpre)
+    tall_sum[...] += dot_tn(hid, dy)
+
+    @pl.when(pl.program_id(0) == pl.num_programs(0) - 1)
+    def _():
+        wide_out[...] = wide_sum[...].astype(b16)
+        tall_out[...] = tall_sum[...].astype(b16)
+
+
+def shared_expert(x, dy, wide, tall, rows, after=()):
+    width, hidden = x.shape[1], tall.shape[0]
+    block = 256
+    per = lambda n: pl.BlockSpec((block, n), lambda s: (s, 0))
+
+    def kernel(*refs):
+        shared_kernel(*refs[:4], *refs[4 + len(after) :])
+
+    return pl.pallas_call(
+        kernel,
+        grid=(rows // block,),
+        in_specs=[per(width), per(width), fixed(*wide.shape), fixed(*tall.shape)]
+        + [pl.BlockSpec(memory_space=pl.ANY)] * len(after),
+        out_specs=[per(hidden), per(2 * hidden), fixed(*wide.shape), fixed(*tall.shape)],
+        out_shape=[
+            jax.ShapeDtypeStruct((rows, hidden), b16),
+            jax.ShapeDtypeStruct((rows, 2 * hidden), b16),
+            jax.ShapeDtypeStruct(wide.shape, b16),
+            jax.ShapeDtypeStruct(tall.shape, b16),
+        ],
+        scratch_shapes=[pltpu.VMEM(wide.shape, f32), pltpu.VMEM(tall.shape, f32)],
+        compiler_params=pltpu.CompilerParams(vmem_limit_bytes=32 << 20),
+        cost_estimate=pl.CostEstimate(flops=0, bytes_accessed=1024, transcendentals=0),
+    )(x, dy, wide, tall, *after)
+
+
 def bank_kernel(parity_ref, gate_ref, up_ref, down_ref, out_ref):
     columns = gate_ref.shape[2]
     rows = down_ref.shape[1]
@@ -906,6 +1069,30 @@
         out_shape=jax.ShapeDtypeStruct((2, half, rows, 3 * columns), b16),
         cost_estimate=pl.CostEstimate(flops=0, bytes_accessed=1024, transcendentals=0),
     )(parity.reshape(1), gate, up, down)
+
+
+def plain_expert(x, dy, gate, bank, planes):
+    width = x.shape[1]
+    hidden = bank.shape[1] // 3
+    gate_up = bank[:, : 2 * hidden]
+    down = bank[:, 2 * hidden :].reshape(planes, 3, hidden // planes, width // 3)
+    down = down.transpose(0, 2, 1, 3).reshape(hidden, width)
+    pre = dot(x, gate_up)
+    soft, slope = silu_parts(pre[:, :hidden])
+    lin = pre[:, hidden:]
+    hid = (soft * lin).astype(b16)
+    made = dot(hid, down).astype(b16).astype(f32)
+    dy = dy.astype(f32)
+    dmade = (dy * gate).astype(b16)
+    dhid = dot_nt(dmade, down)
+    dpre = jnp.concatenate([dhid * lin * slope, dhid * soft], axis=1).astype(b16)
+    return (
+        (made * gate).astype(b16),
+        dot_nt(dpre, gate_up).astype(b16),
+        jnp.sum(made * dy, axis=1, keepdims=True),
+        dot_tn(x, dpre).astype(b16),
+        dot_tn(hid, dmade).astype(b16),
+    )
 
 
 class Heads:
@@ -1017,19 +1204,12 @@
     if sets == 2:
         ends = [[0, 2], [1, 3]]
         sides = bank_rows((place % 2).astype(jnp.int32), expert_gate, expert_up, expert_down)
-        banks = [sides[0, e] for e in range(taken)]
-        gives = [sides[1, e] for e in range(taken)]
+        gives = [sides]
     else:
         banks = [
             jnp.concatenate([expert_gate[e], expert_up[e], stacked(expert_down[e])], axis=1)
             for e in range(local)
         ]
-
-    def settle(e, came):
-        rows = came.shape[0]
-        both = jnp.zeros((2 * rows, came.shape[1]), b16)
-        both = lax.dynamic_update_slice_in_dim(both, banks[e], place % 2 * rows, 0)
-        banks[e] = lax.dynamic_update_slice_in_dim(both, came, (1 - place % 2) * rows, 0)
 
     own_routes = jnp.pad(routes.reshape(tokens, picks).astype(b16), ((0, 0), (0, LANES - picks)))
     flat_in = block_input.reshape(tokens, width)
@@ -1038,8 +1218,8 @@
     all_in, all_grad, all_routes, *swapped = plane_gather(
         0, flat_in, grad_low, own_routes, sets=(1, sets, sets), swaps=gives
     )
-    for e, other in enumerate(swapped):
-        settle(e, other)
+    if sets == 2:
+        banks = [v.reshape(-1, v.shape[2]) for v in swapped]
     proj = gather(came.reshape(plane * shard, -1), "dp")
     in_w = proj[:, :main]
     gate_up = proj[:, main:]
@@ -1137,10 +1317,19 @@
     rows_grad = spread(select, all_grad, taken)
     outs, backs, dgates, sums = [], [], [], []
     tied = []
-    made_grads = []
-
-    def weight_grads(x, depre, ehid, dmade):
-        made_grads[:] = [dot_tn(x, depre).astype(b16), dot_tn(ehid, dmade).astype(b16)]
+    for e in range(taken):
+        gate = slot_gates[:, e].reshape(seqs * slots, 1)
+        if sets == 2:
+            out, grad, dgate, *made_grads = expert(
+                rows_in[e], rows_grad[e], gate, whole[e], ehidden, after=tied
+            )
+        else:
+            out, grad, dgate, *made_grads = plain_expert(
+                rows_in[e], rows_grad[e], gate, whole[e], planes
+            )
+        outs.append(out)
+        backs.append(grad)
+        dgates.append(dgate.reshape(seqs, slots))
         sums.append(
             [
                 lax.psum_scatter(
@@ -1149,42 +1338,11 @@
                 for v in made_grads
             ]
         )
-
-    for e in range(taken):
-        bank = whole[e]
-        x, dy = rows_in[e], rows_grad[e]
-        x, bank, *tied = tie(x, bank, *tied)
-        gu_w = bank[:, : 2 * ehidden]
-        e_down = bank[:, 2 * ehidden :].reshape(planes, 3, part, third)
-        e_down = e_down.transpose(0, 2, 1, 3).reshape(ehidden, width)
-        g = slot_gates[:, e].reshape(seqs * slots, 1)
-        epre = dot(x, gu_w)
-        esoft, eslope = silu_parts(epre[:, :ehidden])
-        elin = epre[:, ehidden:]
-        ehid = (esoft * elin).astype(b16)
-        made = dot(ehid, e_down).astype(b16).astype(f32)
-        dy = dy.astype(f32)
-        dgates.append(jnp.sum(made * dy, axis=1).reshape(seqs, slots))
-        outs.append((made * g).astype(b16))
-        dmade = (dy * g).astype(b16)
-        dehid = dot_nt(dmade, e_down)
-        depre = jnp.concatenate([dehid * elin * eslope, dehid * esoft], axis=1).astype(b16)
-        backs.append(dot_nt(depre, gu_w).astype(b16))
-        weight_grads(x, depre, ehid, dmade)
-        tied = tied + made_grads
         if e == 0:
-            tied = list(tie(all_routed, *tied))
-            near_routed, near_grad = tied[0][:near], all_grad[:near]
-            pre = dot(near_routed, gate_up)
-            soft, slope = silu_parts(pre[:, :fs])
-            lin = pre[:, fs:]
-            hid = (soft * lin).astype(b16)
-            dhid = dot_nt(near_grad, down_w)
-            dpre = jnp.concatenate([dhid * lin * slope, dhid * soft], axis=1).astype(b16)
-            shared_grad = dot_tn(near_routed, dpre).astype(b16)
-            down_grad = dot_tn(hid, near_grad).astype(b16)
-            tied = [shared_grad, down_grad, hid, dpre] + tied[1:]
-    shared_grad, down_grad, hid, dpre = tied[:4]
+            hid, dpre, shared_grad, down_grad = shared_expert(
+                all_routed, all_grad, gate_up, down_w, near, after=made_grads
+            )
+            tied = [hid, dpre, shared_grad, down_grad]
     dgate_rows = jnp.sum(
         jnp.where(chosen, jnp.stack(dgates, axis=1)[:, :, :, None], 0.0), axis=2
     ).transpose(0, 2, 1)
@@ -1250,12 +1408,12 @@
         7,
         dot_nt(dmerged, in_w).astype(b16),
         gathers=[taps_of],
-        after=[shared_rows] + swapped,
+        after=[shared_rows],
     )
     taps_of = jnp.sum(taps_of, axis=0)
-    out_part = merge(select, outs, hid, down_w, after=[dmerged])
+    out_part = merge(select, outs, hid, down_w, after=[dnormed])
     out_part, dnormed = tie(out_part, dnormed)
-    out_sum, small = plane_scatter(5, out_part, sets=sets, lines=[taps_of])
+    out_sum, small = plane_scatter(5, out_part, sets=sets, lines=[taps_of], after=swapped)
     small = jnp.sum(small, axis=0)
 
     shared_grad = shared_rows

time: 988 us -> 949 us (0.961)
  matrix products: 152 us -> 62.9 us
  Pallas kernels: 548 us -> 604 us
  waiting for transfers between devices: 54.2 us -> 34.9 us
    pallas_call x0 -> x3, Pallas kernels: none -> 65.8 us  [the longest x2 54.8 us: expert(): pl.pallas_call(kernel, grid=(rows // block,), in_specs=[per, per, one, pl...]
    ppermute x6, waiting for transfers between devices: 36.9 us -> 0.02 us  [exchange(): return lax.ppermute(value, axis, [(i, i ^ distance) for i in range(size)])]
    dot_general x8 -> x3, matrix products: 52.6 us -> 21.5 us  [dot_nt(): return lax.dot_general(a, b, NT, preferred_element_type=f32)]
    dot_general x9 -> x4, matrix products: 51.9 us -> 22.7 us  [dot(): return jnp.dot(a, b, preferred_element_type=f32)]
    dot_general x9 -> x3, matrix products: 47.2 us -> 18.5 us  [dot_tn(): lax.dot_general(a, b, (((0,), (0,)), ((), ())), preferred_element_type=f32)]
    unnamed x268 -> x224, local copies, waits for them, and re-layouts: 48.6 us -> 65.3 us
    pallas_call x4, Pallas kernels: 219 us -> 203 us  [plane_scatter(): pl.pallas_call(partial(scatter_kernel, sets, count, len(swaps), len(gathe...]
    reduce_scatter x4, waiting for transfers between devices: 0.04 us -> 14.6 us  [body(): lax.psum_scatter(v, 'dp', scatter_dimension=0, tiled=True, axis_index_gro...]
  transfers between devices with their start and end apart: 19 -> 19, of which waited for: 5 -> 4; matrix products, arithmetic and copies ran while one was open for 28% -> 19% of each run, Pallas kernels for 56% -> 64%
where the time goes in v3:
time: 949 us; the launch traced here: 940 us
  Pallas kernels  604 us (64%)
  local copies, waits for them, and re-layouts  111 us (12%)
  other arithmetic  76.8 us (8%)
  matrix products  62.9 us (7%)
  waiting for transfers between devices  34.9 us (4%)
  blocking collectives  20.7 us (2%)
  between operations  16.1 us (2%)
  starting transfers between devices  13.8 us (1%)
    pallas_call x3, Pallas kernels, plane_gather(): pl.pallas_call(partial(gather_kernel, sets, count, len(swaps), len(lines)...  245 us
    pallas_call x4, Pallas kernels, plane_scatter(): pl.pallas_call(partial(scatter_kernel, sets, count, len(swaps), len(gathe...  203 us
    unnamed x224, local copies, waits for them, and re-layouts  65.3 us
    pallas_call x2, Pallas kernels, expert(): pl.pallas_call(kernel, grid=(rows // block,), in_specs=[per, per, one, pl...  54.8 us
    pallas_call x2, Pallas kernels, merge(): pl.pallas_call(partial(merge_kernel, near, len(parts)), grid=(seqs,), in_...  39 us
    dot_general x4, matrix products, dot(): return jnp.dot(a, b, preferred_element_type=f32)  22.7 us
    dot_general x3, matrix products, dot_nt(): return lax.dot_general(a, b, NT, preferred_element_type=f32)  21.5 us
    pallas_call x1, Pallas kernels, mix_backward(): pl.pallas_call(partial(backward_kernel, width // LANES), grid=(tokens //...  21.3 us
  transfers between devices with their start and end apart: 19, of which 4 were waited for; matrix products, arithmetic and copies ran while one was open for 19% of the time, Pallas kernels for 64%

profile of v3, /device:TPU:0, one launch (start us, length us, event | category | flops | bytes accessed | tf_op | source)
XLA Modules:
  0.0 940.2 jit_solution(17466244322249879332)
XLA Ops:
  14.9 20.7 %all_to_all.15 = bf16[8,48,1408]{2,1,0:T(8,128)(2,1)S(1)} all-to-all(bf16[8,48,1408]{2,1,0:T(8,128)(2,1)S(1)} %bitcast.270), channel_id=1, replica_groups=mesh['dp'=4,'expert'=8] {'expert'}, dimensions={0} | all-to-all | bytes 2162688 | tf_op jit(solution)/shard_map/all_to_all | solution.py:1198
  37.9 5.0 shard_map.339.refs_3_
  42.9 147.3 %shard_map.340 = (bf16[8,256,1536]{2,1,0:T(8,128)(2,1)}, bf16[16,256,1536]{2,1,0:T(8,128)(2,1)}, bf16[16,256,128]{2,1,0:T(8,128)(2,1)}, bf16[2,384,1536]{2,1,0:T(8,128)(2,1)}, bf16[2,384,1536]{2,1,0:T(8,128)(2,1)}) custom-call(bf16[256,1536]{1,0:T(8,128)(2,1)} %bitcast.257, bf16[256,1536]{1,0:T(8,128)(2,1)} %bitcast.261, bf16[256,128]{1,0:T(8,128)(2,1)} %pad.29.refs_2_, ...), custom_call_target="tpu_custom_call" | custom-call | bytes 1024 | tf_op jit(solution)/shard_map/pallas_call | solution.py:472
  192.9 4.1 multiply_reduce_fusion
  200.1 5.6 copy-done.2
  205.7 6.9 shard_map.345
  222.4 4.4 fusion.1
  226.9 8.5 fusion.4.merged_ref
  235.4 10.9 %shard_map.341 = (bf16[2048,384]{1,0:T(8,128)(2,1)S(1)}, f32[2048,384]{1,0:T(8,128)S(1)}, f32[2048,128]{1,0:T(8,128)S(1)}) custom-call(f32[2048,1152]{1,0:T(8,128)S(1)} %fusion.4.merged_ref, f32[4,640]{1,0:T(4,128)S(1)} %maximum_convert_fusion.1.weight_ref, f32[1,640]{1,0:T(1,128)S(1)} %maximum_convert_fusion.2.bias_ref, ...), custom_call_target="tpu_custom_call" | custom-call | bytes 1024 | tf_op jit(solution)/shard_map/pallas_call | solution.py:243
  251.6 6.8 convolution_convert_fusion.1
  258.4 36.5 %shard_map.342 = (f32[256,1536]{1,0:T(8,128)}, f32[256,128]{1,0:T(8,128)}) custom-call(bf16[8,256,1536]{2,1,0:T(8,128)(2,1)} %bitcast.264, bf16[8,256,128]{2,1,0:T(8,128)(2,1)} %select_select_fusion.refs_1_), custom_call_target="tpu_custom_call" | custom-call | bytes 1024 | tf_op jit(solution)/shard_map/pallas_call | solution.py:749
  296.0 2.5 multiply_reduce_fusion.4
  300.7 4.3 all-gather.9.cloned.1.call-done.refs_3_
  305.1 63.9 %shard_map.343 = bf16[16,256,1536]{2,1,0:T(8,128)(2,1)} custom-call(bf16[256,1536]{1,0:T(8,128)(2,1)} %multiply_convert_fusion.1.refs_0_), custom_call_target="tpu_custom_call" | custom-call | bytes 1024 | tf_op jit(solution)/shard_map/pallas_call | solution.py:472
  369.0 4.6 copy-done
  373.5 6.9 shard_map.344
  380.5 4.8 select_reduce_fusion.2
  389.2 2.3 copy.328.refs_2_
  391.5 27.0 %shard_map.346 = (bf16[1280,1536]{1,0:T(8,128)(2,1)}, bf16[1280,1536]{1,0:T(8,128)(2,1)}, f32[1280,1]{1,0:T(8,128)S(1)}, bf16[1536,1024]{1,0:T(8,128)(2,1)S(1)}, bf16[512,1536]{1,0:T(8,128)(2,1)}) custom-call(bf16[1280,1536]{1,0:T(8,128)(2,1)} %bitcast.250, bf16[1280,1536]{1,0:T(8,128)(2,1)} %bitcast.248, f32[1280,1]{1,0:T(8,128)S(1)} %reshape_squeeze.8.refs_2_, ...), custom_call_target="tpu_custom_call" | custom-call | bytes 1024 | tf_op jit(solution)/shard_map/pallas_call | solution.py:959
  421.0 4.6 copy-done.1
  428.6 11.0 %shard_map.347 = (bf16[2048,128]{1,0:T(8,128)(2,1)S(1)}, bf16[2048,256]{1,0:T(8,128)(2,1)S(1)}, bf16[1536,256]{1,0:T(8,128)(2,1)}, bf16[128,1536]{1,0:T(8,128)(2,1)S(1)}) custom-call(bf16[4096,1536]{1,0:T(8,128)(2,1)S(1)} %bitcast.239, bf16[4096,1536]{1,0:T(8,128)(2,1)} %bitcast.240, bf16[1536,256]{1,0:T(8,128)(2,1)S(1)} %copy-done.19, ...), custom_call_target="tpu_custom_call" | custom-call | bytes 1024 | tf_op jit(solution)/shard_map/pallas_call | solution.py:1025
  444.2 27.8 %shard_map.348 = (bf16[1280,1536]{1,0:T(8,128)(2,1)}, bf16[1280,1536]{1,0:T(8,128)(2,1)}, f32[1280,1]{1,0:T(8,128)S(1)}, bf16[1536,1024]{1,0:T(8,128)(2,1)}, bf16[512,1536]{1,0:T(8,128)(2,1)}) custom-call(bf16[1280,1536]{1,0:T(8,128)(2,1)} %bitcast.252, bf16[1280,1536]{1,0:T(8,128)(2,1)} %bitcast.251, f32[1280,1]{1,0:T(8,128)S(1)} %reshape_squeeze.9.refs_2_, ...), custom_call_target="tpu_custom_call" | custom-call | bytes 1024 | tf_op jit(solution)/shard_map/pallas_call | solution.py:959
  481.5 2.7 select_reduce_fusion.3
  493.6 2.3 copy.331
  498.8 3.2 maximum_maximum_fusion
  506.2 17.7 %shard_map.349 = bf16[4096,1536]{1,0:T(8,128)(2,1)S(1)} custom-call(bf16[32,80,128]{2,1,0:T(8,128)(2,1)S(1)} %fusion.15.select_ref, bf16[32,40,1536]{2,1,0:T(8,128)(2,1)S(1)} %bitcast.247, bf16[32,40,1536]{2,1,0:T(8,128)(2,1)S(1)} %bitcast.249, bf16[2048,256]{1,0:T(8,128)(2,1)S(1)} %get-tuple-element.87.refs_5_.refs_2_, ...), custom_call_target="tpu_custom_call" | custom-call | bytes 1024 | tf_op jit(solution)/shard_map/pallas_call | solution.py:855
  523.9 4.6 copy-done.3
  528.5 68.7 %shard_map.350 = (f32[256,1536]{1,0:T(8,128)}, f32[256,128]{1,0:T(8,128)}) custom-call(bf16[16,256,1536]{2,1,0:T(8,128)(2,1)} %bitcast.242, bf16[16,256,128]{2,1,0:T(8,128)(2,1)} %bitcast.272, bf16[1536,1024]{1,0:T(8,128)(2,1)} %get-tuple-element.96.refs_2_, bf16[512,1536]{1,0:T(8,128)(2,1)} %get-tuple-element.97.refs_3_), custom_call_target="tpu_custom_call" | custom-call | bytes 1024 | tf_op jit(solution)/shard_map/pallas_call | solution.py:749
  599.9 2.7 multiply_reduce_fusion.1
  606.4 3.4 all-to-all-start.1
  609.9 6.1 all-to-all-done.1
  622.6 2.8 collective-permute-start.4
  627.3 14.6 %reduce-scatter.10.cloned.1.call-done.refs_2_ = bf16[768,1024]{1,0:T(8,128)(2,1)} async-done(((bf16[1536,1024]{1,0:T(8,128)(2,1)}), bf16[768,1024]{1,0:T(8,128)(2,1)}) %reduce-scatter.10.cloned.1.call-update) | async-done | bytes 1572880 | tf_op jit(solution)/shard_map/reduce_scatter | solution.py:1335
  641.8 33.9 %shard_map.351 = (bf16[8,256,1536]{2,1,0:T(8,128)(2,1)}, bf16[8,256,128]{2,1,0:T(8,128)(2,1)}) custom-call(bf16[256,1536]{1,0:T(8,128)(2,1)} %get-tuple-element.200.refs_0_, bf16[256,128]{1,0:T(8,128)(2,1)} %select_select_fusion.1.refs_1_, bf16[768,1024]{1,0:T(8,128)(2,1)} %reduce-scatter.10.cloned.1.call-done.refs_2_, ...), custom_call_target="tpu_custom_call" | custom-call | bytes 1024 | tf_op jit(solution)/shard_map/pallas_call | solution.py:472
  677.4 5.7 fusion.16.grad_ref
  683.6 21.3 %shard_map.352 = (bf16[2048,1152]{1,0:T(8,128)(2,1)S(1)}, f32[4,640]{1,0:T(4,128)S(1)}, f32[1,640]{1,0:T(1,128)S(1)}, f32[1,384]{1,0:T(1,128)S(1)}, f32[8,128]{1,0:T(8,128)S(1)}) custom-call(f32[2048,1152]{1,0:T(8,128)S(1)} %bitcast.244, f32[2048,384]{1,0:T(8,128)S(1)} %copy-done.18, f32[2048,384]{1,0:T(8,128)S(1)} %fusion.16.grad_ref, ...), custom_call_target="tpu_custom_call" | custom-call | bytes 1024 | tf_op jit(solution)/shard_map/pallas_call | solution.py:263
  704.9 12.1 %fusion.51 = f32[1536,1152]{0,1:T(8,128)S(1)} fusion(bf16[2048,1536]{1,0:T(8,128)(2,1)} %copy-done.54, bf16[2048,1152]{1,0:T(8,128)(2,1)S(1)} %get-tuple-element.102), kind=kOutput, calls=%fused_computation.189 | convolution fusion | flops 7247757312 | bytes 18087936 | tf_op jit(solution)/shard_map/dot_general | solution.py:792
  720.1 5.8 copy.356
  730.3 2.5 broadcast_select_fusion.2
  735.8 5.4 convolution_convert_fusion.2
  744.1 13.2 %convolution_convert_fusion = bf16[2048,1536]{1,0:T(8,128)(2,1)} fusion(bf16[2048,1152]{1,0:T(8,128)(2,1)} %copy-done.37, bf16[1536,1408]{0,1:T(8,128)(2,1)} %all-gather.5.cloned.1.call-done), kind=kOutput, calls=%fused_computation.4 | convolution fusion | flops 7250903040 | bytes 14548992 | tf_op jit(solution)/shard_map/dot_general | solution.py:788
  758.0 37.8 %shard_map.353 = (f32[256,1536]{1,0:T(8,128)}, f32[8,16,3328]{2,1,0:T(8,128)}) custom-call(bf16[8,256,1536]{2,1,0:T(8,128)(2,1)} %bitcast.263, f32[16,3328]{1,0:T(8,128)} %pad.35.refs_1_, f32[8,48,256]{2,1,0:T(8,128)} %convert_element_type.268.refs_2_), custom_call_target="tpu_custom_call" | custom-call | bytes 1024 | tf_op jit(solution)/shard_map/pallas_call | solution.py:749
  801.5 21.3 %shard_map.354 = bf16[4096,1536]{1,0:T(8,128)(2,1)} custom-call(bf16[32,80,128]{2,1,0:T(8,128)(2,1)S(1)} %fusion.15.select_ref, bf16[32,40,1536]{2,1,0:T(8,128)(2,1)S(1)} %bitcast.245, bf16[32,40,1536]{2,1,0:T(8,128)(2,1)S(1)} %bitcast.246, bf16[2048,128]{1,0:T(8,128)(2,1)S(1)} %copy-done.22, bf16[128,1536]{1,0:T(8,128)(2,1)S(1)} %bitcast.254, ...), custom_call_target="tpu_custom_call" | custom-call | bytes 1024 | tf_op jit(solution)/shard_map/pallas_call | solution.py:855
  822.8 2.4 reduce_sum.208.refs_1_
  829.0 3.5 select_convert_fusion.2
  832.4 60.1 %shard_map.355 = (f32[256,1536]{1,0:T(8,128)}, f32[4,16,3328]{2,1,0:T(8,128)}) custom-call(bf16[16,256,1536]{2,1,0:T(8,128)(2,1)} %bitcast.256, f32[16,3328]{1,0:T(8,128)} %reduce_sum.208.refs_1_, bf16[384,1024]{1,0:T(8,128)(2,1)} %collective-permute-done.1.refs_2_, bf16[128,1536]{1,0:T(8,128)(2,1)} %collective-permute-done.2.refs_3_, ...), custom_call_target="tpu_custom_call" | custom-call | bytes 1024 | tf_op jit(solution)/shard_map/pallas_call | solution.py:749
  907.3 3.9 all-to-all-start.2
  916.5 8.3 all-to-all-done.2
  (471 shorter events, 142.1 us)
Async XLA Ops:
  7.2 189.8 %all-gather.7.cloned.1.call-start = ((), (), s32[]{:S(2)}) async-start(), calls=%async_computation.11 | async-start | bytes 2129920 | tf_op jit(solution)/shard_map/all_gather | solution.py:1170
  9.9 211.6 %all-gather.5.cloned.1.call-start = ((), (), s32[]{:S(2)}) async-start(), calls=%async_computation.10 | async-start | bytes 5406720 | tf_op jit(solution)/shard_map/all_gather | solution.py:1170
  37.0 268.0 %all-gather.9.cloned.1.call-start = ((), (), s32[]{:S(2)}) async-start(), calls=%async_computation.12 | async-start | bytes 7077888 | tf_op jit(solution)/shard_map/all_gather | solution.py:1291
  190.3 251.8 %all-gather.11.cloned.1.call-start = ((), (), s32[]{:S(2)}) async-start(), calls=%async_computation.13 | async-start | bytes 7077888 | tf_op jit(solution)/shard_map/all_gather | solution.py:1291
  192.3 43.1 %copy-start.33 = (f32[1,128]{1,0:T(1,128)}, f32[1,128]{1,0:T(1,128)S(1)}, u32[]{:S(2)}) copy-start(f32[1,128]{1,0:T(1,128)S(1)} %bitcast_convert_fusion.rate_ref) | copy-start | bytes 1540
  192.3 43.1 %copy-start.35 = (f32[1,128]{1,0:T(1,128)}, f32[1,128]{1,0:T(1,128)S(1)}, u32[]{:S(2)}) copy-start(f32[1,128]{1,0:T(1,128)S(1)} %bitcast_convert_fusion.1.step_ref) | copy-start | bytes 1540
  192.8 42.5 %copy-start.29 = (f32[1,384]{1,0:T(1,128)}, f32[1,384]{1,0:T(1,128)S(1)}, u32[]{:S(2)}) copy-start(f32[1,384]{1,0:T(1,128)S(1)} %fusion.43.skip_ref) | copy-start | bytes 4612
  198.6 19.9 %collective-permute-start = (bf16[2,96,1664]{2,1,0:T(8,128)(2,1)S(1)}, bf16[2,96,1664]{2,1,0:T(8,128)(2,1)}, u32[]{:S(2)}, u32[]{:S(2)}) collective-permute-start(bf16[2,96,1664]{2,1,0:T(8,128)(2,1)S(1)} %broadcast_select_fusion.4), channel_id=1, source_target_pairs={{0,1},{1,0},{2,3},{3,2},{4,5},{5,4},{6,7},{7,6},{8,9},{9,8},{10,11... | collective-permute-start | bytes 1916936 | tf_op jit(solution)/shard_map/ppermute | solution.py:815
  199.7 12.9 %copy-start.72 = (s32[32,2,128]{2,1,0:T(2,128)}, s32[32,2,128]{2,1,0:T(2,128)S(1)}, u32[]{:S(2)}) copy-start(s32[32,2,128]{2,1,0:T(2,128)S(1)} %copy.325) | copy-start | bytes 98308
  199.8 185.8 %copy-start.76 = (pred[32,2,128]{2,1,0:T(4,128)(4,1)}, pred[32,2,128]{2,1,0:T(4,128)(4,1)S(1)}, u32[]{:S(2)}) copy-start(pred[32,2,128]{2,1,0:T(4,128)(4,1)S(1)} %copy.326) | copy-start | bytes 24580
  216.5 389.9 %reduce-scatter.14.cloned.1.call-start = ((), (), s32[]{:S(2)}) async-start(), calls=%async_computation.16 | async-start | bytes 983040 | tf_op jit(solution)/shard_map/reduce_scatter | solution.py:1171
  221.5 13.9 %copy-start.31 = (f32[1,384]{1,0:T(1,128)}, f32[1,384]{1,0:T(1,128)S(1)}, u32[]{:S(2)}) copy-start(f32[1,384]{1,0:T(1,128)S(1)} %reshape.565.gain_ref) | copy-start | bytes 4612
  222.4 76.1 %copy-start.77 = (f32[1536]{0:T(1024)}, f32[1536]{0:T(1024)S(1)}, u32[]{:S(2)}) copy-start(f32[1536]{0:T(1024)S(1)} %get-tuple-element.189) | copy-start | bytes 18436
  226.9 8.5 copy-start.54
  235.4 10.9 %copy-start.4 = (f32[2048,1152]{1,0:T(8,128)}, f32[2048,1152]{1,0:T(8,128)S(1)}, u32[]{:S(2)}) copy-start(f32[2048,1152]{1,0:T(8,128)S(1)} %fusion.4.merged_ref) | copy-start | bytes 28311556
  258.4 37.6 %copy-start.47 = (bf16[2,128,1536]{2,1,0:T(8,128)(2,1)S(1)}, bf16[2,128,1536]{2,1,0:T(8,128)(2,1)}, u32[]{:S(2)}) copy-start(bf16[2,128,1536]{2,1,0:T(8,128)(2,1)} %param.20) | copy-start | bytes 2359300
  298.5 70.4 %copy-start.83 = (f32[256]{0:T(256)}, f32[256]{0:T(256)S(1)}, u32[]{:S(2)}) copy-start(f32[256]{0:T(256)S(1)} %add_rsqrt_fusion.1) | copy-start | bytes 3076
  441.1 179.6 %reduce-scatter.18.cloned.1.call-start = ((), (), s32[]{:S(2)}) async-start(), calls=%async_computation.18 | async-start | bytes 2359296 | tf_op jit(solution)/shard_map/reduce_scatter | solution.py:1335
  472.8 152.5 %reduce-scatter.12.cloned.1.call-start = ((), (), s32[]{:S(2)}) async-start(), calls=%async_computation.15 | async-start | bytes 2359296 | tf_op jit(solution)/shard_map/reduce_scatter | solution.py:1335
  473.6 168.3 %reduce-scatter.10.cloned.1.call-start = ((), (), s32[]{:S(2)}) async-start(), calls=%async_computation.14 | async-start | bytes 4718592 | tf_op jit(solution)/shard_map/reduce_scatter | solution.py:1335
  474.3 14.6 %copy-start.27 = (f32[1280,1]{1,0:T(8,128)S(1)}, f32[1280,1]{1,0:T(8,128)}, u32[]{:S(2)}) copy-start(f32[1280,1]{1,0:T(8,128)} %copy-done.26) | copy-start | bytes 15364
  474.3 256.0 %reduce-scatter.16.cloned.1.call-start = ((), (), s32[]{:S(2)}) async-start(), calls=%async_computation.17 | async-start | bytes 4718592 | tf_op jit(solution)/shard_map/reduce_scatter | solution.py:1335
  528.5 68.7 %copy-start.62 = (f32[256,32]{1,0:T(8,128)S(1)}, f32[256,32]{1,0:T(8,128)}, u32[]{:S(2)}) copy-start(f32[256,32]{1,0:T(8,128)} %copy.334) | copy-start | bytes 98308
  528.5 68.8 %copy-start.74 = (pred[256,32]{1,0:T(8,128)(4,1)S(1)}, pred[256,32]{1,0:T(8,128)(4,1)}, u32[]{:S(2)}) copy-start(pred[256,32]{1,0:T(8,128)(4,1)} %copy.336) | copy-start | bytes 24580
  528.5 68.8 %copy-start.85 = (f32[256]{0:T(256)S(1)}, f32[256]{0:T(256)}, u32[]{:S(2)}) copy-start(f32[256]{0:T(256)} %get-tuple-element.247) | copy-start | bytes 3076
  528.5 71.4 %copy-start.78 = (f32[1536]{0:T(1024)S(1)}, f32[1536]{0:T(1024)}, u32[]{:S(2)}) copy-start(f32[1536]{0:T(1024)} %copy-done.77) | copy-start | bytes 18436
  528.5 71.4 %copy-start.84 = (f32[256]{0:T(256)S(1)}, f32[256]{0:T(256)}, u32[]{:S(2)}) copy-start(f32[256]{0:T(256)} %copy-done.83) | copy-start | bytes 3076
  603.0 6.8 copy-start.93
  606.4 9.6 %all-to-all-start.1 = ((bf16[8,48,256]{2,1,0:T(8,128)(2,1)}), bf16[8,48,256]{2,1,0:T(8,128)(2,1)S(1)}, u32[]{:S(2)}, u32[]{:S(2)}) async-start(bf16[8,48,256]{2,1,0:T(8,128)(2,1)} %bitcast.295), calls=%async_computation.4 | async-start | bytes 393216 | tf_op jit(solution)/shard_map/all_to_all | solution.py:1385
  609.8 297.5 %reduce-scatter.22.cloned.1.call-start = ((), (), s32[]{:S(2)}) async-start(), calls=%async_computation.20 | async-start | bytes 4423680 | tf_op jit(solution)/shard_map/reduce_scatter | solution.py:1171
  622.6 103.6 %collective-permute-start.4 = (bf16[128,1536]{1,0:T(8,128)(2,1)}, bf16[128,1536]{1,0:T(8,128)(2,1)S(1)}, u32[]{:S(2)}, u32[]{:S(2)}) collective-permute-start(bf16[128,1536]{1,0:T(8,128)(2,1)} %broadcast_select_fusion.10), channel_id=1, source_target_pairs={{0,8},{8,0},{16,24},{24,16},{1,9},{9,1},{17,25},{25,17},{2,10},{10... | collective-permute-start | bytes 1179656 | tf_op jit(solution)/shard_map/ppermute | solution.py:815
  627.3 99.9 %collective-permute-start.2 = (bf16[128,1536]{1,0:T(8,128)(2,1)}, bf16[128,1536]{1,0:T(8,128)(2,1)}, u32[]{:S(2)}, u32[]{:S(2)}) collective-permute-start(bf16[128,1536]{1,0:T(8,128)(2,1)} %broadcast_select_fusion.11), channel_id=1, source_target_pairs={{0,8},{8,0},{16,24},{24,16},{1,9},{9,1},{17,25},{25,17},{2,10},{10... | collective-permute-start | bytes 1179656 | tf_op jit(solution)/shard_map/ppermute | solution.py:815
  641.8 41.2 %slice-start = ((s8[9437184]{0:T(1024)(128)(4,1)}), s8[1048576]{0:T(1024)(128)(4,1)S(1)}, s32[]{:S(2)}) async-start(s8[9437184]{0:T(1024)(128)(4,1)} %bitcast.243), calls=%async_computation.21 | async-start | bytes 2097152
  677.3 6.2 copy-start.18
  677.3 6.2 copy-start.30
  677.3 6.2 copy-start.32
  677.3 6.2 copy-start.34
  677.4 6.2 copy-start.36
  704.9 12.1 %copy-start.37 = (bf16[2048,1152]{1,0:T(8,128)(2,1)}, bf16[2048,1152]{1,0:T(8,128)(2,1)S(1)}, u32[]{:S(2)}) copy-start(bf16[2048,1152]{1,0:T(8,128)(2,1)S(1)} %get-tuple-element.102) | copy-start | bytes 14155780
  725.9 186.5 %reduce-scatter.20.cloned.1.call-start = ((), (), s32[]{:S(2)}) async-start(), calls=%async_computation.19 | async-start | bytes 1966080 | tf_op jit(solution)/shard_map/reduce_scatter | solution.py:1171
  732.8 96.1 %collective-permute-start.3 = (bf16[384,1024]{1,0:T(8,128)(2,1)}, bf16[384,1024]{1,0:T(8,128)(2,1)}, u32[]{:S(2)}, u32[]{:S(2)}) collective-permute-start(bf16[384,1024]{1,0:T(8,128)(2,1)} %broadcast_select_fusion.2), channel_id=1, source_target_pairs={{0,8},{8,0},{16,24},{24,16},{1,9},{9,1},{17,25},{25,17},{2,10},{10... | collective-permute-start | bytes 2359304 | tf_op jit(solution)/shard_map/ppermute | solution.py:815
  733.8 98.7 %collective-permute-start.1 = (bf16[384,1024]{1,0:T(8,128)(2,1)}, bf16[384,1024]{1,0:T(8,128)(2,1)}, u32[]{:S(2)}, u32[]{:S(2)}) collective-permute-start(bf16[384,1024]{1,0:T(8,128)(2,1)} %broadcast_select_fusion.3), channel_id=1, source_target_pairs={{0,8},{8,0},{16,24},{24,16},{1,9},{9,1},{17,25},{25,17},{2,10},{10... | collective-permute-start | bytes 2359304 | tf_op jit(solution)/shard_map/ppermute | solution.py:815
  743.1 82.5 %collective-permute-start.5 = (bf16[2,96,1536]{2,1,0:T(8,128)(2,1)}, bf16[2,96,1536]{2,1,0:T(8,128)(2,1)}, u32[]{:S(2)}, u32[]{:S(2)}) collective-permute-start(bf16[2,96,1536]{2,1,0:T(8,128)(2,1)} %fusion.21), channel_id=1, source_target_pairs={{0,1},{1,0},{2,3},{3,2},{4,5},{5,4},{6,7},{7,6},{8,9},{9,8},{10,11... | collective-permute-start | bytes 1769480 | tf_op jit(solution)/shard_map/ppermute | solution.py:815
  758.0 37.9 %copy-start.22 = (bf16[2048,128]{1,0:T(8,128)(2,1)S(1)}, bf16[2048,128]{1,0:T(8,128)(2,1)}, u32[]{:S(2)}) copy-start(bf16[2048,128]{1,0:T(8,128)(2,1)} %copy-done.20) | copy-start | bytes 1572868
  801.5 23.7 %copy-start.48 = (bf16[2,128,1536]{2,1,0:T(8,128)(2,1)S(1)}, bf16[2,128,1536]{2,1,0:T(8,128)(2,1)}, u32[]{:S(2)}) copy-start(bf16[2,128,1536]{2,1,0:T(8,128)(2,1)} %param.20) | copy-start | bytes 2359300
  907.3 6.7 copy-start.68
  907.3 8.7 copy-start.102
  907.3 17.5 %all-to-all-start.2 = ((bf16[8,48,1152]{2,1,0:T(8,128)(2,1)}), bf16[8,48,1152]{2,1,0:T(8,128)(2,1)S(1)}, u32[]{:S(2)}, u32[]{:S(2)}) async-start(bf16[8,48,1152]{2,1,0:T(8,128)(2,1)} %bitcast.292), calls=%async_computation.7 | async-start | bytes 1769472 | tf_op jit(solution)/shard_map/all_to_all | solution.py:1385
  (85 other events, 188.9 us)
Sparse Core Ops, SparseCore 0:
  10.2 42.7 all-gather.6
  55.2 132.0 all-gather.4
  190.4 114.6 all-gather.8
  306.5 113.1 all-gather.10
  441.2 22.9 reduce-scatter.13
  473.0 43.6 reduce-scatter.17
  519.0 42.8 reduce-scatter.11
  564.7 77.1 reduce-scatter.9
  644.8 76.9 reduce-scatter.15
  726.1 97.6 reduce-scatter.21
  829.1 51.6 reduce-scatter.19

commit v4 on v3

--- a/solution.py
+++ b/solution.py
@@ -824,49 +824,83 @@
     return value
 
 
-def merge_kernel(near, parts, select_ref, *refs):
-    rows_refs, (small_ref, weight_ref), out_ref = refs[:parts], refs[parts : parts + 2], refs[-1]
+def merge_kernel(near, parts, experts, tags, lowest_ref, select_ref, *refs):
+    rows_refs, (small_ref, weight_ref) = refs[:parts], refs[parts : parts + 2]
+    tag_refs, outs = refs[parts + 2 : parts + 2 + tags], refs[len(refs) - 1 - bool(tags) :]
     slots = select_ref.shape[1] // parts
-    total = None
-    for k in range(parts):
-        term = lax.dot_general(
-            select_ref[0, k * slots : (k + 1) * slots, :],
-            rows_refs[k][0],
-            (((0,), (0,)), ((), ())),
-            preferred_element_type=f32,
-        )
-        total = term if total is None else total + term
+    picked = [select_ref[0, k * slots : (k + 1) * slots, :] for k in range(parts)]
+    total = sum(dot_tn(picked[k], rows_refs[k][0]) for k in range(parts))
     first = pl.program_id(0) < near
 
     @pl.when(first)
     def _():
-        out_ref[...] = (total + dot(small_ref[...], weight_ref[...])).astype(b16)
+        outs[0][...] = (total + dot(small_ref[...], weight_ref[...])).astype(b16)
 
     @pl.when(jnp.logical_not(first))
     def _():
-        out_ref[...] = total.astype(b16)
-
-
-def merge(select, parts, small, weight, after=()):
+        outs[0][...] = total.astype(b16)
+
+    if tags:
+        lane = lax.broadcasted_iota(jnp.int32, (slots, LANES), 1)
+        tail = jnp.zeros((LEN, LANES), f32)
+        for k in range(tags):
+            value = jnp.broadcast_to(tag_refs[k][0], (slots, LANES))
+            high = value.astype(b16)
+            fine = (value - high.astype(f32)).astype(b16)
+            column = lowest_ref[0] + k
+            wide = jnp.where(
+                lane == column,
+                high.astype(f32),
+                jnp.where(lane == column + experts, fine.astype(f32), 0.0),
+            )
+            tail = tail + dot_tn(picked[k], wide.astype(b16))
+        outs[1][...] = tail.astype(b16)
+
+
+def merge(select, parts, small, weight, experts=0, lowest=None, tags=(), after=()):
     seqs, slots, unused = select.shape
     slots = slots // len(parts)
     width = weight.shape[1]
     near = small.shape[0] // LEN
+    each = lambda n: pl.BlockSpec((1, slots, n), lambda s, low: (s, 0, 0))
+    token = lambda n: pl.BlockSpec((LEN, n), lambda s, low: (s, 0))
+    lowest = jnp.zeros((1,), jnp.int32) if lowest is None else lowest.reshape(1)
+    outs = [jax.ShapeDtypeStruct((seqs * LEN, width), b16)]
+    outs += [jax.ShapeDtypeStruct((seqs * LEN, LANES), b16)] if tags else []
+
+    def kernel(*refs):
+        used = 2 + len(parts) + 2 + len(tags)
+        merge_kernel(near, len(parts), experts, len(tags), *refs[:used], *refs[used + len(after) :])
+
     return pl.pallas_call(
-        partial(merge_kernel, near, len(parts)),
-        grid=(seqs,),
-        in_specs=[pl.BlockSpec((1,) + select.shape[1:], lambda s: (s, 0, 0))]
-        + [pl.BlockSpec((1, slots, width), lambda s: (s, 0, 0))] * len(parts)
-        + [
-            pl.BlockSpec((LEN, small.shape[1]), lambda s: (jnp.minimum(s, near - 1), 0)),
-            fixed(*weight.shape),
-        ]
-        + [pl.BlockSpec(memory_space=pl.ANY)] * len(after),
-        out_specs=rows_of(width),
-        out_shape=jax.ShapeDtypeStruct((seqs * LEN, width), b16),
+        kernel,
+        grid_spec=pltpu.PrefetchScalarGridSpec(
+            num_scalar_prefetch=1,
+            grid=(seqs,),
+            in_specs=[pl.BlockSpec((1,) + select.shape[1:], lambda s, low: (s, 0, 0))]
+            + [each(width)] * len(parts)
+            + [
+                pl.BlockSpec(
+                    (LEN, small.shape[1]), lambda s, low: (jnp.minimum(s, near - 1), 0)
+                ),
+                pl.BlockSpec(weight.shape, lambda s, low: (0, 0)),
+            ]
+            + [each(1)] * len(tags)
+            + [pl.BlockSpec(memory_space=pl.ANY)] * len(after),
+            out_specs=[token(v.shape[1]) for v in outs],
+        ),
+        out_shape=outs,
         compiler_params=pltpu.CompilerParams(vmem_limit_bytes=32 << 20),
         cost_estimate=pl.CostEstimate(flops=0, bytes_accessed=1024, transcendentals=0),
-    )(select, *[v.reshape(seqs, slots, width) for v in parts], small, weight, *after)
+    )(
+        lowest,
+        select,
+        *[v.reshape(seqs, slots, width) for v in parts],
+        small,
+        weight,
+        *[v.reshape(seqs, slots, 1) for v in tags],
+        *after,
+    )
 
 
 def spread_kernel(parts, select_ref, rows_ref, *out_refs):
@@ -1329,7 +1363,7 @@
             )
         outs.append(out)
         backs.append(grad)
-        dgates.append(dgate.reshape(seqs, slots))
+        dgates.append(dgate)
         sums.append(
             [
                 lax.psum_scatter(
@@ -1343,18 +1377,11 @@
                 all_routed, all_grad, gate_up, down_w, near, after=made_grads
             )
             tied = [hid, dpre, shared_grad, down_grad]
-    dgate_rows = jnp.sum(
-        jnp.where(chosen, jnp.stack(dgates, axis=1)[:, :, :, None], 0.0), axis=2
-    ).transpose(0, 2, 1)
-    dgate_wide = lax.dynamic_update_slice_in_dim(
-        jnp.zeros((count, experts), f32), dgate_rows.reshape(count, taken), lowest, axis=1
-    )
-    high = dgate_wide.astype(b16)
-    fine = (dgate_wide - high.astype(f32)).astype(b16)
-    fill = jnp.zeros((count, -(2 * experts) % LANES), b16)
-    back_part = merge(select, backs, dpre, gate_up.T)
+    back_part, back_gates = merge(
+        select, backs, dpre, gate_up.T, experts, lowest, tags=dgates
+    )
     back, back_gates = plane_scatter(
-        4, back_part, jnp.concatenate([high, fine, fill], axis=1), sets=sets, after=made_grads
+        4, back_part, back_gates, sets=sets, after=made_grads
     )
 
     gates = dense_gates(dot(routed, route_proj), routes.reshape(tokens, picks))
@@ -1380,17 +1407,13 @@
         rows = jnp.concatenate([taps, head_rows], axis=0)
         return jnp.pad(rows, ((0, 16 - rows.shape[0]), (0, 0)))
 
-    def owners(grad):
-        grad = scatter(grad.astype(b16), "dp").reshape(plane, shard, -1)
-        return lax.all_to_all(grad, "expert", split_axis=0, concat_axis=0, tiled=True).astype(f32)
-
     scaled = (dmid * scale).astype(b16)
     inward = scale * jnp.sum(scaled.astype(f32) * mixer_out, axis=1, keepdims=True) / inner
     inward_high = inward.astype(b16)
     inward_low = (inward - inward_high.astype(f32)).astype(b16)
     tail = jnp.where(lane == 0, inward_high, jnp.where(lane == 1, inward_low, 0)).astype(b16)
-    shared_rows = owners(shared_grad)
-    all_mid, all_inward = plane_gather(6, scaled, tail, after=sums[0])
+    shared_sum = scatter(shared_grad, "dp")
+    all_mid, all_inward = plane_gather(6, scaled, tail, after=sums[0][1:])
     kept, sent = [], []
     if sets == 2:
         for group in sums:
@@ -1408,15 +1431,14 @@
         7,
         dot_nt(dmerged, in_w).astype(b16),
         gathers=[taps_of],
-        after=[shared_rows],
+        after=[shared_sum],
     )
     taps_of = jnp.sum(taps_of, axis=0)
-    out_part = merge(select, outs, hid, down_w, after=[dnormed])
+    out_part = merge(select, outs, hid, down_w, after=[dnormed])[0]
     out_part, dnormed = tie(out_part, dnormed)
     out_sum, small = plane_scatter(5, out_part, sets=sets, lines=[taps_of], after=swapped)
     small = jnp.sum(small, axis=0)
 
-    shared_grad = shared_rows
     unsplit = lambda v: (
         v.reshape(plane, shard, planes, hr).transpose(1, 2, 0, 3).reshape(shard, planes * plane * hr)
     )
@@ -1447,7 +1469,11 @@
     )
     in_w_grad = dot_tn(normed, dmerged)
     in_w_grad = jnp.concatenate([in_w_grad[:, :-LANES], in_w_grad[:, -LANES:] + extra], axis=1)
-    in_w_grad = owners(in_w_grad)
+    in_w_grad = jnp.concatenate([scatter(in_w_grad.astype(b16), "dp"), shared_sum], axis=1)
+    in_w_grad = lax.all_to_all(
+        in_w_grad.reshape(plane, shard, -1), "expert", split_axis=0, concat_axis=0, tiled=True
+    ).astype(f32)
+    in_w_grad, shared_grad = in_w_grad[:, :, :main], in_w_grad[:, :, main:]
     by_row = in_w_grad.transpose(1, 0, 2)
     step_part = 2 * wide + states
     in_grad = jnp.concatenate(

time: 949 us -> 996 us (1.050)
  waiting for transfers between devices: 34.9 us -> 91.8 us
  Pallas kernels: 604 us -> 619 us
  local copies, waits for them, and re-layouts: 111 us -> 97.2 us
    ppermute x6, waiting for transfers between devices: 0.02 us -> 77 us  [exchange(): return lax.ppermute(value, axis, [(i, i ^ distance) for i in range(size)])]
    reduce_scatter x4, waiting for transfers between devices: 14.6 us -> 0.01 us  [body(): lax.psum_scatter(v, 'dp', scatter_dimension=0, tiled=True, axis_index_gro...]
    unnamed x224 -> x228, local copies, waits for them, and re-layouts: 65.3 us -> 58.2 us
  transfers between devices with their start and end apart: 19 -> 18, of which waited for: 4 -> 4; matrix products, arithmetic and copies ran while one was open for 19% -> 16% of each run, Pallas kernels for 64% -> 60%
where the time goes in v4:
time: 996 us; the launch traced here: 987 us
  Pallas kernels  619 us (62%)
  local copies, waits for them, and re-layouts  97.2 us (10%)
  waiting for transfers between devices  91.8 us (9%)
  other arithmetic  71.6 us (7%)
  matrix products  60.7 us (6%)
  blocking collectives  20.7 us (2%)
  between operations  16.2 us (2%)
    pallas_call x3, Pallas kernels, plane_gather(): pl.pallas_call(partial(gather_kernel, sets, count, len(swaps), len(lines)...  245 us
    pallas_call x4, Pallas kernels, plane_scatter(): pl.pallas_call(partial(scatter_kernel, sets, count, len(swaps), len(gathe...  210 us
    ppermute x6, waiting for transfers between devices, exchange(): return lax.ppermute(value, axis, [(i, i ^ distance) for i in range(size)])  77 us
    unnamed x228, local copies, waits for them, and re-layouts  58.2 us
    pallas_call x2, Pallas kernels, expert(): pl.pallas_call(kernel, grid=(rows // block,), in_specs=[per, per, one, pl...  54.7 us
    pallas_call x2, Pallas kernels, merge(): pl.pallas_call(kernel, grid_spec=pltpu.PrefetchScalarGridSpec(num_scalar_...  46.9 us
    dot_general x4, matrix products, dot(): return jnp.dot(a, b, preferred_element_type=f32)  23.2 us
    pallas_call x1, Pallas kernels, mix_backward(): pl.pallas_call(partial(backward_kernel, width // LANES), grid=(tokens //...  21.4 us
  transfers between devices with their start and end apart: 18, of which 4 were waited for; matrix products, arithmetic and copies ran while one was open for 16% of the time, Pallas kernels for 60%

profile of v4, /device:TPU:0, one launch (start us, length us, event | category | flops | bytes accessed | tf_op | source)
XLA Modules:
  0.0 986.8 jit_solution(13861658494752915223)
XLA Ops:
  14.9 20.7 %all_to_all.10 = bf16[8,48,1408]{2,1,0:T(8,128)(2,1)S(1)} all-to-all(bf16[8,48,1408]{2,1,0:T(8,128)(2,1)S(1)} %bitcast.272), channel_id=1, replica_groups=mesh['dp'=4,'expert'=8] {'expert'}, dimensions={0} | all-to-all | bytes 2162688 | tf_op jit(solution)/shard_map/all_to_all | solution.py:1232
  37.9 5.0 shard_map.339.refs_3_
  42.9 147.3 %shard_map.340 = (bf16[8,256,1536]{2,1,0:T(8,128)(2,1)}, bf16[16,256,1536]{2,1,0:T(8,128)(2,1)}, bf16[16,256,128]{2,1,0:T(8,128)(2,1)}, bf16[2,384,1536]{2,1,0:T(8,128)(2,1)}, bf16[2,384,1536]{2,1,0:T(8,128)(2,1)}) custom-call(bf16[256,1536]{1,0:T(8,128)(2,1)} %bitcast.258, bf16[256,1536]{1,0:T(8,128)(2,1)} %bitcast.262, bf16[256,128]{1,0:T(8,128)(2,1)} %pad.29.refs_2_, ...), custom_call_target="tpu_custom_call" | custom-call | bytes 1024 | tf_op jit(solution)/shard_map/pallas_call | solution.py:472
  192.9 4.1 multiply_reduce_fusion
  197.0 2.4 broadcast_select_fusion.4
  200.7 5.4 copy-done.2
  206.1 6.9 shard_map.345
  220.9 4.4 fusion.1
  225.4 8.5 fusion.4.merged_ref
  233.9 11.1 %shard_map.341 = (bf16[2048,384]{1,0:T(8,128)(2,1)S(1)}, f32[2048,384]{1,0:T(8,128)S(1)}, f32[2048,128]{1,0:T(8,128)S(1)}) custom-call(f32[2048,1152]{1,0:T(8,128)S(1)} %fusion.4.merged_ref, f32[4,640]{1,0:T(4,128)S(1)} %maximum_convert_fusion.1.weight_ref, f32[1,640]{1,0:T(1,128)S(1)} %maximum_convert_fusion.2.bias_ref, ...), custom_call_target="tpu_custom_call" | custom-call | bytes 1024 | tf_op jit(solution)/shard_map/pallas_call | solution.py:243
  249.6 6.8 convolution_convert_fusion.1
  256.4 36.6 %shard_map.342 = (f32[256,1536]{1,0:T(8,128)}, f32[256,128]{1,0:T(8,128)}) custom-call(bf16[8,256,1536]{2,1,0:T(8,128)(2,1)} %bitcast.265, bf16[8,256,128]{2,1,0:T(8,128)(2,1)} %select_select_fusion.refs_1_), custom_call_target="tpu_custom_call" | custom-call | bytes 1024 | tf_op jit(solution)/shard_map/pallas_call | solution.py:749
  294.1 2.4 multiply_reduce_fusion.4
  298.7 6.3 all-gather.9.cloned.1.call-done.refs_3_
  305.1 63.9 %shard_map.343 = bf16[16,256,1536]{2,1,0:T(8,128)(2,1)} custom-call(bf16[256,1536]{1,0:T(8,128)(2,1)} %multiply_convert_fusion.1.refs_0_), custom_call_target="tpu_custom_call" | custom-call | bytes 1024 | tf_op jit(solution)/shard_map/pallas_call | solution.py:472
  369.0 4.6 copy-done
  373.5 6.9 shard_map.344
  380.5 4.9 select_reduce_fusion.1
  390.5 27.0 %shard_map.346 = (bf16[1280,1536]{1,0:T(8,128)(2,1)}, bf16[1280,1536]{1,0:T(8,128)(2,1)}, f32[1280,1]{1,0:T(8,128)S(1)}, bf16[1536,1024]{1,0:T(8,128)(2,1)S(1)}, bf16[512,1536]{1,0:T(8,128)(2,1)}) custom-call(bf16[1280,1536]{1,0:T(8,128)(2,1)} %bitcast.247, bf16[1280,1536]{1,0:T(8,128)(2,1)} %bitcast.244, f32[1280,1]{1,0:T(8,128)S(1)} %reshape_squeeze.8.refs_2_, ...), custom_call_target="tpu_custom_call" | custom-call | bytes 1024 | tf_op jit(solution)/shard_map/pallas_call | solution.py:993
  419.9 4.6 copy-done.1
  427.5 11.0 %shard_map.347 = (bf16[2048,128]{1,0:T(8,128)(2,1)S(1)}, bf16[2048,256]{1,0:T(8,128)(2,1)S(1)}, bf16[1536,256]{1,0:T(8,128)(2,1)}, bf16[128,1536]{1,0:T(8,128)(2,1)S(1)}) custom-call(bf16[4096,1536]{1,0:T(8,128)(2,1)S(1)} %bitcast.237, bf16[4096,1536]{1,0:T(8,128)(2,1)} %bitcast.238, bf16[1536,256]{1,0:T(8,128)(2,1)S(1)} %copy-done.18, ...), custom_call_target="tpu_custom_call" | custom-call | bytes 1024 | tf_op jit(solution)/shard_map/pallas_call | solution.py:1059
  442.1 27.8 %shard_map.348 = (bf16[1280,1536]{1,0:T(8,128)(2,1)}, bf16[1280,1536]{1,0:T(8,128)(2,1)}, f32[1280,1]{1,0:T(8,128)S(1)}, bf16[1536,1024]{1,0:T(8,128)(2,1)}, bf16[512,1536]{1,0:T(8,128)(2,1)}) custom-call(bf16[1280,1536]{1,0:T(8,128)(2,1)} %bitcast.249, bf16[1280,1536]{1,0:T(8,128)(2,1)} %bitcast.248, f32[1280,1]{1,0:T(8,128)S(1)} %reshape_squeeze.9.refs_2_, ...), custom_call_target="tpu_custom_call" | custom-call | bytes 1024 | tf_op jit(solution)/shard_map/pallas_call | solution.py:993
  475.7 3.1 select_reduce_fusion.2
  485.6 25.6 %shard_map.349 = (bf16[4096,1536]{1,0:T(8,128)(2,1)}, bf16[4096,128]{1,0:T(8,128)(2,1)S(1)}) custom-call(s32[1]{0:T(128)} %bitcast.53.refs_0_, bf16[32,80,128]{2,1,0:T(8,128)(2,1)S(1)} %fusion.15.select_ref.refs_1_, bf16[32,40,1536]{2,1,0:T(8,128)(2,1)S(1)} %bitcast.245, bf16[32,40,1536]{2,1,0:T(8,128)(2,1)S(1)} %bitcast.246, ...), custom_call_target="tpu_custom_call" | custom-call | bytes 1024 | tf_op jit(solution)/shard_map/pallas_call | solution.py:875
  512.2 79.3 %shard_map.350 = (f32[256,1536]{1,0:T(8,128)}, f32[256,128]{1,0:T(8,128)}) custom-call(bf16[16,256,1536]{2,1,0:T(8,128)(2,1)} %bitcast.257, bf16[16,256,128]{2,1,0:T(8,128)(2,1)} %bitcast.253, bf16[1536,1024]{1,0:T(8,128)(2,1)} %get-tuple-element.100.refs_2_, bf16[512,1536]{1,0:T(8,128)(2,1)} %get-tuple-element.101.refs_3_), custom_call_target="tpu_custom_call" | custom-call | bytes 1024 | tf_op jit(solution)/shard_map/pallas_call | solution.py:749
  594.3 2.2 multiply_reduce_fusion.1
  602.0 33.9 %shard_map.351 = (bf16[8,256,1536]{2,1,0:T(8,128)(2,1)}, bf16[8,256,128]{2,1,0:T(8,128)(2,1)}) custom-call(bf16[256,1536]{1,0:T(8,128)(2,1)} %get-tuple-element.204.refs_0_, bf16[256,128]{1,0:T(8,128)(2,1)} %select_select_fusion.1.refs_1_, bf16[256,1536]{1,0:T(8,128)(2,1)} %reduce-scatter.10.cloned.1.call-done.refs_2_), custom_call_target="tpu_custom_call" | custom-call | bytes 1024 | tf_op jit(solution)/shard_map/pallas_call | solution.py:472
  635.9 5.6 convolution_convert_fusion.2
  643.1 3.6 fusion.16.grad_ref
  649.8 21.4 %shard_map.352 = (bf16[2048,1152]{1,0:T(8,128)(2,1)S(1)}, f32[4,640]{1,0:T(4,128)S(1)}, f32[1,640]{1,0:T(1,128)S(1)}, f32[1,384]{1,0:T(1,128)S(1)}, f32[8,128]{1,0:T(8,128)S(1)}) custom-call(f32[2048,1152]{1,0:T(8,128)S(1)} %bitcast.241, f32[2048,384]{1,0:T(8,128)S(1)} %copy-done.17, f32[2048,384]{1,0:T(8,128)S(1)} %fusion.16.grad_ref, ...), custom_call_target="tpu_custom_call" | custom-call | bytes 1024 | tf_op jit(solution)/shard_map/pallas_call | solution.py:263
  674.0 11.9 %fusion.49 = f32[1536,1152]{0,1:T(8,128)S(1)} fusion(bf16[2048,1536]{1,0:T(8,128)(2,1)} %copy-done.53, bf16[2048,1152]{1,0:T(8,128)(2,1)} %copy-done.38), kind=kOutput, calls=%fused_computation.183 | convolution fusion | flops 7247757312 | bytes 18087936 | tf_op jit(solution)/shard_map/dot_general | solution.py:792
  689.0 5.8 copy.336
  696.5 13.2 %convolution_convert_fusion = bf16[2048,1536]{1,0:T(8,128)(2,1)} fusion(bf16[2048,1152]{1,0:T(8,128)(2,1)} %copy-done.38, bf16[1536,1408]{0,1:T(8,128)(2,1)} %all-gather.5.cloned.1.call-done), kind=kOutput, calls=%fused_computation.4 | convolution fusion | flops 7250903040 | bytes 14548992 | tf_op jit(solution)/shard_map/dot_general | solution.py:788
  709.6 37.1 %shard_map.353 = (f32[256,1536]{1,0:T(8,128)}, f32[8,16,3328]{2,1,0:T(8,128)}) custom-call(bf16[8,256,1536]{2,1,0:T(8,128)(2,1)} %bitcast.263, f32[16,3328]{1,0:T(8,128)} %pad.35.refs_1_, bf16[384,256]{1,0:T(8,128)(2,1)} %reduce-scatter.12.cloned.1.call-done.refs_2_), custom_call_target="tpu_custom_call" | custom-call | bytes 1024 | tf_op jit(solution)/shard_map/pallas_call | solution.py:749
  748.1 2.2 copy-done.8
  752.5 21.3 %shard_map.354 = bf16[4096,1536]{1,0:T(8,128)(2,1)} custom-call(s32[1]{0:T(128)} %constant.84.clone.1.refs_0_, bf16[32,80,128]{2,1,0:T(8,128)(2,1)S(1)} %fusion.15.select_ref.refs_1_, bf16[32,40,1536]{2,1,0:T(8,128)(2,1)S(1)} %bitcast.242, bf16[32,40,1536]{2,1,0:T(8,128)(2,1)S(1)} %bitcast.243, bf16[2048,128]{1,0:T(8,128)(2,1)S(1)} %copy-done.21, ...), custom_call_target="tpu_custom_call" | custom-call | bytes 1024 | tf_op jit(solution)/shard_map/pallas_call | solution.py:875
  773.8 2.4 reduce_sum.198.refs_1_
  781.3 2.3 broadcast_select_fusion.2
  784.7 2.3 broadcast_select_fusion.3
  788.0 3.3 maximum_convert_fusion
  795.4 21.3 %collective-permute-done.3.refs_4_ = bf16[384,1024]{1,0:T(8,128)(2,1)} collective-permute-done((bf16[384,1024]{1,0:T(8,128)(2,1)}, bf16[384,1024]{1,0:T(8,128)(2,1)}, u32[]{:S(2)}, u32[]{:S(2)}) %collective-permute-start.3) | collective-permute-done | bytes 786464 | tf_op jit(solution)/shard_map/ppermute | solution.py:815
  816.8 55.6 %collective-permute-done.1.refs_2_ = bf16[384,1024]{1,0:T(8,128)(2,1)} collective-permute-done((bf16[384,1024]{1,0:T(8,128)(2,1)}, bf16[384,1024]{1,0:T(8,128)(2,1)}, u32[]{:S(2)}, u32[]{:S(2)}) %collective-permute-start.1) | collective-permute-done | bytes 786464 | tf_op jit(solution)/shard_map/ppermute | solution.py:815
  872.4 57.1 %shard_map.355 = (f32[256,1536]{1,0:T(8,128)}, f32[4,16,3328]{2,1,0:T(8,128)}) custom-call(bf16[16,256,1536]{2,1,0:T(8,128)(2,1)} %bitcast.256, f32[16,3328]{1,0:T(8,128)} %reduce_sum.198.refs_1_, bf16[384,1024]{1,0:T(8,128)(2,1)} %collective-permute-done.1.refs_2_, bf16[128,1536]{1,0:T(8,128)(2,1)} %collective-permute-done.2.refs_3_, ...), custom_call_target="tpu_custom_call" | custom-call | bytes 1024 | tf_op jit(solution)/shard_map/pallas_call | solution.py:749
  942.6 2.2 pad_maximum_fusion.6
  944.8 4.5 all-to-all-start.1
  949.3 4.0 pad_maximum_fusion.1
  956.4 2.3 fusion.11
  958.6 6.4 all-to-all-done.1
  (459 shorter events, 122.3 us)
Async XLA Ops:
  7.2 189.8 %all-gather.7.cloned.1.call-start = ((), (), s32[]{:S(2)}) async-start(), calls=%async_computation.10 | async-start | bytes 2129920 | tf_op jit(solution)/shard_map/all_gather | solution.py:1204
  9.9 210.0 %all-gather.5.cloned.1.call-start = ((), (), s32[]{:S(2)}) async-start(), calls=%async_computation.9 | async-start | bytes 5406720 | tf_op jit(solution)/shard_map/all_gather | solution.py:1204
  37.0 268.0 %all-gather.9.cloned.1.call-start = ((), (), s32[]{:S(2)}) async-start(), calls=%async_computation.11 | async-start | bytes 7077888 | tf_op jit(solution)/shard_map/all_gather | solution.py:1325
  190.3 249.8 %all-gather.11.cloned.1.call-start = ((), (), s32[]{:S(2)}) async-start(), calls=%async_computation.12 | async-start | bytes 7077888 | tf_op jit(solution)/shard_map/all_gather | solution.py:1325
  192.3 41.6 %copy-start.34 = (f32[1,128]{1,0:T(1,128)}, f32[1,128]{1,0:T(1,128)S(1)}, u32[]{:S(2)}) copy-start(f32[1,128]{1,0:T(1,128)S(1)} %bitcast_convert_fusion.rate_ref) | copy-start | bytes 1540
  192.3 41.5 %copy-start.36 = (f32[1,128]{1,0:T(1,128)}, f32[1,128]{1,0:T(1,128)S(1)}, u32[]{:S(2)}) copy-start(f32[1,128]{1,0:T(1,128)S(1)} %bitcast_convert_fusion.1.step_ref) | copy-start | bytes 1540
  192.8 41.0 %copy-start.30 = (f32[1,384]{1,0:T(1,128)}, f32[1,384]{1,0:T(1,128)S(1)}, u32[]{:S(2)}) copy-start(f32[1,384]{1,0:T(1,128)S(1)} %dynamic-slice_convert_fusion.skip_ref) | copy-start | bytes 4612
  199.5 18.9 %collective-permute-start = (bf16[2,96,1664]{2,1,0:T(8,128)(2,1)}, bf16[2,96,1664]{2,1,0:T(8,128)(2,1)}, u32[]{:S(2)}, u32[]{:S(2)}) collective-permute-start(bf16[2,96,1664]{2,1,0:T(8,128)(2,1)} %broadcast_select_fusion.4), channel_id=1, source_target_pairs={{0,1},{1,0},{2,3},{3,2},{4,5},{5,4},{6,7},{7,6},{8,9},{9,8},{10,11... | collective-permute-start | bytes 1916936 | tf_op jit(solution)/shard_map/ppermute | solution.py:815
  200.3 12.7 %copy-start.71 = (s32[32,2,128]{2,1,0:T(2,128)}, s32[32,2,128]{2,1,0:T(2,128)S(1)}, u32[]{:S(2)}) copy-start(s32[32,2,128]{2,1,0:T(2,128)S(1)} %copy.308) | copy-start | bytes 98308
  200.4 12.7 %copy-start.76 = (pred[32,2,128]{2,1,0:T(4,128)(4,1)}, pred[32,2,128]{2,1,0:T(4,128)(4,1)S(1)}, u32[]{:S(2)}) copy-start(pred[32,2,128]{2,1,0:T(4,128)(4,1)S(1)} %copy.309) | copy-start | bytes 24580
  216.9 383.0 %reduce-scatter.18.cloned.1.call-start = ((), (), s32[]{:S(2)}) async-start(), calls=%async_computation.17 | async-start | bytes 2359296 | tf_op jit(solution)/shard_map/reduce_scatter | solution.py:1369
  219.8 29.8 %copy-start.63 = (bf16[2,2,96,1664]{3,2,1,0:T(8,128)(2,1)}, bf16[2,2,96,1664]{3,2,1,0:T(8,128)(2,1)S(1)}, u32[]{:S(2)}) copy-start(bf16[2,2,96,1664]{3,2,1,0:T(8,128)(2,1)S(1)} %pad_maximum_fusion.4) | copy-start | bytes 3833860
  219.9 13.9 %copy-start.32 = (f32[1,384]{1,0:T(1,128)}, f32[1,384]{1,0:T(1,128)S(1)}, u32[]{:S(2)}) copy-start(f32[1,384]{1,0:T(1,128)S(1)} %reshape.568.gain_ref) | copy-start | bytes 4612
  220.9 75.6 %copy-start.74 = (f32[1536]{0:T(1024)}, f32[1536]{0:T(1024)S(1)}, u32[]{:S(2)}) copy-start(f32[1536]{0:T(1024)S(1)} %get-tuple-element.193) | copy-start | bytes 18436
  225.3 8.5 copy-start.53
  233.9 11.1 %copy-start.3 = (f32[2048,1152]{1,0:T(8,128)}, f32[2048,1152]{1,0:T(8,128)S(1)}, u32[]{:S(2)}) copy-start(f32[2048,1152]{1,0:T(8,128)S(1)} %fusion.4.merged_ref) | copy-start | bytes 28311556
  233.9 14.3 %copy-start.94 = (pred[128]{0:T(512)(128)(4,1)S(1)}, pred[128]{0:T(512)(128)(4,1)}, u32[]{:S(2)}) copy-start(pred[128]{0:T(512)(128)(4,1)} %get-tuple-element.254) | copy-start | bytes 388
  233.9 14.3 %copy-start.95 = (pred[128]{0:T(512)(128)(4,1)S(1)}, pred[128]{0:T(512)(128)(4,1)}, u32[]{:S(2)}) copy-start(pred[128]{0:T(512)(128)(4,1)} %get-tuple-element.255) | copy-start | bytes 388
  256.4 37.7 %copy-start.46 = (bf16[2,128,1536]{2,1,0:T(8,128)(2,1)S(1)}, bf16[2,128,1536]{2,1,0:T(8,128)(2,1)}, u32[]{:S(2)}) copy-start(bf16[2,128,1536]{2,1,0:T(8,128)(2,1)} %param.20) | copy-start | bytes 2359300
  470.8 131.2 %reduce-scatter.10.cloned.1.call-start = ((), (), s32[]{:S(2)}) async-start(), calls=%async_computation.13 | async-start | bytes 2359296 | tf_op jit(solution)/shard_map/reduce_scatter | solution.py:1369
  471.3 238.3 %reduce-scatter.12.cloned.1.call-start = ((), (), s32[]{:S(2)}) async-start(), calls=%async_computation.14 | async-start | bytes 983040 | tf_op jit(solution)/shard_map/reduce_scatter | solution.py:1205
  472.1 309.2 %reduce-scatter.16.cloned.1.call-start = ((), (), s32[]{:S(2)}) async-start(), calls=%async_computation.16 | async-start | bytes 4718592 | tf_op jit(solution)/shard_map/reduce_scatter | solution.py:1369
  472.8 311.9 %reduce-scatter.14.cloned.1.call-start = ((), (), s32[]{:S(2)}) async-start(), calls=%async_computation.15 | async-start | bytes 4718592 | tf_op jit(solution)/shard_map/reduce_scatter | solution.py:1369
  475.6 315.6 %reduce-scatter.20.cloned.1.call-start = ((), (), s32[]{:S(2)}) async-start(), calls=%async_computation.18 | async-start | bytes 1966080 | tf_op jit(solution)/shard_map/reduce_scatter | solution.py:1205
  512.2 79.4 %copy-start.61 = (f32[256,32]{1,0:T(8,128)S(1)}, f32[256,32]{1,0:T(8,128)}, u32[]{:S(2)}) copy-start(f32[256,32]{1,0:T(8,128)} %copy.314) | copy-start | bytes 98308
  512.2 79.4 %copy-start.70 = (pred[256,32]{1,0:T(8,128)(4,1)S(1)}, pred[256,32]{1,0:T(8,128)(4,1)}, u32[]{:S(2)}) copy-start(pred[256,32]{1,0:T(8,128)(4,1)} %copy.316) | copy-start | bytes 24580
  512.2 79.4 %copy-start.85 = (f32[256]{0:T(256)S(1)}, f32[256]{0:T(256)}, u32[]{:S(2)}) copy-start(f32[256]{0:T(256)} %get-tuple-element.249) | copy-start | bytes 3076
  512.2 82.0 %copy-start.42 = (f32[256,1536]{1,0:T(8,128)S(1)}, f32[256,1536]{1,0:T(8,128)}, u32[]{:S(2)}) copy-start(f32[256,1536]{1,0:T(8,128)} %copy-done.41) | copy-start | bytes 4718596
  512.2 82.0 %copy-start.75 = (f32[1536]{0:T(1024)S(1)}, f32[1536]{0:T(1024)}, u32[]{:S(2)}) copy-start(f32[1536]{0:T(1024)} %copy-done.74) | copy-start | bytes 18436
  512.2 82.0 %copy-start.84 = (f32[256]{0:T(256)S(1)}, f32[256]{0:T(256)}, u32[]{:S(2)}) copy-start(f32[256]{0:T(256)} %copy-done.83) | copy-start | bytes 3076
  600.0 35.9 %copy-start.40 = (bf16[2048,384]{1,0:T(8,128)(2,1)S(1)}, bf16[2048,384]{1,0:T(8,128)(2,1)}, u32[]{:S(2)}) copy-start(bf16[2048,384]{1,0:T(8,128)(2,1)} %copy-done.39) | copy-start | bytes 4718596
  602.0 174.6 %collective-permute-start.4 = (bf16[128,1536]{1,0:T(8,128)(2,1)}, bf16[128,1536]{1,0:T(8,128)(2,1)}, u32[]{:S(2)}, u32[]{:S(2)}) collective-permute-start(bf16[128,1536]{1,0:T(8,128)(2,1)} %broadcast_select_fusion.10), channel_id=1, source_target_pairs={{0,8},{8,0},{16,24},{24,16},{1,9},{9,1},{17,25},{25,17},{2,10},{10... | collective-permute-start | bytes 1179656 | tf_op jit(solution)/shard_map/ppermute | solution.py:815
  635.9 6.2 copy-start.107
  641.5 8.2 slice-start
  641.6 8.2 slice-start.1
  641.6 8.2 slice-start.2
  641.6 29.7 %collective-permute-start.5 = (bf16[2,96,1536]{2,1,0:T(8,128)(2,1)S(1)}, bf16[2,96,1536]{2,1,0:T(8,128)(2,1)S(1)}, u32[]{:S(2)}, u32[]{:S(2)}) collective-permute-start(bf16[2,96,1536]{2,1,0:T(8,128)(2,1)S(1)} %fusion.21), channel_id=1, source_target_pairs={{0,1},{1,0},{2,3},{3,2},{4,5},{5,4},{6,7},{7,6},{8,9},{9,8},{10,11... | collective-permute-start | bytes 1769480 | tf_op jit(solution)/shard_map/ppermute | solution.py:815
  643.1 6.5 copy-start.60
  647.5 131.8 %collective-permute-start.2 = (bf16[128,1536]{1,0:T(8,128)(2,1)}, bf16[128,1536]{1,0:T(8,128)(2,1)}, u32[]{:S(2)}, u32[]{:S(2)}) collective-permute-start(bf16[128,1536]{1,0:T(8,128)(2,1)} %broadcast_select_fusion.11), channel_id=1, source_target_pairs={{0,8},{8,0},{16,24},{24,16},{1,9},{9,1},{17,25},{25,17},{2,10},{10... | collective-permute-start | bytes 1179656 | tf_op jit(solution)/shard_map/ppermute | solution.py:815
  674.0 268.6 %reduce-scatter.22.cloned.1.call-start = ((), (), s32[]{:S(2)}) async-start(), calls=%async_computation.19 | async-start | bytes 4423680 | tf_op jit(solution)/shard_map/reduce_scatter | solution.py:1205
  709.6 37.1 %copy-start.21 = (bf16[2048,128]{1,0:T(8,128)(2,1)S(1)}, bf16[2048,128]{1,0:T(8,128)(2,1)}, u32[]{:S(2)}) copy-start(bf16[2048,128]{1,0:T(8,128)(2,1)} %copy-done.19) | copy-start | bytes 1572868
  752.5 23.7 %copy-start.47 = (bf16[2,128,1536]{2,1,0:T(8,128)(2,1)S(1)}, bf16[2,128,1536]{2,1,0:T(8,128)(2,1)}, u32[]{:S(2)}) copy-start(bf16[2,128,1536]{2,1,0:T(8,128)(2,1)} %param.20) | copy-start | bytes 2359300
  783.6 33.2 %collective-permute-start.3 = (bf16[384,1024]{1,0:T(8,128)(2,1)}, bf16[384,1024]{1,0:T(8,128)(2,1)}, u32[]{:S(2)}, u32[]{:S(2)}) collective-permute-start(bf16[384,1024]{1,0:T(8,128)(2,1)} %broadcast_select_fusion.2), channel_id=1, source_target_pairs={{0,8},{8,0},{16,24},{24,16},{1,9},{9,1},{17,25},{25,17},{2,10},{10... | collective-permute-start | bytes 2359304 | tf_op jit(solution)/shard_map/ppermute | solution.py:815
  787.0 85.3 %collective-permute-start.1 = (bf16[384,1024]{1,0:T(8,128)(2,1)}, bf16[384,1024]{1,0:T(8,128)(2,1)}, u32[]{:S(2)}, u32[]{:S(2)}) collective-permute-start(bf16[384,1024]{1,0:T(8,128)(2,1)} %broadcast_select_fusion.3), channel_id=1, source_target_pairs={{0,8},{8,0},{16,24},{24,16},{1,9},{9,1},{17,25},{25,17},{2,10},{10... | collective-permute-start | bytes 2359304 | tf_op jit(solution)/shard_map/ppermute | solution.py:815
  944.8 20.3 %all-to-all-start.1 = ((bf16[8,48,1408]{2,1,0:T(8,128)(2,1)}), bf16[8,48,1408]{2,1,0:T(8,128)(2,1)}, u32[]{:S(2)}, u32[]{:S(2)}) async-start(bf16[8,48,1408]{2,1,0:T(8,128)(2,1)} %bitcast.271), calls=%async_computation.6 | async-start | bytes 2162688 | tf_op jit(solution)/shard_map/all_to_all | solution.py:1473
  949.3 7.1 copy-start.43
  949.3 7.1 copy-start.45
  949.3 7.1 copy-start.62
  (86 other events, 191.9 us)
Sparse Core Ops, SparseCore 0:
  10.2 42.7 all-gather.6
  55.2 132.0 all-gather.4
  190.4 114.6 all-gather.8
  306.5 113.2 all-gather.10
  470.9 43.5 reduce-scatter.17
  516.6 42.9 reduce-scatter.9
  562.0 26.9 reduce-scatter.11
  591.8 78.0 reduce-scatter.15
  672.8 76.9 reduce-scatter.13
  752.5 34.2 reduce-scatter.19
  789.2 95.0 reduce-scatter.21
